TPU v7x, 1024 devices: a whole 4x8x16 slice. The times are simulated.
1024 devices in a mesh: dp: 128 (over z_hi, x, y, core), mp: 8 (over z_lo).
Axes of the slice: x: 4, y: 8, z: 16 (z_hi: 2, z_lo: 8; z = z_hi * 8 + z_lo), core: 2. Of those that a mesh axis runs over, the one named last changes fastest.
Arguments:
- tokens: bfloat16 [32768, 4096], P('dp'), may hold values from -72 to 72
- qkv_weight: bfloat16 [4096, 3, 2048], P('dp', None, 'mp'), may hold values from -0.09375 to 0.09375
- out_weight: bfloat16 [2048, 4096], P('mp'), may hold values from -0.125 to 0.125
Outputs:
- attended: bfloat16 [32768, 4096], P(('dp', 'mp'))
All inputs are finite; a program needn't handle non-finite values.
Results may differ from a plain program's by a relative error of at most 0.022.
The roundings to bfloat16 on the way count: a program that leaves them out, or rounds other values in their place, can miss the bound.
Values may be sent and summed in bfloat16 or wider, within the bound.
No kernel may reach another device: no remote copies, remote signals or barrier semaphores. Data moves between devices by JAX's collectives and lax.ppermute only.
A program may use at most 32 MiB of HBM per device.

v0:
```python
import math

import jax
import jax.numpy as jnp
from jax import lax
from jax.sharding import PartitionSpec as P

HD = 128


def attend(projected):
    tok_count = projected.shape[0]
    queries = projected[:, 0].reshape(tok_count, -1, HD)
    key_rows = projected[:, 1].reshape(tok_count, -1, HD)
    values = projected[:, 2].reshape(tok_count, -1, HD)
    scores = jnp.einsum(
        "qhe,khe->hqk", queries, key_rows, preferred_element_type=jnp.float32
    ) / math.sqrt(HD)
    attn_weights = jax.nn.softmax(scores, axis=-1).astype(jnp.bfloat16)
    mixed = jnp.einsum("hqk,khe->qhe", attn_weights, values, preferred_element_type=jnp.float32)
    return mixed.astype(jnp.bfloat16).reshape(tok_count, -1)


def body(tokens, qkv_weight, out_weight):
    gathered = lax.all_gather(qkv_weight, "dp", axis=0, tiled=True)
    projected = jnp.einsum(
        "td,dsc->tsc", tokens, gathered, preferred_element_type=jnp.float32
    ).astype(jnp.bfloat16)
    mixed = attend(projected)
    return lax.psum_scatter(
        jnp.dot(mixed, out_weight, preferred_element_type=jnp.float32).astype(jnp.bfloat16),
        "mp",
        scatter_dimension=0,
        tiled=True,
    )


def solution(mesh):
    return jax.shard_map(
        body,
        mesh=mesh,
        in_specs=(P("dp", None), P("dp", None, "mp"), P("mp", None)),
        out_specs=P(("dp", "mp"), None),
        check_vma=False,
    )
```

profile of v0, /device:TPU:6, one launch (start us, length us, event | category | flops | bytes accessed | tf_op | source)
XLA Modules:
  0.0 305.2 jit_solution(5847360927017931004)
XLA Ops:
  6.5 0.0 copy-start
  6.5 0.0 all-gather.2.cloned.1.call-start
  6.5 0.7 all-gather.2.cloned.1.call-update
  7.3 0.0 reduce-scatter.2.cloned.1.call-start
  7.3 216.8 %all-gather.2.cloned.1.call-done = bf16[4096,3,256]{2,0,1:T(8,128)(2,1)} async-done(((bf16[32,3,256]{2,0,1:T(8,128)(2,1)}), bf16[4096,3,256]{2,0,1:T(8,128)(2,1)}) %all-gather.2.cloned.1.call-update) | async-done | bytes 6291472 | tf_op jit(solution)/shard_map/all_gather | solution.py:25
  224.1 6.0 %fusion.4 = bf16[256,3,256]{0,2,1:T(8,128)(2,1)S(1)} fusion(bf16[4096,3,256]{2,0,1:T(8,128)(2,1)} %all-gather.2.cloned.1.call-done, bf16[256,4096]{1,0:T(8,128)(2,1)} %param.3), kind=kOutput, calls=%fused_computation.5 | convolution fusion | flops 1610809344 | bytes 8781824 | tf_op jit(solution)/shard_map/td,dsc->tsc/dot_general | solution.py:26
  230.1 0.4 fusion.11
  230.5 0.3 convolution_multiply_fusion
  230.7 0.3 convolution_convert_fusion.1
  231.0 0.0 copy-done
  231.0 2.1 convolution_convert_fusion
  233.1 0.0 reduce-scatter.2.cloned.1.call-update
  233.2 65.2 %reduce-scatter.2.cloned.1.call-done = bf16[32,4096]{1,0:T(8,128)(2,1)} async-done(((bf16[256,4096]{1,0:T(8,128)(2,1)}), bf16[32,4096]{1,0:T(8,128)(2,1)}) %reduce-scatter.2.cloned.1.call-update) | async-done | bytes 262160 | tf_op jit(solution)/shard_map/reduce_scatter | solution.py:30
  (1 shorter events, 0.0 us)
Async XLA Ops:
  6.5 224.5 %copy-start = (bf16[256,4096]{1,0:T(8,128)(2,1)S(1)}, bf16[256,4096]{1,0:T(8,128)(2,1)}, u32[]{:S(2)}) copy-start(bf16[256,4096]{1,0:T(8,128)(2,1)} %param.5) | copy-start | bytes 6291460
  6.5 217.5 %all-gather.2.cloned.1.call-start = ((), (), s32[]{:S(2)}) async-start(), calls=%async_computation.1 | async-start | bytes 6340608 | tf_op jit(solution)/shard_map/all_gather | solution.py:25
  7.3 291.1 %reduce-scatter.2.cloned.1.call-start = ((), (), s32[]{:S(2)}) async-start(), calls=%async_computation.2 | async-start | bytes 2359296 | tf_op jit(solution)/shard_map/reduce_scatter | solution.py:30
Sparse Core Ops, SparseCore 0:
  13.2 210.8 all-gather.1
  233.3 65.0 reduce-scatter.1
where the time goes:
time: 305 us
  waiting for transfers between devices  283 us (93%)
  between operations  13.4 us (4%)
  matrix products  9 us (3%)
    all_gather x1, waiting for transfers between devices, body(): gathered = lax.all_gather(qkv_weight, 'dp', axis=0, tiled=True)  217 us
    reduce_scatter x1, waiting for transfers between devices, body(): lax.psum_scatter(jnp.dot(mixed, out_weight, preferred_element_type=jnp.fl...  65.2 us
  transfers between devices with their start and end apart: 2, of which 2 were waited for; matrix products, arithmetic and copies ran while one was open for 0% of the time, Pallas kernels for 0%

commit v1 on v0

v1 whole, which is shorter than its diff:
```python
import functools
import math

import jax
import jax.numpy as jnp
from jax import lax
from jax.experimental import pallas as pl
from jax.experimental.pallas import tpu as pltpu
from jax.sharding import Mesh
from jax.sharding import PartitionSpec as P

HD = 128
ZH, X, YQ, YP, C = 2, 4, 4, 2, 2
RG, CB = 2, 4
AXES = ("zh", "x", "yq", "yp", "c", "rg", "cb")
DP, MP = AXES[:5], AXES[5:]


def spread(block, axes, n):
    return lax.all_to_all(jnp.broadcast_to(block[None], (n,) + block.shape), axes, 0, 0, tiled=True)


def attend_kernel(own_ref, other_ref, w_ref, out_ref):
    part = w_ref.shape[3]
    span = YQ * YP * part
    totals = [None, None]
    for zh in range(ZH):
        for x in range(X):
            weight = jnp.concatenate(
                [w_ref[x * YP + yp, yq, zh] for yq in range(YQ) for yp in range(YP)], axis=0
            )
            start = (zh * X + x) * span
            for g, ref in enumerate((own_ref, other_ref)):
                product = jnp.dot(
                    ref[:, start : start + span], weight, preferred_element_type=jnp.float32
                )
                totals[g] = product if totals[g] is None else totals[g] + product
    for g in range(2):
        projected = totals[g].astype(jnp.bfloat16)
        queries, key_rows, values = (projected[:, i * HD : (i + 1) * HD] for i in range(3))
        scores = lax.dot_general(
            queries, key_rows, (((1,), (1,)), ((), ())), preferred_element_type=jnp.float32
        ) * (1.0 / math.sqrt(HD))
        raised = jnp.exp(scores - jnp.max(scores, axis=-1, keepdims=True))
        attn = (raised / jnp.sum(raised, axis=-1, keepdims=True)).astype(jnp.bfloat16)
        out_ref[g] = jnp.dot(attn, values, preferred_element_type=jnp.float32).astype(jnp.bfloat16)


def project_kernel(mixed_ref, w_ref, out_ref):
    total = None
    for block in range(mixed_ref.shape[1]):
        mixed = jnp.concatenate([mixed_ref[c, block] for c in range(C)], axis=1)
        weight = jnp.concatenate([w_ref[i, block] for i in range(w_ref.shape[0])], axis=0)
        term = jnp.dot(mixed, weight, preferred_element_type=jnp.float32).astype(jnp.bfloat16)
        wide = term.astype(jnp.float32)
        total = wide if total is None else total + wide
    out_ref[...] = total.astype(jnp.bfloat16)


def body(tokens, qkv_weight, out_weight):
    rows, width = tokens.shape
    k_rows = qkv_weight.shape[0]
    other = lax.ppermute(tokens, "c", [(0, 1), (1, 0)])

    heads = qkv_weight.reshape(k_rows, 3, C, HD).transpose(2, 0, 1, 3).reshape(C, k_rows, 3 * HD)
    heads = jnp.broadcast_to(heads[None], (ZH,) + heads.shape).reshape(ZH * C, k_rows, 3 * HD)
    heads = lax.all_to_all(heads, ("zh", "c"), 0, 0, tiled=True)
    heads = spread(heads, "yq", YQ)
    heads = spread(heads, ("x", "yp"), X * YP)
    heads = heads.reshape(X * YP, YQ, ZH, C * k_rows, 3 * HD)

    parts = X * C
    block = out_weight.shape[0] // parts
    columns = out_weight.shape[1] // CB
    mine = lax.axis_index("x") * C + lax.axis_index("c")
    share = lax.dynamic_slice_in_dim(out_weight, mine * block, block, 0)
    share = share.reshape(block, CB, columns).transpose(1, 0, 2)
    share = jnp.broadcast_to(share[None], (RG,) + share.shape).reshape(RG * CB, block, columns)
    share = lax.all_to_all(share, MP, 0, 0, tiled=True)
    out_full = lax.all_gather(share, ("x", "c"))

    mixed = pl.pallas_call(
        attend_kernel,
        out_shape=jax.ShapeDtypeStruct((2, rows, HD), jnp.bfloat16),
        compiler_params=pltpu.CompilerParams(vmem_limit_bytes=48 << 20),
        cost_estimate=pl.CostEstimate(flops=2 * 2 * rows * width * 3 * HD, bytes_accessed=8 << 20, transcendentals=0),
        name="attend",
    )(tokens, other, heads)
    core = lax.axis_index("c")
    mixed = jnp.where(core == 0, mixed, mixed[::-1])
    mixed = mixed.reshape(C, RG, 1, rows // RG, HD)
    mixed = jnp.broadcast_to(mixed, (C, RG, CB, rows // RG, HD)).reshape(C * RG * CB, rows // RG, HD)
    mixed = lax.all_to_all(mixed, ("c",) + MP, 0, 0, tiled=True).reshape(C, RG * CB, rows // RG, HD)

    summed = pl.pallas_call(
        project_kernel,
        out_shape=jax.ShapeDtypeStruct((rows // RG, columns), jnp.bfloat16),
        compiler_params=pltpu.CompilerParams(vmem_limit_bytes=48 << 20),
        cost_estimate=pl.CostEstimate(flops=2 * rows * 2048 * columns // RG, bytes_accessed=5 << 20, transcendentals=0),
        name="project",
    )(mixed, out_full)
    summed = summed.reshape(CB, rows // (RG * CB), columns)
    summed = lax.all_to_all(summed, "cb", 0, 0, tiled=True)
    return summed.transpose(1, 0, 2).reshape(rows // (RG * CB), CB * columns)


def solution(mesh):
    named = Mesh(mesh.devices.reshape(ZH, X, YQ, YP, C, RG, CB), AXES)
    return jax.shard_map(
        body,
        mesh=named,
        in_specs=(P(DP, None), P(DP, None, MP), P(MP, None)),
        out_specs=P(DP + MP, None),
        check_vma=False,
    )
```

time: 305 us -> 215 us (0.70); the launches traced: 305 us -> 210 us
  waiting for transfers between devices: 283 us -> 47.7 us
  blocking collectives: 0 us -> 120 us
  starting transfers between devices: 0.04 us -> 13.9 us
  matrix products: 9 us -> 0 us
  local copies, waits for them, and re-layouts: 0.03 us -> 8.99 us
  Pallas kernels: 0 us -> 6.19 us
    all_gather x1, waiting for transfers between devices: 217 us -> 0.01 us  [body(): out_full = lax.all_gather(share, ('x', 'c'))]
    all_to_all x0 -> x4, blocking collectives: none -> 120 us  [the longest x1 37.7 us: body(): share = lax.all_to_all(share, MP, 0, 0, tiled=True)]
    reduce_scatter x1 -> x0, waiting for transfers between devices: 65.2 us -> none  [body(): lax.psum_scatter(jnp.dot(mixed, out_weight, preferred_element_type=jnp.fl...]
    all_to_all x0 -> x2, waiting for transfers between devices: none -> 42.6 us  [spread(): lax.all_to_all(jnp.broadcast_to(block[None], (n,) + block.shape), axes, 0...]
    all_to_all x0 -> x2, starting transfers between devices: none -> 11.9 us  [spread(): lax.all_to_all(jnp.broadcast_to(block[None], (n,) + block.shape), axes, 0...]
    dot_general x4 -> x0, matrix products: 8.61 us -> none  [the longest x1 5.97 us: body(): jnp.einsum('td,dsc->tsc', tokens, gathered, preferred_element_type=jnp.fl...]
    pallas_call x0 -> x2, Pallas kernels: none -> 6.19 us  [the longest x1 5.43 us: body(): pl.pallas_call(attend_kernel, out_shape=jax.ShapeDtypeStruct((2, rows, HD...]
    ppermute x0 -> x1, waiting for transfers between devices: none -> 4.46 us  [body(): other = lax.ppermute(tokens, 'c', [(0, 1), (1, 0)])]
  transfers between devices with their start and end apart: 2 -> 4, of which waited for: 2 -> 3; matrix products, arithmetic and copies ran while one was open for 0% -> 0% of each run, Pallas kernels for 0% -> 3%
where the time goes in v1:
time: 215 us; the launch traced here: 210 us
  blocking collectives  120 us (56%)
  waiting for transfers between devices  47.7 us (22%)
  starting transfers between devices  13.9 us (6%)
  between operations  13.5 us (6%)
  local copies, waits for them, and re-layouts  8.99 us (4%)
  Pallas kernels  6.19 us (3%)
    all_to_all x2, waiting for transfers between devices, spread(): lax.all_to_all(jnp.broadcast_to(block[None], (n,) + block.shape), axes, 0...  42.6 us
    all_to_all x1, blocking collectives, body(): share = lax.all_to_all(share, MP, 0, 0, tiled=True)  37.7 us
    all_to_all x1, blocking collectives, body(): lax.all_to_all(mixed, ('c',) + MP, 0, 0, tiled=True)  37.5 us
    all_to_all x1, blocking collectives, body(): heads = lax.all_to_all(heads, ('zh', 'c'), 0, 0, tiled=True)  33.5 us
    all_to_all x2, starting transfers between devices, spread(): lax.all_to_all(jnp.broadcast_to(block[None], (n,) + block.shape), axes, 0...  11.9 us
    all_to_all x1, blocking collectives, body(): summed = lax.all_to_all(summed, 'cb', 0, 0, tiled=True)  11.4 us
    pallas_call x1, Pallas kernels, body(): pl.pallas_call(attend_kernel, out_shape=jax.ShapeDtypeStruct((2, rows, HD...  5.43 us
    ppermute x1, waiting for transfers between devices, body(): other = lax.ppermute(tokens, 'c', [(0, 1), (1, 0)])  4.46 us
  transfers between devices with their start and end apart: 4, of which 3 were waited for; matrix products, arithmetic and copies ran while one was open for 0% of the time, Pallas kernels for 3%

profile of v1, /device:TPU:6, one launch (start us, length us, event | category | flops | bytes accessed | tf_op | source)
XLA Modules:
  0.0 210.4 jit_solution(15278915938535583498)
XLA Ops:
  6.5 1.0 reshape.33
  7.6 0.1 broadcast_in_dim.14
  7.6 33.5 %all_to_all.30 = bf16[4,32,384]{2,1,0:T(8,128)(2,1)S(1)} all-to-all(bf16[4,32,384]{2,1,0:T(8,128)(2,1)S(1)} %bitcast.25), channel_id=1, replica_groups=mesh['zh'=2,'x'=4,'yq'=4,'yp'=2,'c'=2,'rg'=2,'cb'=4] {'zh','c'}, dimensions={0} | all-to-all | bytes 196608 | tf_op jit(solution)/shard_map/all_to_all | solution.py:67
  41.1 0.8 broadcast_in_dim.16
  41.9 7.1 %all-to-all-start.1 = ((bf16[4,4,32,384]{3,2,1,0:T(8,128)(2,1)}), bf16[4,4,32,384]{3,2,1,0:T(8,128)(2,1)S(1)}, u32[]{:S(2)}, u32[]{:S(2)}) async-start(bf16[4,4,32,384]{3,2,1,0:T(8,128)(2,1)} %broadcast_in_dim.16), calls=%async_computation.1 | async-start | bytes 786432 | tf_op jit(solution)/shard_map/all_to_all | solution.py:20
  49.0 0.2 reshape.38
  49.2 0.1 copy.9
  49.3 10.4 %all-to-all-done.1 = bf16[4,4,32,384]{3,2,1,0:T(8,128)(2,1)S(1)} async-done(((bf16[4,4,32,384]{3,2,1,0:T(8,128)(2,1)}), bf16[4,4,32,384]{3,2,1,0:T(8,128)(2,1)S(1)}, u32[]{:S(2)}, u32[]{:S(2)}) %all-to-all-start.1) | async-done | bytes 393248 | tf_op jit(solution)/shard_map/all_to_all | solution.py:20
  59.7 0.1 broadcast_in_dim.38
  59.8 37.7 %all_to_all.31 = bf16[8,32,1024]{2,1,0:T(8,128)(2,1)} all-to-all(bf16[8,32,1024]{2,1,0:T(8,128)(2,1)S(1)} %bitcast.21), channel_id=1, replica_groups=mesh['zh'=2,'x'=4,'yq'=4,'yp'=2,'c'=2,'rg'=2,'cb'=4] {'rg','cb'}, dimensions={0} | all-to-all | bytes 1048576 | tf_op jit(solution)/shard_map/all_to_all | solution.py:79
  97.5 2.2 %broadcast_in_dim.17 = bf16[8,4,4,32,384]{4,3,2,1,0:T(8,128)(2,1)} broadcast(bf16[4,4,32,384]{3,2,1,0:T(8,128)(2,1)S(1)} %all-to-all-done.1), dimensions={1,2,3,4} | broadcast | bytes 3538944 | tf_op jit(solution)/shard_map/broadcast_in_dim | solution.py:20
  99.7 4.8 %all-to-all-start.2 = ((bf16[8,4,4,32,384]{4,3,2,1,0:T(8,128)(2,1)}), bf16[8,4,4,32,384]{4,3,2,1,0:T(8,128)(2,1)}, u32[]{:S(2)}, u32[]{:S(2)}) async-start(bf16[8,4,4,32,384]{4,3,2,1,0:T(8,128)(2,1)} %broadcast_in_dim.17), calls=%async_computation.2 | async-start | bytes 6291456 | tf_op jit(solution)/shard_map/all_to_all | solution.py:20
  104.5 0.7 all-gather.3.cloned.1.call-update
  105.2 1.9 collective-permute-start
  107.2 4.5 %collective-permute-done.other_ref = bf16[256,4096]{1,0:T(8,128)(2,1)} collective-permute-done((bf16[256,4096]{1,0:T(8,128)(2,1)}, bf16[256,4096]{1,0:T(8,128)(2,1)}, u32[]{:S(2)}, u32[]{:S(2)}) %collective-permute-start) | collective-permute-done | bytes 2097184 | tf_op jit(solution)/shard_map/ppermute | solution.py:63
  111.6 32.2 %all-to-all-done.2 = bf16[8,4,4,32,384]{4,3,2,1,0:T(8,128)(2,1)} async-done(((bf16[8,4,4,32,384]{4,3,2,1,0:T(8,128)(2,1)}), bf16[8,4,4,32,384]{4,3,2,1,0:T(8,128)(2,1)}, u32[]{:S(2)}, u32[]{:S(2)}) %all-to-all-start.2) | async-done | bytes 3145760 | tf_op jit(solution)/shard_map/all_to_all | solution.py:20
  143.8 1.6 copy-done.2
  145.4 5.4 %attend.1 = bf16[2,256,128]{2,1,0:T(8,128)(2,1)S(1)} custom-call(bf16[256,4096]{1,0:T(8,128)(2,1)S(1)} %copy-done.2, bf16[256,4096]{1,0:T(8,128)(2,1)} %collective-permute-done.other_ref, bf16[8,4,2,64,384]{4,3,2,1,0:T(8,128)(2,1)} %bitcast.2.w_ref), custom_call_target="tpu_custom_call" | custom-call | flops 1610612736 | bytes 8388608 | tf_op jit(solution)/shard_map/attend/pallas_call | solution.py:82
  150.9 0.1 broadcast_in_dim.37
  151.0 37.5 %all_to_all.32 = bf16[16,128,128]{2,1,0:T(8,128)(2,1)S(1)} all-to-all(bf16[16,128,128]{2,1,0:T(8,128)(2,1)S(1)} %bitcast.20), channel_id=1, replica_groups=mesh['zh'=2,'x'=4,'yq'=4,'yp'=2,'c'=2,'rg'=2,'cb'=4] {'c','rg','cb'}, dimensions={0} | all-to-all | bytes 1048576 | tf_op jit(solution)/shard_map/all_to_all | solution.py:93
  188.4 2.2 %copy-done.1 = bf16[64,32,1024]{2,1,0:T(8,128)(2,1)S(1)} copy-done((bf16[64,32,1024]{2,1,0:T(8,128)(2,1)S(1)}, bf16[64,32,1024]{2,1,0:T(8,128)(2,1)}, u32[]{:S(2)}) %copy-start.1) | copy-done | bytes 4194328
  190.6 0.8 project.1
  191.4 11.4 %all_to_all.33 = bf16[4,32,1024]{2,1,0:T(8,128)(2,1)S(1)} all-to-all(bf16[4,32,1024]{2,1,0:T(8,128)(2,1)S(1)} %bitcast.19), channel_id=1, replica_groups=mesh['zh'=2,'x'=4,'yq'=4,'yp'=2,'c'=2,'rg'=2,'cb'=4] {'cb'}, dimensions={0} | all-to-all | bytes 524288 | tf_op jit(solution)/shard_map/all_to_all | solution.py:103
  202.8 0.7 copy.11
  (10 shorter events, 0.1 us)
Async XLA Ops:
  6.5 42.5 %copy-start = (bf16[256,4096]{1,0:T(8,128)(2,1)S(1)}, bf16[256,4096]{1,0:T(8,128)(2,1)}, u32[]{:S(2)}) copy-start(bf16[256,4096]{1,0:T(8,128)(2,1)} %param.5) | copy-start | bytes 6291460
  41.9 17.8 %all-to-all-start.1 = ((bf16[4,4,32,384]{3,2,1,0:T(8,128)(2,1)}), bf16[4,4,32,384]{3,2,1,0:T(8,128)(2,1)S(1)}, u32[]{:S(2)}, u32[]{:S(2)}) async-start(bf16[4,4,32,384]{3,2,1,0:T(8,128)(2,1)} %broadcast_in_dim.16), calls=%async_computation.1 | async-start | bytes 786432 | tf_op jit(solution)/shard_map/all_to_all | solution.py:20
  99.7 44.1 %all-to-all-start.2 = ((bf16[8,4,4,32,384]{4,3,2,1,0:T(8,128)(2,1)}), bf16[8,4,4,32,384]{4,3,2,1,0:T(8,128)(2,1)}, u32[]{:S(2)}, u32[]{:S(2)}) async-start(bf16[8,4,4,32,384]{4,3,2,1,0:T(8,128)(2,1)} %broadcast_in_dim.17), calls=%async_computation.2 | async-start | bytes 6291456 | tf_op jit(solution)/shard_map/all_to_all | solution.py:20
  104.5 83.9 %all-gather.3.cloned.1.call-start = ((), (), s32[]{:S(2)}) async-start(), calls=%async_computation.6 | async-start | bytes 4718592 | tf_op jit(solution)/shard_map/all_gather | solution.py:80
  105.2 6.4 %collective-permute-start = (bf16[256,4096]{1,0:T(8,128)(2,1)}, bf16[256,4096]{1,0:T(8,128)(2,1)}, u32[]{:S(2)}, u32[]{:S(2)}) collective-permute-start(bf16[256,4096]{1,0:T(8,128)(2,1)} %own_ref.1), channel_id=1, source_target_pairs={{0,8},{8,0},{1,9},{9,1},{2,10},{10,2},{3,11},{11,3},{4,12},{12,4},... | collective-permute-start | bytes 6291464 | tf_op jit(solution)/shard_map/ppermute | solution.py:63
  143.8 1.6 copy-start.2
  188.4 2.2 %copy-start.1 = (bf16[64,32,1024]{2,1,0:T(8,128)(2,1)S(1)}, bf16[64,32,1024]{2,1,0:T(8,128)(2,1)}, u32[]{:S(2)}) copy-start(bf16[64,32,1024]{2,1,0:T(8,128)(2,1)} %all-gather.3.cloned.1.call-done) | copy-start | bytes 12582916
Sparse Core Ops, SparseCore 0:
  108.1 44.0 all-gather.2

commit v2 on v1

v2 whole, which is shorter than its diff:
```python
import math

import jax
import jax.numpy as jnp
from jax import lax
from jax.experimental import pallas as pl
from jax.experimental.pallas import tpu as pltpu
from jax.sharding import Mesh
from jax.sharding import PartitionSpec as P

HD = 128
ZH, X, Y, C = 2, 4, 8, 2
XQ, YQ = X // 2, Y // 2
RG, CB = 4, 2
AXES = ("zh", "x", "yq", "yp", "c", "rg", "cb")
DP, MP = AXES[:5], AXES[5:]


def place(zh, x, y, c):
    return ((zh * X + x % X) * Y + y % Y) * C + c


FAR = [
    [place(zh, 2 * xq + px, 2 * yq + py, c) for xq in range(XQ) for yq in range(YQ)]
    for zh in range(ZH) for c in range(C) for px in range(2) for py in range(2)
]
NEAR = [
    [place(zh, 2 * xq + (1 - 2 * c) * px, 2 * yq + (1 - 2 * c) * py, c) for px in range(2) for py in range(2)]
    for zh in range(ZH) for c in range(C) for xq in range(XQ) for yq in range(YQ)
]


ACROSS = [
    [
        (place(zh, x, y, c), place(zh ^ dz, x, y, c ^ dc))
        for zh in range(ZH) for x in range(X) for y in range(Y) for c in range(C)
    ]
    for dz, dc in ((0, 1), (1, 0), (1, 1))
]


def spread(block, groups):
    n = len(groups[0])
    blocks = jnp.broadcast_to(block[None], (n,) + block.shape)
    return lax.all_to_all(blocks, DP, 0, 0, axis_index_groups=groups, tiled=True)


def attend_kernel(own_ref, other_ref, w_ref, out_ref):
    span = Y * w_ref.shape[5]
    totals = [None, None]
    for zh in range(ZH):
        for x in range(X):
            weight = jnp.concatenate(
                [w_ref[x % 2, y % 2, x // 2, y // 2, zh] for y in range(Y)], axis=0
            )
            start = (zh * X + x) * span
            for g, ref in enumerate((own_ref, other_ref)):
                product = jnp.dot(
                    ref[:, start : start + span], weight, preferred_element_type=jnp.float32
                )
                totals[g] = product if totals[g] is None else totals[g] + product
    for g in range(2):
        projected = totals[g].astype(jnp.bfloat16)
        queries, key_rows, values = (projected[:, i * HD : (i + 1) * HD] for i in range(3))
        scores = lax.dot_general(
            queries, key_rows, (((1,), (1,)), ((), ())), preferred_element_type=jnp.float32
        ) * (1.0 / math.sqrt(HD))
        raised = jnp.exp(scores - jnp.max(scores, axis=-1, keepdims=True))
        attn = (raised / jnp.sum(raised, axis=-1, keepdims=True)).astype(jnp.bfloat16)
        out_ref[g] = jnp.dot(attn, values, preferred_element_type=jnp.float32).astype(jnp.bfloat16)


def project_kernel(mixed_ref, w_ref, out_ref, total_ref):
    block = pl.program_id(0)
    mixed = jnp.concatenate([mixed_ref[c, 0] for c in range(C)], axis=1)
    weight = jnp.concatenate([w_ref[i, 0] for i in range(w_ref.shape[0])], axis=0)
    term = jnp.dot(mixed, weight, preferred_element_type=jnp.float32).astype(jnp.bfloat16)

    @pl.when(block == 0)
    def _():
        total_ref[...] = term.astype(jnp.float32)

    @pl.when(block > 0)
    def _():
        total_ref[...] += term.astype(jnp.float32)

    @pl.when(block == pl.num_programs(0) - 1)
    def _():
        out_ref[...] = total_ref[...].astype(jnp.bfloat16)


def body(tokens, qkv_weight, out_weight):
    rows, width = tokens.shape
    k_rows = qkv_weight.shape[0]
    other = lax.ppermute(tokens, "c", [(0, 1), (1, 0)])

    heads = qkv_weight.reshape(k_rows, 3, C, HD).transpose(2, 0, 1, 3).reshape(C, k_rows, 3 * HD)
    core, half = lax.axis_index("c"), lax.axis_index("zh")
    own = jnp.where(core == 0, heads[0], heads[1])
    rest = jnp.where(core == 0, heads[1], heads[0])
    near = jnp.stack([own, lax.ppermute(rest, DP, ACROSS[0])])
    far = jnp.stack([lax.ppermute(own, DP, ACROSS[1]), lax.ppermute(rest, DP, ACROSS[2])])
    near, far = (jnp.where(core == 0, pair, pair[::-1]) for pair in (near, far))
    heads = jnp.where(half == 0, jnp.concatenate([near, far]), jnp.concatenate([far, near]))
    heads = spread(spread(heads, FAR), NEAR)
    heads = heads.reshape(2, 2, XQ, YQ, ZH, C * k_rows, 3 * HD)

    parts = X * 2 * C
    block = out_weight.shape[0] // parts
    columns = out_weight.shape[1] // CB
    mine = (lax.axis_index("x") * 2 + lax.axis_index("yp")) * C + core
    share = lax.dynamic_slice_in_dim(out_weight, mine * block, block, 0)
    share = jnp.stack([share[:, i * columns : (i + 1) * columns] for i in range(CB)])
    share = jnp.broadcast_to(share[None], (RG,) + share.shape).reshape(RG * CB, block, columns)
    share = lax.all_to_all(share, MP, 0, 0, tiled=True)
    out_full = lax.all_gather(share, ("x", "yp", "c"))

    mixed = pl.pallas_call(
        attend_kernel,
        out_shape=jax.ShapeDtypeStruct((2, rows, HD), jnp.bfloat16),
        compiler_params=pltpu.CompilerParams(vmem_limit_bytes=48 << 20),
        cost_estimate=pl.CostEstimate(flops=2 * 2 * rows * width * 3 * HD, bytes_accessed=8 << 20, transcendentals=0),
        name="attend",
    )(tokens, other, heads)
    mixed = jnp.where(core == 0, mixed, mixed[::-1])
    mixed = mixed.reshape(C, RG, 1, rows // RG, HD)
    mixed = jnp.broadcast_to(mixed, (C, RG, CB, rows // RG, HD)).reshape(C * RG * CB, rows // RG, HD)
    mixed = lax.all_to_all(mixed, ("c",) + MP, 0, 0, tiled=True).reshape(C, RG * CB, rows // RG, HD)

    summed = pl.pallas_call(
        project_kernel,
        out_shape=jax.ShapeDtypeStruct((rows // RG, columns), jnp.bfloat16),
        grid=(RG * CB,),
        in_specs=[
            pl.BlockSpec((C, 1, rows // RG, HD), lambda i: (0, i, 0, 0)),
            pl.BlockSpec((parts, 1, block, columns), lambda i: (0, i, 0, 0)),
        ],
        out_specs=pl.BlockSpec((rows // RG, columns), lambda i: (0, 0)),
        scratch_shapes=[pltpu.VMEM((rows // RG, columns), jnp.float32)],
        compiler_params=pltpu.CompilerParams(vmem_limit_bytes=48 << 20),
        cost_estimate=pl.CostEstimate(flops=2 * rows * 2048 * columns // RG, bytes_accessed=5 << 20, transcendentals=0),
        name="project",
    )(mixed, out_full)
    summed = summed.reshape(CB, rows // (RG * CB), columns)
    summed = lax.all_to_all(summed, "cb", 0, 0, tiled=True)
    return summed.transpose(1, 0, 2).reshape(rows // (RG * CB), CB * columns)


def solution(mesh):
    named = Mesh(mesh.devices.reshape(ZH, X, YQ, 2, C, RG, CB), AXES)
    return jax.shard_map(
        body,
        mesh=named,
        in_specs=(P(DP, None), P(DP, None, MP), P(MP, None)),
        out_specs=P(DP + MP, None),
        check_vma=False,
    )
```

time: 215 us -> 205 us (0.953); the launches traced: 210 us -> 204 us
  waiting for transfers between devices: 47.7 us -> 31 us
  starting transfers between devices: 13.9 us -> 25.2 us
  Pallas kernels: 6.19 us -> 11.7 us
  blocking collectives: 120 us -> 116 us
    all_to_all x2 -> x1, waiting for transfers between devices: 42.6 us -> 17.8 us  [spread(): lax.all_to_all(blocks, DP, 0, 0, axis_index_groups=groups, tiled=True)]
    ppermute x0 -> x3, starting transfers between devices: none -> 16.6 us  [the longest x1 11.9 us: body(): lax.ppermute(own, DP, ACROSS[1])]
    ppermute x0 -> x3, waiting for transfers between devices: none -> 9.08 us  [the longest x1 9.07 us: body(): lax.ppermute(rest, DP, ACROSS[2])]
    all_to_all x1, blocking collectives: 37.5 us -> 28.7 us  [body(): lax.all_to_all(mixed, ('c',) + MP, 0, 0, tiled=True)]
    all_to_all x1, blocking collectives: 37.7 us -> 44.3 us  [body(): share = lax.all_to_all(share, MP, 0, 0, tiled=True)]
    pallas_call x1, Pallas kernels: 0.77 us -> 6.97 us  [body(): pl.pallas_call(project_kernel, out_shape=jax.ShapeDtypeStruct((rows // RG...]
    all_to_all x2 -> x1, starting transfers between devices: 11.9 us -> 6.73 us  [spread(): lax.all_to_all(blocks, DP, 0, 0, axis_index_groups=groups, tiled=True)]
    all_to_all x1, blocking collectives: 11.4 us -> 7.56 us  [body(): summed = lax.all_to_all(summed, 'cb', 0, 0, tiled=True)]
  transfers between devices with their start and end apart: 4 -> 6, of which waited for: 3 -> 3; matrix products, arithmetic and copies ran while one was open for 0% -> 1% of each run, Pallas kernels for 3% -> 2%
where the time goes in v2:
time: 205 us; the launch traced here: 204 us
  blocking collectives  116 us (57%)
  waiting for transfers between devices  31 us (15%)
  starting transfers between devices  25.2 us (12%)
  between operations  13.6 us (7%)
  Pallas kernels  11.7 us (6%)
  local copies, waits for them, and re-layouts  7 us (3%)
    all_to_all x1, blocking collectives, body(): share = lax.all_to_all(share, MP, 0, 0, tiled=True)  44.3 us
    all_to_all x1, blocking collectives, spread(): lax.all_to_all(blocks, DP, 0, 0, axis_index_groups=groups, tiled=True)  35 us
    all_to_all x1, blocking collectives, body(): lax.all_to_all(mixed, ('c',) + MP, 0, 0, tiled=True)  28.7 us
    all_to_all x1, waiting for transfers between devices, spread(): lax.all_to_all(blocks, DP, 0, 0, axis_index_groups=groups, tiled=True)  17.8 us
    ppermute x1, starting transfers between devices, body(): lax.ppermute(own, DP, ACROSS[1])  11.9 us
    ppermute x1, waiting for transfers between devices, body(): lax.ppermute(rest, DP, ACROSS[2])  9.07 us
    all_to_all x1, blocking collectives, body(): summed = lax.all_to_all(summed, 'cb', 0, 0, tiled=True)  7.56 us
    pallas_call x1, Pallas kernels, body(): pl.pallas_call(project_kernel, out_shape=jax.ShapeDtypeStruct((rows // RG...  6.97 us
  transfers between devices with their start and end apart: 6, of which 3 were waited for; matrix products, arithmetic and copies ran while one was open for 1% of the time, Pallas kernels for 2%

profile of v2, /device:TPU:6, one launch (start us, length us, event | category | flops | bytes accessed | tf_op | source)
XLA Modules:
  0.0 204.3 jit_solution(16405623535681345510)
XLA Ops:
  6.5 0.0 all-gather.3.cloned.1.call-start
  6.5 0.9 dynamic-slice_bitcast_fusion.1
  7.5 44.3 %all_to_all.25 = bf16[8,16,2048]{2,1,0:T(8,128)(2,1)} all-to-all(bf16[8,16,2048]{2,1,0:T(8,128)(2,1)S(1)} %bitcast.35), channel_id=1, replica_groups=mesh['zh'=2,'x'=4,'yq'=4,'yp'=2,'c'=2,'rg'=4,'cb'=2] {'rg','cb'}, dimensions={0} | all-to-all | bytes 1048576 | tf_op jit(solution)/shard_map/all_to_all | solution.py:115
  51.9 0.0 all-gather.3.cloned.1.call-update
  52.0 11.9 %collective-permute-start.2 = (bf16[32,384]{1,0:T(8,128)(2,1)S(1)}, bf16[32,384]{1,0:T(8,128)(2,1)S(1)}, u32[]{:S(2)}, u32[]{:S(2)}) collective-permute-start(bf16[32,384]{1,0:T(8,128)(2,1)S(1)} %bitcast.44), channel_id=1, source_target_pairs={{0,512},{8,520},{16,528},{24,536},{32,544},{40,552},{48,560},{56,5... | collective-permute-start | bytes 73736 | tf_op jit(solution)/shard_map/ppermute | solution.py:102
  63.9 1.9 collective-permute-start.3
  65.8 2.8 %collective-permute-start.1 = (bf16[32,384]{1,0:T(8,128)(2,1)S(1)}, bf16[32,384]{1,0:T(8,128)(2,1)S(1)}, u32[]{:S(2)}, u32[]{:S(2)}) collective-permute-start(bf16[32,384]{1,0:T(8,128)(2,1)S(1)} %bitcast.43), channel_id=1, source_target_pairs={{0,8},{8,0},{16,24},{24,16},{32,40},{40,32},{48,56},{56,48},{64,72... | collective-permute-start | bytes 73736 | tf_op jit(solution)/shard_map/ppermute | solution.py:101
  68.7 0.0 collective-permute-done.2
  68.7 9.1 %collective-permute-done.3 = bf16[32,384]{1,0:T(8,128)(2,1)S(1)} collective-permute-done((bf16[32,384]{1,0:T(8,128)(2,1)S(1)}, bf16[32,384]{1,0:T(8,128)(2,1)S(1)}, u32[]{:S(2)}, u32[]{:S(2)}) %collective-permute-start.3) | collective-permute-done | bytes 24608 | tf_op jit(solution)/shard_map/ppermute | solution.py:102
  77.8 0.0 collective-permute-done.1
  77.9 0.1 broadcast_in_dim.10
  78.0 35.0 %all_to_all.26 = bf16[8,4,32,384]{3,2,1,0:T(8,128)(2,1)S(1)} all-to-all(bf16[8,4,32,384]{3,2,1,0:T(8,128)(2,1)S(1)} %broadcast_in_dim.10), channel_id=1, replica_groups={{0,32,64,96,256,288,320,352},{16,48,80,112,272,304,336,368},{128,160,19..., dimensions={0} | all-to-all | bytes 1572864 | tf_op jit(solution)/shard_map/all_to_all | solution.py:45
  113.0 2.2 %broadcast_in_dim.11 = bf16[4,8,4,32,384]{4,3,2,1,0:T(8,128)(2,1)} broadcast(bf16[8,4,32,384]{3,2,1,0:T(8,128)(2,1)S(1)} %all_to_all.26), dimensions={1,2,3,4} | broadcast | bytes 3932160 | tf_op jit(solution)/shard_map/broadcast_in_dim | solution.py:44
  115.2 6.7 %all-to-all-start.1 = ((bf16[4,8,4,32,384]{4,3,2,1,0:T(8,128)(2,1)}), bf16[4,8,4,32,384]{4,3,2,1,0:T(8,128)(2,1)}, u32[]{:S(2)}, u32[]{:S(2)}) async-start(bf16[4,8,4,32,384]{4,3,2,1,0:T(8,128)(2,1)} %broadcast_in_dim.11), calls=%async_computation.1 | async-start | bytes 6291456 | tf_op jit(solution)/shard_map/all_to_all | solution.py:45
  121.9 1.9 collective-permute-start
  123.8 4.1 %collective-permute-done.other_ref = bf16[256,4096]{1,0:T(8,128)(2,1)S(1)} collective-permute-done((bf16[256,4096]{1,0:T(8,128)(2,1)S(1)}, bf16[256,4096]{1,0:T(8,128)(2,1)S(1)}, u32[]{:S(2)}, u32[]{:S(2)}) %collective-permute-start) | collective-permute-done | bytes 2097184 | tf_op jit(solution)/shard_map/ppermute | solution.py:95
  128.0 1.3 copy-done.1
  129.3 17.8 %all-to-all-done.1 = bf16[4,8,4,32,384]{4,3,2,1,0:T(8,128)(2,1)} async-done(((bf16[4,8,4,32,384]{4,3,2,1,0:T(8,128)(2,1)}), bf16[4,8,4,32,384]{4,3,2,1,0:T(8,128)(2,1)}, u32[]{:S(2)}, u32[]{:S(2)}) %all-to-all-start.1) | async-done | bytes 3145760 | tf_op jit(solution)/shard_map/all_to_all | solution.py:45
  147.1 1.6 copy-done.2
  148.7 4.7 %attend.1 = bf16[2,256,128]{2,1,0:T(8,128)(2,1)S(1)} custom-call(bf16[256,4096]{1,0:T(8,128)(2,1)S(1)} %copy-done, bf16[256,4096]{1,0:T(8,128)(2,1)S(1)} %copy-done.2, bf16[2,2,2,4,2,64,384]{6,5,4,3,2,1,0:T(8,128)(2,1)} %bitcast.4.w_ref), custom_call_target="tpu_custom_call" | custom-call | flops 1610612736 | bytes 8388608 | tf_op jit(solution)/shard_map/attend/pallas_call | solution.py:118
  153.5 28.7 %all_to_all.27 = bf16[16,64,128]{2,1,0:T(8,128)(2,1)S(1)} all-to-all(bf16[16,64,128]{2,1,0:T(8,128)(2,1)S(1)} %bitcast.36), channel_id=1, replica_groups=mesh['zh'=2,'x'=4,'yq'=4,'yp'=2,'c'=2,'rg'=4,'cb'=2] {'c','rg','cb'}, dimensions={0} | all-to-all | bytes 524288 | tf_op jit(solution)/shard_map/all_to_all | solution.py:128
  182.2 7.0 %project.1 = bf16[64,2048]{1,0:T(8,128)(2,1)S(1)} custom-call(bf16[2,8,64,128]{3,2,1,0:T(8,128)(2,1)S(1)} %bitcast.32, bf16[16,8,16,2048]{3,2,1,0:T(8,128)(2,1)} %bitcast.34), custom_call_target="tpu_custom_call" | custom-call | flops 536870912 | bytes 5242880 | tf_op jit(solution)/shard_map/project/pallas_call | solution.py:130
  189.2 7.6 %all_to_all.28 = bf16[2,32,2048]{2,1,0:T(8,128)(2,1)S(1)} all-to-all(bf16[2,32,2048]{2,1,0:T(8,128)(2,1)S(1)} %bitcast.33), channel_id=1, replica_groups=mesh['zh'=2,'x'=4,'yq'=4,'yp'=2,'c'=2,'rg'=4,'cb'=2] {'cb'}, dimensions={0} | all-to-all | bytes 524288 | tf_op jit(solution)/shard_map/all_to_all | solution.py:145
  196.7 0.7 copy.9
  (21 shorter events, 0.3 us)
Async XLA Ops:
  6.5 45.4 %copy-start.3 = (bf16[32,3,256]{2,0,1:T(8,128)(2,1)S(1)}, bf16[32,3,256]{2,0,1:T(8,128)(2,1)}, u32[]{:S(2)}) copy-start(bf16[32,3,256]{2,0,1:T(8,128)(2,1)} %param.4) | copy-start | bytes 147460
  6.5 175.6 %all-gather.3.cloned.1.call-start = ((), (), s32[]{:S(2)}) async-start(), calls=%async_computation.5 | async-start | bytes 8912896 | tf_op jit(solution)/shard_map/all_gather | solution.py:116
  52.0 16.7 %collective-permute-start.2 = (bf16[32,384]{1,0:T(8,128)(2,1)S(1)}, bf16[32,384]{1,0:T(8,128)(2,1)S(1)}, u32[]{:S(2)}, u32[]{:S(2)}) collective-permute-start(bf16[32,384]{1,0:T(8,128)(2,1)S(1)} %bitcast.44), channel_id=1, source_target_pairs={{0,512},{8,520},{16,528},{24,536},{32,544},{40,552},{48,560},{56,5... | collective-permute-start | bytes 73736 | tf_op jit(solution)/shard_map/ppermute | solution.py:102
  63.9 13.9 %collective-permute-start.3 = (bf16[32,384]{1,0:T(8,128)(2,1)S(1)}, bf16[32,384]{1,0:T(8,128)(2,1)S(1)}, u32[]{:S(2)}, u32[]{:S(2)}) collective-permute-start(bf16[32,384]{1,0:T(8,128)(2,1)S(1)} %bitcast.42), channel_id=1, source_target_pairs={{0,520},{8,512},{16,536},{24,528},{32,552},{40,544},{48,568},{56,5... | collective-permute-start | bytes 73736 | tf_op jit(solution)/shard_map/ppermute | solution.py:102
  65.8 11.9 %collective-permute-start.1 = (bf16[32,384]{1,0:T(8,128)(2,1)S(1)}, bf16[32,384]{1,0:T(8,128)(2,1)S(1)}, u32[]{:S(2)}, u32[]{:S(2)}) collective-permute-start(bf16[32,384]{1,0:T(8,128)(2,1)S(1)} %bitcast.43), channel_id=1, source_target_pairs={{0,8},{8,0},{16,24},{24,16},{32,40},{40,32},{48,56},{56,48},{64,72... | collective-permute-start | bytes 73736 | tf_op jit(solution)/shard_map/ppermute | solution.py:101
  115.2 6.7 %copy-start = (bf16[256,4096]{1,0:T(8,128)(2,1)S(1)}, bf16[256,4096]{1,0:T(8,128)(2,1)}, u32[]{:S(2)}) copy-start(bf16[256,4096]{1,0:T(8,128)(2,1)} %own_ref.1) | copy-start | bytes 6291460
  115.2 31.9 %all-to-all-start.1 = ((bf16[4,8,4,32,384]{4,3,2,1,0:T(8,128)(2,1)}), bf16[4,8,4,32,384]{4,3,2,1,0:T(8,128)(2,1)}, u32[]{:S(2)}, u32[]{:S(2)}) async-start(bf16[4,8,4,32,384]{4,3,2,1,0:T(8,128)(2,1)} %broadcast_in_dim.11), calls=%async_computation.1 | async-start | bytes 6291456 | tf_op jit(solution)/shard_map/all_to_all | solution.py:45
  121.9 6.0 %collective-permute-start = (bf16[256,4096]{1,0:T(8,128)(2,1)S(1)}, bf16[256,4096]{1,0:T(8,128)(2,1)S(1)}, u32[]{:S(2)}, u32[]{:S(2)}) collective-permute-start(bf16[256,4096]{1,0:T(8,128)(2,1)S(1)} %copy-done), channel_id=1, source_target_pairs={{0,8},{8,0},{1,9},{9,1},{2,10},{10,2},{3,11},{11,3},{4,12},{12,4},... | collective-permute-start | bytes 6291464 | tf_op jit(solution)/shard_map/ppermute | solution.py:95
  128.0 1.3 copy-start.1
  147.1 1.6 copy-start.2
Sparse Core Ops, SparseCore 0:
  52.0 85.1 all-gather.2

commit v3 on v2

v3 whole, which is shorter than its diff:
```python
import math

import jax
import jax.numpy as jnp
from jax import lax
from jax.experimental import pallas as pl
from jax.experimental.pallas import tpu as pltpu
from jax.sharding import Mesh
from jax.sharding import PartitionSpec as P

HD = 128
ZH, X, Y, C = 2, 4, 8, 2
XQ, YQ = X // 2, Y // 2
RG, CB = 2, 4
AXES = ("zh", "x", "y", "c", "rg", "cb")
DP, MP = AXES[:4], AXES[4:]


def place(zh, x, y, c):
    return ((zh * X + x % X) * Y + y % Y) * C + c


FAR = [
    [place(zh, 2 * xq + px, 2 * yq + py, c) for xq in range(XQ) for yq in range(YQ)]
    for zh in range(ZH) for c in range(C) for px in range(2) for py in range(2)
]
NEAR = [
    [place(zh, 2 * xq + (1 - 2 * c) * px, 2 * yq + (1 - 2 * c) * py, c) for px in range(2) for py in range(2)]
    for zh in range(ZH) for c in range(C) for xq in range(XQ) for yq in range(YQ)
]


def spread(block, groups):
    n = len(groups[0])
    blocks = jnp.broadcast_to(block[None], (n,) + block.shape)
    return lax.all_to_all(blocks, DP, 0, 0, axis_index_groups=groups, tiled=True)


def attend_kernel(own_ref, other_ref, w_ref, *refs):
    out_ref = refs[-1]
    span = Y * w_ref.shape[5]
    totals = [None, None]
    for zh in range(ZH):
        for x in range(X):
            weight = jnp.concatenate(
                [w_ref[x % 2, y % 2, x // 2, y // 2, zh] for y in range(Y)], axis=0
            )
            start = (zh * X + x) * span
            for g, ref in enumerate((own_ref, other_ref)):
                product = jnp.dot(
                    ref[:, start : start + span], weight, preferred_element_type=jnp.float32
                )
                totals[g] = product if totals[g] is None else totals[g] + product
    for g in range(2):
        projected = totals[g].astype(jnp.bfloat16)
        queries, key_rows, values = (projected[:, i * HD : (i + 1) * HD] for i in range(3))
        scores = lax.dot_general(
            queries, key_rows, (((1,), (1,)), ((), ())), preferred_element_type=jnp.float32
        ) * (1.0 / math.sqrt(HD))
        raised = jnp.exp(scores - jnp.max(scores, axis=-1, keepdims=True))
        attn = (raised / jnp.sum(raised, axis=-1, keepdims=True)).astype(jnp.bfloat16)
        out_ref[g] = jnp.dot(attn, values, preferred_element_type=jnp.float32).astype(jnp.bfloat16)


def split_kernel(place_ref, w_ref, after_ref, own_ref, *out_refs):
    column, core = place_ref[0], place_ref[1]
    part, width = out_refs[0].shape
    own_ref[...] = w_ref[:, pl.ds(pl.multiple_of(column * width, width), width)]
    rows = pl.ds(pl.multiple_of(core * part, part), part)
    for i, out_ref in enumerate(out_refs):
        start = pl.multiple_of((column ^ (i + 1)) * width, width)
        out_ref[...] = w_ref[rows, pl.ds(start, width)]


def project_kernel(place_ref, mixed_ref, own_ref, held_ref, partner_ref, far_ref, near_ref):
    column, half, core = place_ref[0], place_ref[1], place_ref[2]
    rows = far_ref.shape[0]
    for out_ref, start in ((far_ref, (1 - half) * rows), (near_ref, half * rows)):
        span = pl.ds(pl.multiple_of(start, rows), rows)
        mixed = jnp.concatenate([mixed_ref[c, column, span] for c in range(C)], axis=1)
        term = jnp.dot(mixed, own_ref[...], preferred_element_type=jnp.float32).astype(jnp.bfloat16)
        total = term.astype(jnp.float32)
        for i in range(CB - 1):
            block = column ^ (i + 1)
            mixed = jnp.concatenate([mixed_ref[core, block, span], mixed_ref[1 - core, block, span]], axis=1)
            weight = jnp.concatenate([held_ref[i], partner_ref[i]], axis=0)
            term = jnp.dot(mixed, weight, preferred_element_type=jnp.float32).astype(jnp.bfloat16)
            total += term.astype(jnp.float32)
        out_ref[...] = total.astype(out_ref.dtype)


def body(tokens, qkv_weight, out_weight):
    rows, width = tokens.shape
    k_rows = qkv_weight.shape[0]
    other = lax.ppermute(tokens, "c", [(0, 1), (1, 0)])

    heads = qkv_weight.reshape(k_rows, 3, C, HD).transpose(2, 0, 1, 3).reshape(C, k_rows, 3 * HD)
    heads = jnp.broadcast_to(heads[None], (ZH,) + heads.shape).reshape(ZH * C, k_rows, 3 * HD)
    heads = lax.all_to_all(heads, ("zh", "c"), 0, 0, tiled=True)
    first = heads
    heads = spread(spread(heads, FAR), NEAR)
    heads = heads.reshape(2, 2, XQ, YQ, ZH, C * k_rows, 3 * HD)

    column, half, core = lax.axis_index("cb"), lax.axis_index("rg"), lax.axis_index("c")
    depth, columns = out_weight.shape[0], out_weight.shape[1] // CB
    smem, vmem = pl.BlockSpec(memory_space=pltpu.SMEM), pl.BlockSpec(memory_space=pltpu.VMEM)
    own_weight, *sent = pl.pallas_call(
        split_kernel,
        out_shape=[jax.ShapeDtypeStruct((depth, columns), jnp.bfloat16)]
        + [jax.ShapeDtypeStruct((depth // C, columns), jnp.bfloat16)] * (CB - 1),
        in_specs=[smem, vmem, vmem],
        out_specs=[vmem] * CB,
        compiler_params=pltpu.CompilerParams(vmem_limit_bytes=24 << 20),
        cost_estimate=pl.CostEstimate(flops=0, bytes_accessed=4 << 20, transcendentals=0),
        name="split",
    )(jnp.stack([column, core]), out_weight, first)
    held = [lax.ppermute(block, "cb", [(j, j ^ (i + 1)) for j in range(CB)]) for i, block in enumerate(sent)]

    mixed = pl.pallas_call(
        attend_kernel,
        out_shape=jax.ShapeDtypeStruct((2, rows, HD), jnp.bfloat16),
        in_specs=[vmem] * 3 + [pl.BlockSpec(memory_space=pl.ANY)] * len(held),
        compiler_params=pltpu.CompilerParams(vmem_limit_bytes=48 << 20),
        cost_estimate=pl.CostEstimate(flops=2 * 2 * rows * width * 3 * HD, bytes_accessed=8 << 20, transcendentals=0),
        name="attend",
    )(tokens, other, heads, *held)
    held = jnp.stack(held)
    partner = lax.ppermute(held, "c", [(0, 1), (1, 0)])
    mixed = jnp.where(core == 0, mixed, mixed[::-1])
    mixed = jnp.broadcast_to(mixed[:, None], (C, CB, rows, HD)).reshape(C * CB, rows, HD)
    mixed = lax.all_to_all(mixed, ("c", "cb"), 0, 0, tiled=True).reshape(C, CB, rows, HD)

    part = rows // RG
    far, near = pl.pallas_call(
        project_kernel,
        out_shape=[
            jax.ShapeDtypeStruct((part, columns), jnp.bfloat16),
            jax.ShapeDtypeStruct((part, columns), jnp.float32),
        ],
        in_specs=[smem] + [vmem] * 4,
        out_specs=[vmem] * 2,
        compiler_params=pltpu.CompilerParams(vmem_limit_bytes=24 << 20),
        cost_estimate=pl.CostEstimate(flops=2 * rows * CB * C * HD * columns, bytes_accessed=4 << 20, transcendentals=0),
        name="project",
    )(jnp.stack([column, half, core]), mixed, own_weight, held, partner)
    far = lax.ppermute(far, "rg", [(0, 1), (1, 0)])
    summed = (near + far.astype(jnp.float32)).astype(jnp.bfloat16)
    summed = summed.reshape(CB, part // CB, columns)
    summed = lax.all_to_all(summed, "cb", 0, 0, tiled=True)
    return summed.transpose(1, 0, 2).reshape(part // CB, CB * columns)


def solution(mesh):
    named = Mesh(mesh.devices.reshape(ZH, X, Y, C, RG, CB), AXES)
    return jax.shard_map(
        body,
        mesh=named,
        in_specs=(P(DP, None), P(DP, None, MP), P(MP, None)),
        out_specs=P(DP + MP, None),
        check_vma=False,
    )
```

time: 205 us -> 178 us (0.87)
  blocking collectives: 116 us -> 74.1 us
  waiting for transfers between devices: 31 us -> 49.7 us
  between operations: 13.6 us -> 0.14 us
  starting transfers between devices: 25.2 us -> 37.6 us
  Pallas kernels: 11.7 us -> 7.31 us
    all_to_all x2 -> x1, blocking collectives: 73 us -> 33.5 us  [body(): heads = lax.all_to_all(heads, ('zh', 'c'), 0, 0, tiled=True)]
    ppermute x3 -> x5, waiting for transfers between devices: 9.08 us -> 39.2 us  [the longest x1 21.8 us: body(): far = lax.ppermute(far, 'rg', [(0, 1), (1, 0)])]
    all_to_all x1, waiting for transfers between devices: 17.8 us -> 0.01 us  [spread(): lax.all_to_all(blocks, DP, 0, 0, axis_index_groups=groups, tiled=True)]
    all_to_all x0 -> x1, waiting for transfers between devices: none -> 10.5 us  [body(): lax.all_to_all(mixed, ('c', 'cb'), 0, 0, tiled=True)]
    all_to_all x0 -> x1, starting transfers between devices: none -> 8.97 us  [body(): lax.all_to_all(mixed, ('c', 'cb'), 0, 0, tiled=True)]
    all_to_all x1, blocking collectives: 35 us -> 28.8 us  [spread(): lax.all_to_all(blocks, DP, 0, 0, axis_index_groups=groups, tiled=True)]
    pallas_call x1 -> x2, Pallas kernels: 6.97 us -> 1.96 us  [the longest x1 1.33 us: body(): pl.pallas_call(project_kernel, out_shape=[jax.ShapeDtypeStruct((part, col...]
    ppermute x3 -> x5, starting transfers between devices: 16.6 us -> 21.2 us  [the longest x3 10.8 us: body(): lax.ppermute(block, 'cb', [(j, j ^ i + 1) for j in range(CB)])]
  transfers between devices with their start and end apart: 6 -> 8, of which waited for: 3 -> 5; matrix products, arithmetic and copies ran while one was open for 1% -> 0% of each run, Pallas kernels for 2% -> 0%
where the time goes in v3:
time: 178 us; the launch traced here: 176 us
  blocking collectives  74.1 us (42%)
  waiting for transfers between devices  49.7 us (28%)
  starting transfers between devices  37.6 us (21%)
  Pallas kernels  7.31 us (4%)
  local copies, waits for them, and re-layouts  6.34 us (4%)
    all_to_all x1, blocking collectives, body(): heads = lax.all_to_all(heads, ('zh', 'c'), 0, 0, tiled=True)  33.5 us
    all_to_all x1, blocking collectives, spread(): lax.all_to_all(blocks, DP, 0, 0, axis_index_groups=groups, tiled=True)  28.8 us
    ppermute x1, waiting for transfers between devices, body(): far = lax.ppermute(far, 'rg', [(0, 1), (1, 0)])  21.8 us
    ppermute x3, waiting for transfers between devices, body(): lax.ppermute(block, 'cb', [(j, j ^ i + 1) for j in range(CB)])  15.6 us
    all_to_all x1, blocking collectives, body(): summed = lax.all_to_all(summed, 'cb', 0, 0, tiled=True)  11.8 us
    ppermute x3, starting transfers between devices, body(): lax.ppermute(block, 'cb', [(j, j ^ i + 1) for j in range(CB)])  10.8 us
    all_to_all x1, waiting for transfers between devices, body(): lax.all_to_all(mixed, ('c', 'cb'), 0, 0, tiled=True)  10.5 us
    all_to_all x1, starting transfers between devices, body(): lax.all_to_all(mixed, ('c', 'cb'), 0, 0, tiled=True)  8.97 us
  transfers between devices with their start and end apart: 8, of which 5 were waited for; matrix products, arithmetic and copies ran while one was open for 0% of the time, Pallas kernels for 0%

profile of v3, /device:TPU:6, one launch (start us, length us, event | category | flops | bytes accessed | tf_op | source)
XLA Modules:
  0.0 175.5 jit_solution(13297247653222539701)
XLA Ops:
  0.0 0.8 reshape.25
  0.9 33.5 %all_to_all.25.after_ref = bf16[4,32,384]{2,1,0:T(8,128)(2,1)S(1)} all-to-all(bf16[4,32,384]{2,1,0:T(8,128)(2,1)S(1)} %bitcast.25), channel_id=1, replica_groups=mesh['zh'=2,'x'=4,'y'=8,'c'=2,'rg'=2,'cb'=4] {'zh','c'}, dimensions={0} | all-to-all | bytes 196608 | tf_op jit(solution)/shard_map/all_to_all | solution.py:99
  34.5 28.8 %all_to_all.26 = bf16[8,4,32,384]{3,2,1,0:T(8,128)(2,1)S(1)} all-to-all(bf16[8,4,32,384]{3,2,1,0:T(8,128)(2,1)S(1)} %broadcast_in_dim.12), channel_id=1, replica_groups={{0,32,64,96,256,288,320,352},{16,48,80,112,272,304,336,368},{128,160,19..., dimensions={0} | all-to-all | bytes 1572864 | tf_op jit(solution)/shard_map/all_to_all | solution.py:36
  63.3 2.2 %broadcast_in_dim.13 = bf16[4,8,4,32,384]{4,3,2,1,0:T(8,128)(2,1)} broadcast(bf16[8,4,32,384]{3,2,1,0:T(8,128)(2,1)S(1)} %all_to_all.26), dimensions={1,2,3,4} | broadcast | bytes 3932160 | tf_op jit(solution)/shard_map/broadcast_in_dim | solution.py:35
  65.5 5.6 %all-to-all-start.2 = ((bf16[4,8,4,32,384]{4,3,2,1,0:T(8,128)(2,1)}), bf16[4,8,4,32,384]{4,3,2,1,0:T(8,128)(2,1)}, u32[]{:S(2)}, u32[]{:S(2)}) async-start(bf16[4,8,4,32,384]{4,3,2,1,0:T(8,128)(2,1)} %broadcast_in_dim.13), calls=%async_computation.2 | async-start | bytes 6291456 | tf_op jit(solution)/shard_map/all_to_all | solution.py:36
  71.1 1.9 %collective-permute-start = (bf16[256,4096]{1,0:T(8,128)(2,1)}, bf16[256,4096]{1,0:T(8,128)(2,1)}, u32[]{:S(2)}, u32[]{:S(2)}) collective-permute-start(bf16[256,4096]{1,0:T(8,128)(2,1)} %own_ref.1), channel_id=1, source_target_pairs={{0,8},{8,0},{1,9},{9,1},{2,10},{10,2},{3,11},{11,3},{4,12},{12,4},... | collective-permute-start | bytes 6291464 | tf_op jit(solution)/shard_map/ppermute | solution.py:95
  73.1 0.6 split.1
  73.7 3.2 %collective-permute-start.1 = (bf16[128,1024]{1,0:T(8,128)(2,1)S(1)}, bf16[128,1024]{1,0:T(8,128)(2,1)S(1)}, u32[]{:S(2)}, u32[]{:S(2)}) collective-permute-start(bf16[128,1024]{1,0:T(8,128)(2,1)S(1)} %get-tuple-element.11), channel_id=1, source_target_pairs={{0,1},{1,0},{2,3},{3,2},{4,5},{5,4},{6,7},{7,6},{8,9},{9,8},{10,11... | collective-permute-start | bytes 786440 | tf_op jit(solution)/shard_map/ppermute | solution.py:117
  77.0 4.3 %collective-permute-start.2 = (bf16[128,1024]{1,0:T(8,128)(2,1)S(1)}, bf16[128,1024]{1,0:T(8,128)(2,1)S(1)}, u32[]{:S(2)}, u32[]{:S(2)}) collective-permute-start(bf16[128,1024]{1,0:T(8,128)(2,1)S(1)} %get-tuple-element.12), channel_id=1, source_target_pairs={{0,2},{1,3},{2,0},{3,1},{4,6},{5,7},{6,4},{7,5},{8,10},{9,11},{10,... | collective-permute-start | bytes 786440 | tf_op jit(solution)/shard_map/ppermute | solution.py:117
  81.2 3.3 %collective-permute-start.3 = (bf16[128,1024]{1,0:T(8,128)(2,1)S(1)}, bf16[128,1024]{1,0:T(8,128)(2,1)S(1)}, u32[]{:S(2)}, u32[]{:S(2)}) collective-permute-start(bf16[128,1024]{1,0:T(8,128)(2,1)S(1)} %get-tuple-element.13), channel_id=1, source_target_pairs={{0,3},{1,2},{2,1},{3,0},{4,7},{5,6},{6,5},{7,4},{8,11},{9,10},{10,... | collective-permute-start | bytes 786440 | tf_op jit(solution)/shard_map/ppermute | solution.py:117
  84.5 4.6 %collective-permute-done.1.refs_0_ = bf16[128,1024]{1,0:T(8,128)(2,1)S(1)} collective-permute-done((bf16[128,1024]{1,0:T(8,128)(2,1)S(1)}, bf16[128,1024]{1,0:T(8,128)(2,1)S(1)}, u32[]{:S(2)}, u32[]{:S(2)}) %collective-permute-start.1) | collective-permute-done | bytes 262176 | tf_op jit(solution)/shard_map/ppermute | solution.py:117
  89.2 11.0 %collective-permute-done.2.refs_1_ = bf16[128,1024]{1,0:T(8,128)(2,1)S(1)} collective-permute-done((bf16[128,1024]{1,0:T(8,128)(2,1)S(1)}, bf16[128,1024]{1,0:T(8,128)(2,1)S(1)}, u32[]{:S(2)}, u32[]{:S(2)}) %collective-permute-start.2) | collective-permute-done | bytes 262176 | tf_op jit(solution)/shard_map/ppermute | solution.py:117
  100.2 1.6 copy-done.1
  101.8 5.4 %attend.1 = bf16[2,256,128]{2,1,0:T(8,128)(2,1)S(1)} custom-call(bf16[256,4096]{1,0:T(8,128)(2,1)S(1)} %copy-done.1, bf16[256,4096]{1,0:T(8,128)(2,1)} %collective-permute-done.other_ref, bf16[2,2,2,4,2,64,384]{6,5,4,3,2,1,0:T(8,128)(2,1)} %bitcast.5.w_ref, bf16[128,1024]{1,0:T(8,128)(2,1)S(1)} %collective-permute-done.1.refs_0_, ...), custom_call_target="tpu_custom_call" | custom-call | flops 1610612736 | bytes 8388608 | tf_op jit(solution)/shard_map/attend/pallas_call | solution.py:119
  107.2 0.9 broadcast_in_dim.14
  108.0 9.0 %all-to-all-start.3 = ((bf16[8,256,128]{2,1,0:T(8,128)(2,1)}), bf16[8,256,128]{2,1,0:T(8,128)(2,1)S(1)}, u32[]{:S(2)}, u32[]{:S(2)}) async-start(bf16[8,256,128]{2,1,0:T(8,128)(2,1)} %bitcast.6), calls=%async_computation.3 | async-start | bytes 1048576 | tf_op jit(solution)/shard_map/all_to_all | solution.py:131
  117.1 2.4 %collective-permute-start.4 = (bf16[3,128,1024]{2,1,0:T(8,128)(2,1)S(1)}, bf16[3,128,1024]{2,1,0:T(8,128)(2,1)S(1)}, u32[]{:S(2)}, u32[]{:S(2)}) collective-permute-start(bf16[3,128,1024]{2,1,0:T(8,128)(2,1)S(1)} %pad_maximum_fusion.held_ref), channel_id=1, source_target_pairs={{0,8},{8,0},{1,9},{9,1},{2,10},{10,2},{3,11},{11,3},{4,12},{12,4},... | collective-permute-start | bytes 2359304 | tf_op jit(solution)/shard_map/ppermute | solution.py:128
  119.6 1.8 %collective-permute-done.4.partner_ref = bf16[3,128,1024]{2,1,0:T(8,128)(2,1)S(1)} collective-permute-done((bf16[3,128,1024]{2,1,0:T(8,128)(2,1)S(1)}, bf16[3,128,1024]{2,1,0:T(8,128)(2,1)S(1)}, u32[]{:S(2)}, u32[]{:S(2)}) %collective-permute-start.4) | collective-permute-done | bytes 786464 | tf_op jit(solution)/shard_map/ppermute | solution.py:128
  121.4 10.5 %all-to-all-done.3 = bf16[8,256,128]{2,1,0:T(8,128)(2,1)S(1)} async-done(((bf16[8,256,128]{2,1,0:T(8,128)(2,1)}), bf16[8,256,128]{2,1,0:T(8,128)(2,1)S(1)}, u32[]{:S(2)}, u32[]{:S(2)}) %all-to-all-start.3) | async-done | bytes 524320 | tf_op jit(solution)/shard_map/all_to_all | solution.py:131
  131.9 1.3 project.1
  133.2 7.9 %collective-permute-start.5 = (bf16[128,1024]{1,0:T(8,128)(2,1)S(1)}, bf16[128,1024]{1,0:T(8,128)(2,1)S(1)}, u32[]{:S(2)}, u32[]{:S(2)}) collective-permute-start(bf16[128,1024]{1,0:T(8,128)(2,1)S(1)} %get-tuple-element.16), channel_id=1, source_target_pairs={{0,4},{4,0},{1,5},{5,1},{2,6},{6,2},{3,7},{7,3},{8,12},{12,8},{9,1... | collective-permute-start | bytes 786440 | tf_op jit(solution)/shard_map/ppermute | solution.py:146
  141.2 21.8 %collective-permute-done.5 = bf16[128,1024]{1,0:T(8,128)(2,1)S(1)} collective-permute-done((bf16[128,1024]{1,0:T(8,128)(2,1)S(1)}, bf16[128,1024]{1,0:T(8,128)(2,1)S(1)}, u32[]{:S(2)}, u32[]{:S(2)}) %collective-permute-start.5) | collective-permute-done | bytes 262176 | tf_op jit(solution)/shard_map/ppermute | solution.py:146
  163.0 11.8 %all_to_all.27 = bf16[4,32,1024]{2,1,0:T(8,128)(2,1)S(1)} all-to-all(bf16[4,32,1024]{2,1,0:T(8,128)(2,1)S(1)} %bitcast.24), channel_id=1, replica_groups=mesh['zh'=2,'x'=4,'y'=8,'c'=2,'rg'=2,'cb'=4] {'cb'}, dimensions={0} | all-to-all | bytes 524288 | tf_op jit(solution)/shard_map/all_to_all | solution.py:149
  174.8 0.7 copy.7
  (15 shorter events, 0.5 us)
Async XLA Ops:
  65.5 7.6 %copy-start = (bf16[256,4096]{1,0:T(8,128)(2,1)S(1)}, bf16[256,4096]{1,0:T(8,128)(2,1)}, u32[]{:S(2)}) copy-start(bf16[256,4096]{1,0:T(8,128)(2,1)} %w_ref.1) | copy-start | bytes 6291460
  65.5 34.7 %all-to-all-start.2 = ((bf16[4,8,4,32,384]{4,3,2,1,0:T(8,128)(2,1)}), bf16[4,8,4,32,384]{4,3,2,1,0:T(8,128)(2,1)}, u32[]{:S(2)}, u32[]{:S(2)}) async-start(bf16[4,8,4,32,384]{4,3,2,1,0:T(8,128)(2,1)} %broadcast_in_dim.13), calls=%async_computation.2 | async-start | bytes 6291456 | tf_op jit(solution)/shard_map/all_to_all | solution.py:36
  71.1 29.1 %collective-permute-start = (bf16[256,4096]{1,0:T(8,128)(2,1)}, bf16[256,4096]{1,0:T(8,128)(2,1)}, u32[]{:S(2)}, u32[]{:S(2)}) collective-permute-start(bf16[256,4096]{1,0:T(8,128)(2,1)} %own_ref.1), channel_id=1, source_target_pairs={{0,8},{8,0},{1,9},{9,1},{2,10},{10,2},{3,11},{11,3},{4,12},{12,4},... | collective-permute-start | bytes 6291464 | tf_op jit(solution)/shard_map/ppermute | solution.py:95
  73.7 15.5 %collective-permute-start.1 = (bf16[128,1024]{1,0:T(8,128)(2,1)S(1)}, bf16[128,1024]{1,0:T(8,128)(2,1)S(1)}, u32[]{:S(2)}, u32[]{:S(2)}) collective-permute-start(bf16[128,1024]{1,0:T(8,128)(2,1)S(1)} %get-tuple-element.11), channel_id=1, source_target_pairs={{0,1},{1,0},{2,3},{3,2},{4,5},{5,4},{6,7},{7,6},{8,9},{9,8},{10,11... | collective-permute-start | bytes 786440 | tf_op jit(solution)/shard_map/ppermute | solution.py:117
  77.0 23.2 %collective-permute-start.2 = (bf16[128,1024]{1,0:T(8,128)(2,1)S(1)}, bf16[128,1024]{1,0:T(8,128)(2,1)S(1)}, u32[]{:S(2)}, u32[]{:S(2)}) collective-permute-start(bf16[128,1024]{1,0:T(8,128)(2,1)S(1)} %get-tuple-element.12), channel_id=1, source_target_pairs={{0,2},{1,3},{2,0},{3,1},{4,6},{5,7},{6,4},{7,5},{8,10},{9,11},{10,... | collective-permute-start | bytes 786440 | tf_op jit(solution)/shard_map/ppermute | solution.py:117
  81.2 18.9 %collective-permute-start.3 = (bf16[128,1024]{1,0:T(8,128)(2,1)S(1)}, bf16[128,1024]{1,0:T(8,128)(2,1)S(1)}, u32[]{:S(2)}, u32[]{:S(2)}) collective-permute-start(bf16[128,1024]{1,0:T(8,128)(2,1)S(1)} %get-tuple-element.13), channel_id=1, source_target_pairs={{0,3},{1,2},{2,1},{3,0},{4,7},{5,6},{6,5},{7,4},{8,11},{9,10},{10,... | collective-permute-start | bytes 786440 | tf_op jit(solution)/shard_map/ppermute | solution.py:117
  100.2 1.6 copy-start.1
  108.0 23.8 %all-to-all-start.3 = ((bf16[8,256,128]{2,1,0:T(8,128)(2,1)}), bf16[8,256,128]{2,1,0:T(8,128)(2,1)S(1)}, u32[]{:S(2)}, u32[]{:S(2)}) async-start(bf16[8,256,128]{2,1,0:T(8,128)(2,1)} %bitcast.6), calls=%async_computation.3 | async-start | bytes 1048576 | tf_op jit(solution)/shard_map/all_to_all | solution.py:131
  117.1 4.3 %collective-permute-start.4 = (bf16[3,128,1024]{2,1,0:T(8,128)(2,1)S(1)}, bf16[3,128,1024]{2,1,0:T(8,128)(2,1)S(1)}, u32[]{:S(2)}, u32[]{:S(2)}) collective-permute-start(bf16[3,128,1024]{2,1,0:T(8,128)(2,1)S(1)} %pad_maximum_fusion.held_ref), channel_id=1, source_target_pairs={{0,8},{8,0},{1,9},{9,1},{2,10},{10,2},{3,11},{11,3},{4,12},{12,4},... | collective-permute-start | bytes 2359304 | tf_op jit(solution)/shard_map/ppermute | solution.py:128
  133.2 29.7 %collective-permute-start.5 = (bf16[128,1024]{1,0:T(8,128)(2,1)S(1)}, bf16[128,1024]{1,0:T(8,128)(2,1)S(1)}, u32[]{:S(2)}, u32[]{:S(2)}) collective-permute-start(bf16[128,1024]{1,0:T(8,128)(2,1)S(1)} %get-tuple-element.16), channel_id=1, source_target_pairs={{0,4},{4,0},{1,5},{5,1},{2,6},{6,2},{3,7},{7,3},{8,12},{12,8},{9,1... | collective-permute-start | bytes 786440 | tf_op jit(solution)/shard_map/ppermute | solution.py:146

commit v4 on v3

--- a/solution.py
+++ b/solution.py
@@ -30,9 +30,34 @@
 ]
 
 
-def spread(block, groups):
-    n = len(groups[0])
-    blocks = jnp.broadcast_to(block[None], (n,) + block.shape)
+def copies_kernel(block_ref, *refs):
+    out_ref, sems = refs[-2:]
+    lead = len(out_ref.shape) - len(block_ref.shape) == 1 and out_ref.shape[1:] == block_ref.shape
+    moves = [
+        pltpu.make_async_copy(block_ref, out_ref.at[i] if lead else out_ref.at[:, i], sems.at[i])
+        for i in range(sems.shape[0])
+    ]
+    for move in moves:
+        move.start()
+    for move in moves:
+        move.wait()
+
+
+def copies(block, n, axis, after=()):
+    anywhere = pl.BlockSpec(memory_space=pl.ANY)
+    return pl.pallas_call(
+        copies_kernel,
+        out_shape=jax.ShapeDtypeStruct(block.shape[:axis] + (n,) + block.shape[axis:], block.dtype),
+        in_specs=[anywhere] * (1 + len(after)),
+        out_specs=anywhere,
+        scratch_shapes=[pltpu.SemaphoreType.DMA((n,))],
+        cost_estimate=pl.CostEstimate(flops=0, bytes_accessed=2 * n * block.size, transcendentals=0),
+        name="copies",
+    )(block, *after)
+
+
+def spread(block, groups, after=()):
+    blocks = copies(block, len(groups[0]), 0, after)
     return lax.all_to_all(blocks, DP, 0, 0, axis_index_groups=groups, tiled=True)
 
 
@@ -98,8 +123,7 @@
     heads = jnp.broadcast_to(heads[None], (ZH,) + heads.shape).reshape(ZH * C, k_rows, 3 * HD)
     heads = lax.all_to_all(heads, ("zh", "c"), 0, 0, tiled=True)
     first = heads
-    heads = spread(spread(heads, FAR), NEAR)
-    heads = heads.reshape(2, 2, XQ, YQ, ZH, C * k_rows, 3 * HD)
+    heads = spread(heads, FAR)
 
     column, half, core = lax.axis_index("cb"), lax.axis_index("rg"), lax.axis_index("c")
     depth, columns = out_weight.shape[0], out_weight.shape[1] // CB
@@ -116,14 +140,16 @@
     )(jnp.stack([column, core]), out_weight, first)
     held = [lax.ppermute(block, "cb", [(j, j ^ (i + 1)) for j in range(CB)]) for i, block in enumerate(sent)]
 
+    heads = spread(heads, NEAR, held[:2]).reshape(2, 2, XQ, YQ, ZH, C * k_rows, 3 * HD)
+
     mixed = pl.pallas_call(
         attend_kernel,
         out_shape=jax.ShapeDtypeStruct((2, rows, HD), jnp.bfloat16),
-        in_specs=[vmem] * 3 + [pl.BlockSpec(memory_space=pl.ANY)] * len(held),
+        in_specs=[vmem] * 3 + [pl.BlockSpec(memory_space=pl.ANY)],
         compiler_params=pltpu.CompilerParams(vmem_limit_bytes=48 << 20),
         cost_estimate=pl.CostEstimate(flops=2 * 2 * rows * width * 3 * HD, bytes_accessed=8 << 20, transcendentals=0),
         name="attend",
-    )(tokens, other, heads, *held)
+    )(tokens, other, heads, held[2])
     held = jnp.stack(held)
     partner = lax.ppermute(held, "c", [(0, 1), (1, 0)])
     mixed = jnp.where(core == 0, mixed, mixed[::-1])

time: 178 us -> 284 us (1.60)
  Pallas kernels: 7.31 us -> 129 us
  blocking collectives: 74.1 us -> 45.4 us
  waiting for transfers between devices: 49.7 us -> 60.9 us
  starting transfers between devices: 37.6 us -> 43.1 us
  local copies, waits for them, and re-layouts: 6.34 us -> 2.68 us
    pallas_call x0 -> x2, Pallas kernels: none -> 121 us  [copies(): pl.pallas_call(copies_kernel, out_shape=jax.ShapeDtypeStruct(block.shape[...]
    all_to_all x1 -> x0, blocking collectives: 28.8 us -> none  [spread(): lax.all_to_all(blocks, DP, 0, 0, axis_index_groups=groups, tiled=True)]
    all_to_all x1 -> x2, starting transfers between devices: 5.58 us -> 15.7 us  [spread(): lax.all_to_all(blocks, DP, 0, 0, axis_index_groups=groups, tiled=True)]
    all_to_all x1 -> x2, waiting for transfers between devices: 0.01 us -> 8.16 us  [spread(): lax.all_to_all(blocks, DP, 0, 0, axis_index_groups=groups, tiled=True)]
    all_to_all x1, starting transfers between devices: 8.97 us -> 4.34 us  [body(): lax.all_to_all(mixed, ('c', 'cb'), 0, 0, tiled=True)]
    ppermute x3, waiting for transfers between devices: 15.6 us -> 18.7 us  [body(): lax.ppermute(block, 'cb', [(j, j ^ i + 1) for j in range(CB)])]
  transfers between devices with their start and end apart: 8 -> 9, of which waited for: 5 -> 8; matrix products, arithmetic and copies ran while one was open for 0% -> 0% of each run, Pallas kernels for 0% -> 0%
where the time goes in v4:
time: 284 us; the launch traced here: 281 us
  Pallas kernels  129 us (45%)
  waiting for transfers between devices  60.9 us (21%)
  blocking collectives  45.4 us (16%)
  starting transfers between devices  43.1 us (15%)
    pallas_call x2, Pallas kernels, copies(): pl.pallas_call(copies_kernel, out_shape=jax.ShapeDtypeStruct(block.shape[...  121 us
    all_to_all x1, blocking collectives, body(): heads = lax.all_to_all(heads, ('zh', 'c'), 0, 0, tiled=True)  33.6 us
    ppermute x1, waiting for transfers between devices, body(): far = lax.ppermute(far, 'rg', [(0, 1), (1, 0)])  21.8 us
    ppermute x3, waiting for transfers between devices, body(): lax.ppermute(block, 'cb', [(j, j ^ i + 1) for j in range(CB)])  18.7 us
    all_to_all x2, starting transfers between devices, spread(): lax.all_to_all(blocks, DP, 0, 0, axis_index_groups=groups, tiled=True)  15.7 us
    all_to_all x1, blocking collectives, body(): summed = lax.all_to_all(summed, 'cb', 0, 0, tiled=True)  11.8 us
    all_to_all x1, waiting for transfers between devices, body(): lax.all_to_all(mixed, ('c', 'cb'), 0, 0, tiled=True)  10.5 us
    ppermute x3, starting transfers between devices, body(): lax.ppermute(block, 'cb', [(j, j ^ i + 1) for j in range(CB)])  10.4 us
  transfers between devices with their start and end apart: 9, of which 8 were waited for; matrix products, arithmetic and copies ran while one was open for 0% of the time, Pallas kernels for 0%

profile of v4, /device:TPU:6, one launch (start us, length us, event | category | flops | bytes accessed | tf_op | source)
XLA Modules:
  0.0 281.4 jit_solution(274390759243623742)
XLA Ops:
  0.0 1.0 reshape.23
  1.1 33.6 %all_to_all.25.block_ref.after_ref = bf16[4,32,384]{2,1,0:T(8,128)(2,1)} all-to-all(bf16[4,32,384]{2,1,0:T(8,128)(2,1)S(1)} %bitcast.25), channel_id=1, replica_groups=mesh['zh'=2,'x'=4,'y'=8,'c'=2,'rg'=2,'cb'=4] {'zh','c'}, dimensions={0} | all-to-all | bytes 196608 | tf_op jit(solution)/shard_map/all_to_all | solution.py:124
  34.7 25.0 %copies.2 = bf16[8,4,32,384]{3,2,1,0:T(8,128)(2,1)} custom-call(bf16[4,32,384]{2,1,0:T(8,128)(2,1)} %all_to_all.25.block_ref.after_ref), custom_call_target="tpu_custom_call" | custom-call | bytes 786432 | tf_op jit(solution)/shard_map/copies/pallas_call | solution.py:48
  59.7 10.1 %all-to-all-start.1 = ((bf16[8,4,32,384]{3,2,1,0:T(8,128)(2,1)}), bf16[8,4,32,384]{3,2,1,0:T(8,128)(2,1)}, u32[]{:S(2)}, u32[]{:S(2)}) async-start(bf16[8,4,32,384]{3,2,1,0:T(8,128)(2,1)} %copies.2), calls=%async_computation.1 | async-start | bytes 1572864 | tf_op jit(solution)/shard_map/all_to_all | solution.py:61
  70.5 1.9 collective-permute-start.1
  72.4 3.8 %collective-permute-start.2 = (bf16[128,1024]{1,0:T(8,128)(2,1)S(1)}, bf16[128,1024]{1,0:T(8,128)(2,1)S(1)}, u32[]{:S(2)}, u32[]{:S(2)}) collective-permute-start(bf16[128,1024]{1,0:T(8,128)(2,1)S(1)} %get-tuple-element.12), channel_id=1, source_target_pairs={{0,2},{1,3},{2,0},{3,1},{4,6},{5,7},{6,4},{7,5},{8,10},{9,11},{10,... | collective-permute-start | bytes 786440 | tf_op jit(solution)/shard_map/ppermute | solution.py:141
  76.2 7.5 %collective-permute-done.1.refs_0_ = bf16[128,1024]{1,0:T(8,128)(2,1)S(1)} collective-permute-done((bf16[128,1024]{1,0:T(8,128)(2,1)S(1)}, bf16[128,1024]{1,0:T(8,128)(2,1)S(1)}, u32[]{:S(2)}, u32[]{:S(2)}) %collective-permute-start.1) | collective-permute-done | bytes 262176 | tf_op jit(solution)/shard_map/ppermute | solution.py:141
  83.7 3.6 %collective-permute-done.2.refs_1_ = bf16[128,1024]{1,0:T(8,128)(2,1)S(1)} collective-permute-done((bf16[128,1024]{1,0:T(8,128)(2,1)S(1)}, bf16[128,1024]{1,0:T(8,128)(2,1)S(1)}, u32[]{:S(2)}, u32[]{:S(2)}) %collective-permute-start.2) | collective-permute-done | bytes 262176 | tf_op jit(solution)/shard_map/ppermute | solution.py:141
  87.3 2.4 all-to-all-done.1.block_ref
  89.7 96.4 %copies.3 = bf16[4,8,4,32,384]{4,3,2,1,0:T(8,128)(2,1)} custom-call(bf16[8,4,32,384]{3,2,1,0:T(8,128)(2,1)} %all-to-all-done.1.block_ref, bf16[128,1024]{1,0:T(8,128)(2,1)} %copy-done.3, bf16[128,1024]{1,0:T(8,128)(2,1)} %copy-done.5), custom_call_target="tpu_custom_call" | custom-call | bytes 3145728 | tf_op jit(solution)/shard_map/copies/pallas_call | solution.py:48
  186.1 5.6 %all-to-all-start.2 = ((bf16[4,8,4,32,384]{4,3,2,1,0:T(8,128)(2,1)}), bf16[4,8,4,32,384]{4,3,2,1,0:T(8,128)(2,1)}, u32[]{:S(2)}, u32[]{:S(2)}) async-start(bf16[4,8,4,32,384]{4,3,2,1,0:T(8,128)(2,1)} %copies.3), calls=%async_computation.2 | async-start | bytes 6291456 | tf_op jit(solution)/shard_map/all_to_all | solution.py:61
  191.7 2.1 collective-permute-start
  193.8 4.7 %collective-permute-start.3 = (bf16[128,1024]{1,0:T(8,128)(2,1)S(1)}, bf16[128,1024]{1,0:T(8,128)(2,1)S(1)}, u32[]{:S(2)}, u32[]{:S(2)}) collective-permute-start(bf16[128,1024]{1,0:T(8,128)(2,1)S(1)} %get-tuple-element.13), channel_id=1, source_target_pairs={{0,3},{1,2},{2,1},{3,0},{4,7},{5,6},{6,5},{7,4},{8,11},{9,10},{10,... | collective-permute-start | bytes 786440 | tf_op jit(solution)/shard_map/ppermute | solution.py:141
  198.5 7.6 %collective-permute-done.3.refs_0_ = bf16[128,1024]{1,0:T(8,128)(2,1)S(1)} collective-permute-done((bf16[128,1024]{1,0:T(8,128)(2,1)S(1)}, bf16[128,1024]{1,0:T(8,128)(2,1)S(1)}, u32[]{:S(2)}, u32[]{:S(2)}) %collective-permute-start.3) | collective-permute-done | bytes 262176 | tf_op jit(solution)/shard_map/ppermute | solution.py:141
  206.2 5.8 %all-to-all-done.2 = bf16[4,8,4,32,384]{4,3,2,1,0:T(8,128)(2,1)} async-done(((bf16[4,8,4,32,384]{4,3,2,1,0:T(8,128)(2,1)}), bf16[4,8,4,32,384]{4,3,2,1,0:T(8,128)(2,1)}, u32[]{:S(2)}, u32[]{:S(2)}) %all-to-all-start.2) | async-done | bytes 3145760 | tf_op jit(solution)/shard_map/all_to_all | solution.py:61
  212.0 5.4 %attend.1 = bf16[2,256,128]{2,1,0:T(8,128)(2,1)S(1)} custom-call(bf16[256,4096]{1,0:T(8,128)(2,1)S(1)} %copy-done.1, bf16[256,4096]{1,0:T(8,128)(2,1)} %collective-permute-done.other_ref, bf16[2,2,2,4,2,64,384]{6,5,4,3,2,1,0:T(8,128)(2,1)} %bitcast.5.w_ref, bf16[128,1024]{1,0:T(8,128)(2,1)S(1)} %collective-permute-done.3.refs_0_), custom_call_target="tpu_custom_call" | custom-call | flops 1610612736 | bytes 8388608 | tf_op jit(solution)/shard_map/attend/pallas_call | solution.py:145
  218.2 4.3 %all-to-all-start.3 = ((bf16[8,256,128]{2,1,0:T(8,128)(2,1)}), bf16[8,256,128]{2,1,0:T(8,128)(2,1)S(1)}, u32[]{:S(2)}, u32[]{:S(2)}) async-start(bf16[8,256,128]{2,1,0:T(8,128)(2,1)} %bitcast.6), calls=%async_computation.3 | async-start | bytes 1048576 | tf_op jit(solution)/shard_map/all_to_all | solution.py:157
  222.7 2.4 collective-permute-start.4
  225.2 1.8 collective-permute-done.4.partner_ref
  227.0 10.5 %all-to-all-done.3 = bf16[8,256,128]{2,1,0:T(8,128)(2,1)S(1)} async-done(((bf16[8,256,128]{2,1,0:T(8,128)(2,1)}), bf16[8,256,128]{2,1,0:T(8,128)(2,1)S(1)}, u32[]{:S(2)}, u32[]{:S(2)}) %all-to-all-start.3) | async-done | bytes 524320 | tf_op jit(solution)/shard_map/all_to_all | solution.py:157
  237.5 1.3 project.1
  238.8 8.2 %collective-permute-start.5 = (bf16[128,1024]{1,0:T(8,128)(2,1)S(1)}, bf16[128,1024]{1,0:T(8,128)(2,1)S(1)}, u32[]{:S(2)}, u32[]{:S(2)}) collective-permute-start(bf16[128,1024]{1,0:T(8,128)(2,1)S(1)} %get-tuple-element.16), channel_id=1, source_target_pairs={{0,4},{4,0},{1,5},{5,1},{2,6},{6,2},{3,7},{7,3},{8,12},{12,8},{9,1... | collective-permute-start | bytes 786440 | tf_op jit(solution)/shard_map/ppermute | solution.py:172
  247.0 21.8 %collective-permute-done.5 = bf16[128,1024]{1,0:T(8,128)(2,1)S(1)} collective-permute-done((bf16[128,1024]{1,0:T(8,128)(2,1)S(1)}, bf16[128,1024]{1,0:T(8,128)(2,1)S(1)}, u32[]{:S(2)}, u32[]{:S(2)}) %collective-permute-start.5) | collective-permute-done | bytes 262176 | tf_op jit(solution)/shard_map/ppermute | solution.py:172
  268.9 11.8 %all_to_all.26 = bf16[4,32,1024]{2,1,0:T(8,128)(2,1)S(1)} all-to-all(bf16[4,32,1024]{2,1,0:T(8,128)(2,1)S(1)} %bitcast.24), channel_id=1, replica_groups=mesh['zh'=2,'x'=4,'y'=8,'c'=2,'rg'=2,'cb'=4] {'cb'}, dimensions={0} | all-to-all | bytes 524288 | tf_op jit(solution)/shard_map/all_to_all | solution.py:175
  (26 shorter events, 2.7 us)
Async XLA Ops:
  0.0 69.9 %copy-start = (bf16[256,4096]{1,0:T(8,128)(2,1)S(1)}, bf16[256,4096]{1,0:T(8,128)(2,1)}, u32[]{:S(2)}) copy-start(bf16[256,4096]{1,0:T(8,128)(2,1)} %w_ref.1) | copy-start | bytes 6291460
  34.7 35.2 %copy-start.2 = (bf16[4,32,384]{2,1,0:T(8,128)(2,1)S(1)}, bf16[4,32,384]{2,1,0:T(8,128)(2,1)}, u32[]{:S(2)}) copy-start(bf16[4,32,384]{2,1,0:T(8,128)(2,1)} %all_to_all.25.block_ref.after_ref) | copy-start | bytes 294916
  59.7 30.0 %all-to-all-start.1 = ((bf16[8,4,32,384]{3,2,1,0:T(8,128)(2,1)}), bf16[8,4,32,384]{3,2,1,0:T(8,128)(2,1)}, u32[]{:S(2)}, u32[]{:S(2)}) async-start(bf16[8,4,32,384]{3,2,1,0:T(8,128)(2,1)} %copies.2), calls=%async_computation.1 | async-start | bytes 1572864 | tf_op jit(solution)/shard_map/all_to_all | solution.py:61
  70.5 13.2 %collective-permute-start.1 = (bf16[128,1024]{1,0:T(8,128)(2,1)S(1)}, bf16[128,1024]{1,0:T(8,128)(2,1)S(1)}, u32[]{:S(2)}, u32[]{:S(2)}) collective-permute-start(bf16[128,1024]{1,0:T(8,128)(2,1)S(1)} %get-tuple-element.11), channel_id=1, source_target_pairs={{0,1},{1,0},{2,3},{3,2},{4,5},{5,4},{6,7},{7,6},{8,9},{9,8},{10,11... | collective-permute-start | bytes 786440 | tf_op jit(solution)/shard_map/ppermute | solution.py:141
  72.4 14.9 %collective-permute-start.2 = (bf16[128,1024]{1,0:T(8,128)(2,1)S(1)}, bf16[128,1024]{1,0:T(8,128)(2,1)S(1)}, u32[]{:S(2)}, u32[]{:S(2)}) collective-permute-start(bf16[128,1024]{1,0:T(8,128)(2,1)S(1)} %get-tuple-element.12), channel_id=1, source_target_pairs={{0,2},{1,3},{2,0},{3,1},{4,6},{5,7},{6,4},{7,5},{8,10},{9,11},{10,... | collective-permute-start | bytes 786440 | tf_op jit(solution)/shard_map/ppermute | solution.py:141
  83.7 6.0 %copy-start.3 = (bf16[128,1024]{1,0:T(8,128)(2,1)}, bf16[128,1024]{1,0:T(8,128)(2,1)S(1)}, u32[]{:S(2)}) copy-start(bf16[128,1024]{1,0:T(8,128)(2,1)S(1)} %collective-permute-done.1.refs_0_) | copy-start | bytes 786436
  87.3 2.4 copy-start.5
  186.1 5.6 %copy-start.1 = (bf16[256,4096]{1,0:T(8,128)(2,1)S(1)}, bf16[256,4096]{1,0:T(8,128)(2,1)}, u32[]{:S(2)}) copy-start(bf16[256,4096]{1,0:T(8,128)(2,1)} %own_ref.1) | copy-start | bytes 6291460
  186.1 25.8 %all-to-all-start.2 = ((bf16[4,8,4,32,384]{4,3,2,1,0:T(8,128)(2,1)}), bf16[4,8,4,32,384]{4,3,2,1,0:T(8,128)(2,1)}, u32[]{:S(2)}, u32[]{:S(2)}) async-start(bf16[4,8,4,32,384]{4,3,2,1,0:T(8,128)(2,1)} %copies.3), calls=%async_computation.2 | async-start | bytes 6291456 | tf_op jit(solution)/shard_map/all_to_all | solution.py:61
  191.7 14.4 %collective-permute-start = (bf16[256,4096]{1,0:T(8,128)(2,1)S(1)}, bf16[256,4096]{1,0:T(8,128)(2,1)}, u32[]{:S(2)}, u32[]{:S(2)}) collective-permute-start(bf16[256,4096]{1,0:T(8,128)(2,1)S(1)} %copy-done.1), channel_id=1, source_target_pairs={{0,8},{8,0},{1,9},{9,1},{2,10},{10,2},{3,11},{11,3},{4,12},{12,4},... | collective-permute-start | bytes 6291464 | tf_op jit(solution)/shard_map/ppermute | solution.py:120
  193.8 12.3 %collective-permute-start.3 = (bf16[128,1024]{1,0:T(8,128)(2,1)S(1)}, bf16[128,1024]{1,0:T(8,128)(2,1)S(1)}, u32[]{:S(2)}, u32[]{:S(2)}) collective-permute-start(bf16[128,1024]{1,0:T(8,128)(2,1)S(1)} %get-tuple-element.13), channel_id=1, source_target_pairs={{0,3},{1,2},{2,1},{3,0},{4,7},{5,6},{6,5},{7,4},{8,11},{9,10},{10,... | collective-permute-start | bytes 786440 | tf_op jit(solution)/shard_map/ppermute | solution.py:141
  217.3 5.3 %copy-start.4 = (bf16[128,1024]{1,0:T(8,128)(2,1)S(1)}, bf16[128,1024]{1,0:T(8,128)(2,1)}, u32[]{:S(2)}) copy-start(bf16[128,1024]{1,0:T(8,128)(2,1)} %copy-done.3) | copy-start | bytes 786436
  217.3 5.3 %copy-start.6 = (bf16[128,1024]{1,0:T(8,128)(2,1)S(1)}, bf16[128,1024]{1,0:T(8,128)(2,1)}, u32[]{:S(2)}) copy-start(bf16[128,1024]{1,0:T(8,128)(2,1)} %copy-done.5) | copy-start | bytes 786436
  218.2 19.2 %all-to-all-start.3 = ((bf16[8,256,128]{2,1,0:T(8,128)(2,1)}), bf16[8,256,128]{2,1,0:T(8,128)(2,1)S(1)}, u32[]{:S(2)}, u32[]{:S(2)}) async-start(bf16[8,256,128]{2,1,0:T(8,128)(2,1)} %bitcast.6), calls=%async_computation.3 | async-start | bytes 1048576 | tf_op jit(solution)/shard_map/all_to_all | solution.py:157
  222.7 4.3 %collective-permute-start.4 = (bf16[3,128,1024]{2,1,0:T(8,128)(2,1)S(1)}, bf16[3,128,1024]{2,1,0:T(8,128)(2,1)S(1)}, u32[]{:S(2)}, u32[]{:S(2)}) collective-permute-start(bf16[3,128,1024]{2,1,0:T(8,128)(2,1)S(1)} %pad_maximum_fusion.held_ref), channel_id=1, source_target_pairs={{0,8},{8,0},{1,9},{9,1},{2,10},{10,2},{3,11},{11,3},{4,12},{12,4},... | collective-permute-start | bytes 2359304 | tf_op jit(solution)/shard_map/ppermute | solution.py:154
  238.8 30.0 %collective-permute-start.5 = (bf16[128,1024]{1,0:T(8,128)(2,1)S(1)}, bf16[128,1024]{1,0:T(8,128)(2,1)S(1)}, u32[]{:S(2)}, u32[]{:S(2)}) collective-permute-start(bf16[128,1024]{1,0:T(8,128)(2,1)S(1)} %get-tuple-element.16), channel_id=1, source_target_pairs={{0,4},{4,0},{1,5},{5,1},{2,6},{6,2},{3,7},{7,3},{8,12},{12,8},{9,1... | collective-permute-start | bytes 786440 | tf_op jit(solution)/shard_map/ppermute | solution.py:172

commit v5 on v3

--- a/solution.py
+++ b/solution.py
@@ -25,9 +25,36 @@
     for zh in range(ZH) for c in range(C) for px in range(2) for py in range(2)
 ]
 NEAR = [
-    [place(zh, 2 * xq + (1 - 2 * c) * px, 2 * yq + (1 - 2 * c) * py, c) for px in range(2) for py in range(2)]
-    for zh in range(ZH) for c in range(C) for xq in range(XQ) for yq in range(YQ)
+    [
+        (
+            place(zh, x, y, c),
+            place(
+                zh,
+                x + dx * (1 - 2 * (x % 2)) * (1 - 2 * c),
+                y + dy * (1 - 2 * (y % 2)) * (1 - 2 * c),
+                c,
+            ),
+        )
+        for zh in range(ZH) for x in range(X) for y in range(Y) for c in range(C)
+    ]
+    for dx, dy in ((0, 1), (1, 0), (1, 1))
 ]
+ANYWHERE = pl.BlockSpec(memory_space=pl.ANY)
+
+
+def behind_kernel(*refs):
+    pass
+
+
+def behind(array, after):
+    return pl.pallas_call(
+        behind_kernel,
+        out_shape=jax.ShapeDtypeStruct(array.shape, array.dtype),
+        in_specs=[ANYWHERE] * (1 + len(after)),
+        out_specs=ANYWHERE,
+        input_output_aliases={0: 0},
+        name="behind",
+    )(array, *after)
 
 
 def spread(block, groups):
@@ -36,21 +63,27 @@
     return lax.all_to_all(blocks, DP, 0, 0, axis_index_groups=groups, tiled=True)
 
 
-def attend_kernel(own_ref, other_ref, w_ref, *refs):
-    out_ref = refs[-1]
-    span = Y * w_ref.shape[5]
+def attend_kernel(place_ref, own_ref, other_ref, *refs):
+    w_refs, (out_ref, held_ref, sems) = refs[:4], refs[5:]
+    me = place_ref[0]
+    for i, w_ref in enumerate(w_refs):
+        pltpu.make_async_copy(w_ref, held_ref.at[me ^ i], sems.at[i]).start()
+    span = Y * held_ref.shape[4]
     totals = [None, None]
-    for zh in range(ZH):
-        for x in range(X):
-            weight = jnp.concatenate(
-                [w_ref[x % 2, y % 2, x // 2, y // 2, zh] for y in range(Y)], axis=0
-            )
-            start = (zh * X + x) * span
-            for g, ref in enumerate((own_ref, other_ref)):
-                product = jnp.dot(
-                    ref[:, start : start + span], weight, preferred_element_type=jnp.float32
+    for px in range(2):
+        for slot in (2 * px, 2 * px + 1):
+            pltpu.make_async_copy(w_refs[0], held_ref.at[slot], sems.at[me ^ slot]).wait()
+        for zh in range(ZH):
+            for xq in range(XQ):
+                weight = jnp.concatenate(
+                    [held_ref[2 * px + y % 2, xq, y // 2, zh] for y in range(Y)], axis=0
                 )
-                totals[g] = product if totals[g] is None else totals[g] + product
+                start = (zh * X + 2 * xq + px) * span
+                for g, ref in enumerate((own_ref, other_ref)):
+                    product = jnp.dot(
+                        ref[:, start : start + span], weight, preferred_element_type=jnp.float32
+                    )
+                    totals[g] = product if totals[g] is None else totals[g] + product
     for g in range(2):
         projected = totals[g].astype(jnp.bfloat16)
         queries, key_rows, values = (projected[:, i * HD : (i + 1) * HD] for i in range(3))
@@ -98,8 +131,7 @@
     heads = jnp.broadcast_to(heads[None], (ZH,) + heads.shape).reshape(ZH * C, k_rows, 3 * HD)
     heads = lax.all_to_all(heads, ("zh", "c"), 0, 0, tiled=True)
     first = heads
-    heads = spread(spread(heads, FAR), NEAR)
-    heads = heads.reshape(2, 2, XQ, YQ, ZH, C * k_rows, 3 * HD)
+    heads = spread(heads, FAR)
 
     column, half, core = lax.axis_index("cb"), lax.axis_index("rg"), lax.axis_index("c")
     depth, columns = out_weight.shape[0], out_weight.shape[1] // CB
@@ -116,14 +148,19 @@
     )(jnp.stack([column, core]), out_weight, first)
     held = [lax.ppermute(block, "cb", [(j, j ^ (i + 1)) for j in range(CB)]) for i, block in enumerate(sent)]
 
+    heads = behind(heads, held[:2]).reshape(XQ, YQ, ZH, C * k_rows, 3 * HD)
+    squares = [heads] + [lax.ppermute(heads, DP, pairs) for pairs in NEAR]
+    parity = lax.axis_index("x") % 2 * 2 + lax.axis_index("y") % 2
+
     mixed = pl.pallas_call(
         attend_kernel,
         out_shape=jax.ShapeDtypeStruct((2, rows, HD), jnp.bfloat16),
-        in_specs=[vmem] * 3 + [pl.BlockSpec(memory_space=pl.ANY)] * len(held),
+        in_specs=[smem] + [vmem] * 2 + [ANYWHERE] * 5,
+        scratch_shapes=[pltpu.VMEM((4,) + heads.shape, jnp.bfloat16), pltpu.SemaphoreType.DMA((4,))],
         compiler_params=pltpu.CompilerParams(vmem_limit_bytes=48 << 20),
         cost_estimate=pl.CostEstimate(flops=2 * 2 * rows * width * 3 * HD, bytes_accessed=8 << 20, transcendentals=0),
         name="attend",
-    )(tokens, other, heads, *held)
+    )(parity[None], tokens, other, *squares, held[2])
     held = jnp.stack(held)
     partner = lax.ppermute(held, "c", [(0, 1), (1, 0)])
     mixed = jnp.where(core == 0, mixed, mixed[::-1])

time: 178 us -> 167 us (0.938); the launches traced: 176 us -> 167 us
  blocking collectives: 74.1 us -> 45.3 us
  starting transfers between devices: 37.6 us -> 47.1 us
  waiting for transfers between devices: 49.7 us -> 58.1 us
    all_to_all x1 -> x0, blocking collectives: 28.8 us -> none  [spread(): lax.all_to_all(blocks, DP, 0, 0, axis_index_groups=groups, tiled=True)]
    ppermute x0 -> x3, starting transfers between devices: none -> 9.2 us  [body(): squares = [heads] + [lax.ppermute(heads, DP, pairs) for pairs in NEAR]]
    ppermute x3, waiting for transfers between devices: 15.6 us -> 21.7 us  [body(): lax.ppermute(block, 'cb', [(j, j ^ i + 1) for j in range(CB)])]
    all_to_all x1, starting transfers between devices: 5.58 us -> 10.1 us  [spread(): lax.all_to_all(blocks, DP, 0, 0, axis_index_groups=groups, tiled=True)]
    all_to_all x1, starting transfers between devices: 8.97 us -> 4.69 us  [body(): lax.all_to_all(mixed, ('c', 'cb'), 0, 0, tiled=True)]
    ppermute x0 -> x3, waiting for transfers between devices: none -> 3.33 us  [body(): squares = [heads] + [lax.ppermute(heads, DP, pairs) for pairs in NEAR]]
  transfers between devices with their start and end apart: 8 -> 11, of which waited for: 5 -> 7; matrix products, arithmetic and copies ran while one was open for 0% -> 1% of each run, Pallas kernels for 0% -> 0%
where the time goes in v5:
time: 167 us
  waiting for transfers between devices  58.1 us (35%)
  starting transfers between devices  47.1 us (28%)
  blocking collectives  45.3 us (27%)
  Pallas kernels  8.07 us (5%)
  local copies, waits for them, and re-layouts  6.49 us (4%)
    all_to_all x1, blocking collectives, body(): heads = lax.all_to_all(heads, ('zh', 'c'), 0, 0, tiled=True)  33.5 us
    ppermute x1, waiting for transfers between devices, body(): far = lax.ppermute(far, 'rg', [(0, 1), (1, 0)])  21.8 us
    ppermute x3, waiting for transfers between devices, body(): lax.ppermute(block, 'cb', [(j, j ^ i + 1) for j in range(CB)])  21.7 us
    all_to_all x1, blocking collectives, body(): summed = lax.all_to_all(summed, 'cb', 0, 0, tiled=True)  11.8 us
    ppermute x3, starting transfers between devices, body(): lax.ppermute(block, 'cb', [(j, j ^ i + 1) for j in range(CB)])  10.2 us
    all_to_all x1, starting transfers between devices, spread(): lax.all_to_all(blocks, DP, 0, 0, axis_index_groups=groups, tiled=True)  10.1 us
    all_to_all x1, waiting for transfers between devices, body(): lax.all_to_all(mixed, ('c', 'cb'), 0, 0, tiled=True)  9.53 us
    ppermute x3, starting transfers between devices, body(): squares = [heads] + [lax.ppermute(heads, DP, pairs) for pairs in NEAR]  9.2 us
  transfers between devices with their start and end apart: 11, of which 7 were waited for; matrix products, arithmetic and copies ran while one was open for 1% of the time, Pallas kernels for 0%

profile of v5, /device:TPU:6, one launch (start us, length us, event | category | flops | bytes accessed | tf_op | source)
XLA Modules:
  0.0 166.5 jit_solution(13800650622100362339)
XLA Ops:
  1.1 33.5 %all_to_all.20.after_ref = bf16[4,32,384]{2,1,0:T(8,128)(2,1)S(1)} all-to-all(bf16[4,32,384]{2,1,0:T(8,128)(2,1)S(1)} %bitcast.29), channel_id=1, replica_groups=mesh['zh'=2,'x'=4,'y'=8,'c'=2,'rg'=2,'cb'=4] {'zh','c'}, dimensions={0} | all-to-all | bytes 196608 | tf_op jit(solution)/shard_map/all_to_all | solution.py:132
  35.6 10.1 %all-to-all-start.1 = ((bf16[8,4,32,384]{3,2,1,0:T(8,128)(2,1)}), bf16[8,4,32,384]{3,2,1,0:T(8,128)(2,1)S(1)}, u32[]{:S(2)}, u32[]{:S(2)}) async-start(bf16[8,4,32,384]{3,2,1,0:T(8,128)(2,1)} %broadcast_in_dim.25), calls=%async_computation.1 | async-start | bytes 1572864 | tf_op jit(solution)/shard_map/all_to_all | solution.py:63
  45.6 1.9 %collective-permute-start = (bf16[256,4096]{1,0:T(8,128)(2,1)}, bf16[256,4096]{1,0:T(8,128)(2,1)}, u32[]{:S(2)}, u32[]{:S(2)}) collective-permute-start(bf16[256,4096]{1,0:T(8,128)(2,1)} %own_ref.1), channel_id=1, source_target_pairs={{0,8},{8,0},{1,9},{9,1},{2,10},{10,2},{3,11},{11,3},{4,12},{12,4},... | collective-permute-start | bytes 6291464 | tf_op jit(solution)/shard_map/ppermute | solution.py:128
  49.1 2.0 %collective-permute-start.1 = (bf16[128,1024]{1,0:T(8,128)(2,1)S(1)}, bf16[128,1024]{1,0:T(8,128)(2,1)S(1)}, u32[]{:S(2)}, u32[]{:S(2)}) collective-permute-start(bf16[128,1024]{1,0:T(8,128)(2,1)S(1)} %get-tuple-element.11), channel_id=1, source_target_pairs={{0,1},{1,0},{2,3},{3,2},{4,5},{5,4},{6,7},{7,6},{8,9},{9,8},{10,11... | collective-permute-start | bytes 786440 | tf_op jit(solution)/shard_map/ppermute | solution.py:149
  51.1 3.8 %collective-permute-start.2 = (bf16[128,1024]{1,0:T(8,128)(2,1)S(1)}, bf16[128,1024]{1,0:T(8,128)(2,1)}, u32[]{:S(2)}, u32[]{:S(2)}) collective-permute-start(bf16[128,1024]{1,0:T(8,128)(2,1)S(1)} %get-tuple-element.12), channel_id=1, source_target_pairs={{0,2},{1,3},{2,0},{3,1},{4,6},{5,7},{6,4},{7,5},{8,10},{9,11},{10,... | collective-permute-start | bytes 786440 | tf_op jit(solution)/shard_map/ppermute | solution.py:149
  54.9 8.5 %collective-permute-done.1.refs_1_ = bf16[128,1024]{1,0:T(8,128)(2,1)S(1)} collective-permute-done((bf16[128,1024]{1,0:T(8,128)(2,1)S(1)}, bf16[128,1024]{1,0:T(8,128)(2,1)S(1)}, u32[]{:S(2)}, u32[]{:S(2)}) %collective-permute-start.1) | collective-permute-done | bytes 262176 | tf_op jit(solution)/shard_map/ppermute | solution.py:149
  63.4 5.0 %collective-permute-done.2.refs_2_ = bf16[128,1024]{1,0:T(8,128)(2,1)} collective-permute-done((bf16[128,1024]{1,0:T(8,128)(2,1)S(1)}, bf16[128,1024]{1,0:T(8,128)(2,1)}, u32[]{:S(2)}, u32[]{:S(2)}) %collective-permute-start.2) | collective-permute-done | bytes 262176 | tf_op jit(solution)/shard_map/ppermute | solution.py:149
  69.3 2.6 %collective-permute-start.3 = (bf16[2,4,2,64,384]{4,3,2,1,0:T(8,128)(2,1)}, bf16[2,4,2,64,384]{4,3,2,1,0:T(8,128)(2,1)S(1)}, u32[]{:S(2)}, u32[]{:S(2)}) collective-permute-start(bf16[2,4,2,64,384]{4,3,2,1,0:T(8,128)(2,1)} %bitcast.20), channel_id=1, source_target_pairs={{0,16},{8,120},{16,0},{24,40},{32,48},{40,24},{48,32},{56,72},{64,... | collective-permute-start | bytes 2359304 | tf_op jit(solution)/shard_map/ppermute | solution.py:152
  71.9 2.7 %collective-permute-start.4 = (bf16[2,4,2,64,384]{4,3,2,1,0:T(8,128)(2,1)}, bf16[2,4,2,64,384]{4,3,2,1,0:T(8,128)(2,1)}, u32[]{:S(2)}, u32[]{:S(2)}) collective-permute-start(bf16[2,4,2,64,384]{4,3,2,1,0:T(8,128)(2,1)} %bitcast.21), channel_id=1, source_target_pairs={{0,128},{8,392},{16,144},{24,408},{32,160},{40,424},{48,176},{56,4... | collective-permute-start | bytes 2359304 | tf_op jit(solution)/shard_map/ppermute | solution.py:152
  74.6 3.9 %collective-permute-start.5 = (bf16[2,4,2,64,384]{4,3,2,1,0:T(8,128)(2,1)}, bf16[2,4,2,64,384]{4,3,2,1,0:T(8,128)(2,1)}, u32[]{:S(2)}, u32[]{:S(2)}) collective-permute-start(bf16[2,4,2,64,384]{4,3,2,1,0:T(8,128)(2,1)} %bitcast.22), channel_id=1, source_target_pairs={{0,144},{8,504},{16,128},{24,424},{32,176},{40,408},{48,160},{56,4... | collective-permute-start | bytes 2359304 | tf_op jit(solution)/shard_map/ppermute | solution.py:152
  78.5 4.4 %collective-permute-start.6 = (bf16[128,1024]{1,0:T(8,128)(2,1)S(1)}, bf16[128,1024]{1,0:T(8,128)(2,1)S(1)}, u32[]{:S(2)}, u32[]{:S(2)}) collective-permute-start(bf16[128,1024]{1,0:T(8,128)(2,1)S(1)} %get-tuple-element.13), channel_id=1, source_target_pairs={{0,3},{1,2},{2,1},{3,0},{4,7},{5,6},{6,5},{7,4},{8,11},{9,10},{10,... | collective-permute-start | bytes 786440 | tf_op jit(solution)/shard_map/ppermute | solution.py:149
  83.0 8.2 %collective-permute-done.6.refs_4_ = bf16[128,1024]{1,0:T(8,128)(2,1)S(1)} collective-permute-done((bf16[128,1024]{1,0:T(8,128)(2,1)S(1)}, bf16[128,1024]{1,0:T(8,128)(2,1)S(1)}, u32[]{:S(2)}, u32[]{:S(2)}) %collective-permute-start.6) | collective-permute-done | bytes 262176 | tf_op jit(solution)/shard_map/ppermute | solution.py:149
  91.2 3.3 %collective-permute-done.4.refs_2_ = bf16[2,4,2,64,384]{4,3,2,1,0:T(8,128)(2,1)} collective-permute-done((bf16[2,4,2,64,384]{4,3,2,1,0:T(8,128)(2,1)}, bf16[2,4,2,64,384]{4,3,2,1,0:T(8,128)(2,1)}, u32[]{:S(2)}, u32[]{:S(2)}) %collective-permute-start.4) | collective-permute-done | bytes 786464 | tf_op jit(solution)/shard_map/ppermute | solution.py:152
  94.5 1.1 copy-done.1
  95.7 6.1 %attend.1 = bf16[2,256,128]{2,1,0:T(8,128)(2,1)S(1)} custom-call(s32[1]{0:T(128)} %bitcast.3.place_ref, bf16[256,4096]{1,0:T(8,128)(2,1)S(1)} %copy-done.3, bf16[256,4096]{1,0:T(8,128)(2,1)} %collective-permute-done.other_ref, bf16[2,4,2,64,384]{4,3,2,1,0:T(8,128)(2,1)S(1)} %bitcast.23, bf16[2,4,2,64,384]{4,3,2,1,0:T(8,128)(2,1)S(1)} %collective-permute-done.3.refs_1_, ...), custom_call_target="tpu_custom_call" | custom-call | flops 1610612736 | bytes 8388608 | tf_op jit(solution)/shard_map/attend/pallas_call | solution.py:155
  102.7 4.7 %all-to-all-start.2 = ((bf16[8,256,128]{2,1,0:T(8,128)(2,1)}), bf16[8,256,128]{2,1,0:T(8,128)(2,1)S(1)}, u32[]{:S(2)}, u32[]{:S(2)}) async-start(bf16[8,256,128]{2,1,0:T(8,128)(2,1)} %bitcast.7), calls=%async_computation.2 | async-start | bytes 1048576 | tf_op jit(solution)/shard_map/all_to_all | solution.py:168
  107.4 1.0 pad_maximum_fusion.held_ref
  108.5 2.4 %collective-permute-start.7 = (bf16[3,128,1024]{2,1,0:T(8,128)(2,1)S(1)}, bf16[3,128,1024]{2,1,0:T(8,128)(2,1)S(1)}, u32[]{:S(2)}, u32[]{:S(2)}) collective-permute-start(bf16[3,128,1024]{2,1,0:T(8,128)(2,1)S(1)} %pad_maximum_fusion.held_ref), channel_id=1, source_target_pairs={{0,8},{8,0},{1,9},{9,1},{2,10},{10,2},{3,11},{11,3},{4,12},{12,4},... | collective-permute-start | bytes 2359304 | tf_op jit(solution)/shard_map/ppermute | solution.py:165
  111.0 1.8 %collective-permute-done.7.partner_ref = bf16[3,128,1024]{2,1,0:T(8,128)(2,1)S(1)} collective-permute-done((bf16[3,128,1024]{2,1,0:T(8,128)(2,1)S(1)}, bf16[3,128,1024]{2,1,0:T(8,128)(2,1)S(1)}, u32[]{:S(2)}, u32[]{:S(2)}) %collective-permute-start.7) | collective-permute-done | bytes 786464 | tf_op jit(solution)/shard_map/ppermute | solution.py:165
  112.8 9.5 %all-to-all-done.2 = bf16[8,256,128]{2,1,0:T(8,128)(2,1)S(1)} async-done(((bf16[8,256,128]{2,1,0:T(8,128)(2,1)}), bf16[8,256,128]{2,1,0:T(8,128)(2,1)S(1)}, u32[]{:S(2)}, u32[]{:S(2)}) %all-to-all-start.2) | async-done | bytes 524320 | tf_op jit(solution)/shard_map/all_to_all | solution.py:168
  122.3 1.3 project.1
  123.6 8.5 %collective-permute-start.8 = (bf16[128,1024]{1,0:T(8,128)(2,1)S(1)}, bf16[128,1024]{1,0:T(8,128)(2,1)S(1)}, u32[]{:S(2)}, u32[]{:S(2)}) collective-permute-start(bf16[128,1024]{1,0:T(8,128)(2,1)S(1)} %get-tuple-element.16), channel_id=1, source_target_pairs={{0,4},{4,0},{1,5},{5,1},{2,6},{6,2},{3,7},{7,3},{8,12},{12,8},{9,1... | collective-permute-start | bytes 786440 | tf_op jit(solution)/shard_map/ppermute | solution.py:183
  132.2 21.8 %collective-permute-done.8 = bf16[128,1024]{1,0:T(8,128)(2,1)S(1)} collective-permute-done((bf16[128,1024]{1,0:T(8,128)(2,1)S(1)}, bf16[128,1024]{1,0:T(8,128)(2,1)S(1)}, u32[]{:S(2)}, u32[]{:S(2)}) %collective-permute-start.8) | collective-permute-done | bytes 262176 | tf_op jit(solution)/shard_map/ppermute | solution.py:183
  154.0 11.8 %all_to_all.21 = bf16[4,32,1024]{2,1,0:T(8,128)(2,1)S(1)} all-to-all(bf16[4,32,1024]{2,1,0:T(8,128)(2,1)S(1)} %bitcast.27), channel_id=1, replica_groups=mesh['zh'=2,'x'=4,'y'=8,'c'=2,'rg'=2,'cb'=4] {'cb'}, dimensions={0} | all-to-all | bytes 524288 | tf_op jit(solution)/shard_map/all_to_all | solution.py:186
  (32 shorter events, 6.2 us)
Async XLA Ops:
  0.0 47.6 %copy-start.2 = (bf16[256,4096]{1,0:T(8,128)(2,1)S(1)}, bf16[256,4096]{1,0:T(8,128)(2,1)}, u32[]{:S(2)}) copy-start(bf16[256,4096]{1,0:T(8,128)(2,1)} %w_ref.1) | copy-start | bytes 6291460
  35.6 32.8 %all-to-all-start.1 = ((bf16[8,4,32,384]{3,2,1,0:T(8,128)(2,1)}), bf16[8,4,32,384]{3,2,1,0:T(8,128)(2,1)S(1)}, u32[]{:S(2)}, u32[]{:S(2)}) async-start(bf16[8,4,32,384]{3,2,1,0:T(8,128)(2,1)} %broadcast_in_dim.25), calls=%async_computation.1 | async-start | bytes 1572864 | tf_op jit(solution)/shard_map/all_to_all | solution.py:63
  45.6 45.5 %collective-permute-start = (bf16[256,4096]{1,0:T(8,128)(2,1)}, bf16[256,4096]{1,0:T(8,128)(2,1)}, u32[]{:S(2)}, u32[]{:S(2)}) collective-permute-start(bf16[256,4096]{1,0:T(8,128)(2,1)} %own_ref.1), channel_id=1, source_target_pairs={{0,8},{8,0},{1,9},{9,1},{2,10},{10,2},{3,11},{11,3},{4,12},{12,4},... | collective-permute-start | bytes 6291464 | tf_op jit(solution)/shard_map/ppermute | solution.py:128
  48.3 0.8 copy-start.4
  49.1 45.4 %copy-start.3 = (bf16[256,4096]{1,0:T(8,128)(2,1)S(1)}, bf16[256,4096]{1,0:T(8,128)(2,1)}, u32[]{:S(2)}) copy-start(bf16[256,4096]{1,0:T(8,128)(2,1)} %own_ref.1) | copy-start | bytes 6291460
  49.1 14.4 %collective-permute-start.1 = (bf16[128,1024]{1,0:T(8,128)(2,1)S(1)}, bf16[128,1024]{1,0:T(8,128)(2,1)S(1)}, u32[]{:S(2)}, u32[]{:S(2)}) collective-permute-start(bf16[128,1024]{1,0:T(8,128)(2,1)S(1)} %get-tuple-element.11), channel_id=1, source_target_pairs={{0,1},{1,0},{2,3},{3,2},{4,5},{5,4},{6,7},{7,6},{8,9},{9,8},{10,11... | collective-permute-start | bytes 786440 | tf_op jit(solution)/shard_map/ppermute | solution.py:149
  51.1 17.3 %collective-permute-start.2 = (bf16[128,1024]{1,0:T(8,128)(2,1)S(1)}, bf16[128,1024]{1,0:T(8,128)(2,1)}, u32[]{:S(2)}, u32[]{:S(2)}) collective-permute-start(bf16[128,1024]{1,0:T(8,128)(2,1)S(1)} %get-tuple-element.12), channel_id=1, source_target_pairs={{0,2},{1,3},{2,0},{3,1},{4,6},{5,7},{6,4},{7,5},{8,10},{9,11},{10,... | collective-permute-start | bytes 786440 | tf_op jit(solution)/shard_map/ppermute | solution.py:149
  63.4 5.0 %copy-start.6 = (bf16[128,1024]{1,0:T(8,128)(2,1)}, bf16[128,1024]{1,0:T(8,128)(2,1)S(1)}, u32[]{:S(2)}) copy-start(bf16[128,1024]{1,0:T(8,128)(2,1)S(1)} %collective-permute-done.1.refs_1_) | copy-start | bytes 786436
  68.4 0.9 copy-start
  69.3 21.9 %collective-permute-start.3 = (bf16[2,4,2,64,384]{4,3,2,1,0:T(8,128)(2,1)}, bf16[2,4,2,64,384]{4,3,2,1,0:T(8,128)(2,1)S(1)}, u32[]{:S(2)}, u32[]{:S(2)}) collective-permute-start(bf16[2,4,2,64,384]{4,3,2,1,0:T(8,128)(2,1)} %bitcast.20), channel_id=1, source_target_pairs={{0,16},{8,120},{16,0},{24,40},{32,48},{40,24},{48,32},{56,72},{64,... | collective-permute-start | bytes 2359304 | tf_op jit(solution)/shard_map/ppermute | solution.py:152
  71.9 22.6 %collective-permute-start.4 = (bf16[2,4,2,64,384]{4,3,2,1,0:T(8,128)(2,1)}, bf16[2,4,2,64,384]{4,3,2,1,0:T(8,128)(2,1)}, u32[]{:S(2)}, u32[]{:S(2)}) collective-permute-start(bf16[2,4,2,64,384]{4,3,2,1,0:T(8,128)(2,1)} %bitcast.21), channel_id=1, source_target_pairs={{0,128},{8,392},{16,144},{24,408},{32,160},{40,424},{48,176},{56,4... | collective-permute-start | bytes 2359304 | tf_op jit(solution)/shard_map/ppermute | solution.py:152
  74.6 19.9 %collective-permute-start.5 = (bf16[2,4,2,64,384]{4,3,2,1,0:T(8,128)(2,1)}, bf16[2,4,2,64,384]{4,3,2,1,0:T(8,128)(2,1)}, u32[]{:S(2)}, u32[]{:S(2)}) collective-permute-start(bf16[2,4,2,64,384]{4,3,2,1,0:T(8,128)(2,1)} %bitcast.22), channel_id=1, source_target_pairs={{0,144},{8,504},{16,128},{24,424},{32,176},{40,408},{48,160},{56,4... | collective-permute-start | bytes 2359304 | tf_op jit(solution)/shard_map/ppermute | solution.py:152
  78.5 12.6 %collective-permute-start.6 = (bf16[128,1024]{1,0:T(8,128)(2,1)S(1)}, bf16[128,1024]{1,0:T(8,128)(2,1)S(1)}, u32[]{:S(2)}, u32[]{:S(2)}) collective-permute-start(bf16[128,1024]{1,0:T(8,128)(2,1)S(1)} %get-tuple-element.13), channel_id=1, source_target_pairs={{0,3},{1,2},{2,1},{3,0},{4,7},{5,6},{6,5},{7,4},{8,11},{9,10},{10,... | collective-permute-start | bytes 786440 | tf_op jit(solution)/shard_map/ppermute | solution.py:149
  94.5 1.1 copy-start.1
  101.8 5.6 %copy-start.7 = (bf16[128,1024]{1,0:T(8,128)(2,1)S(1)}, bf16[128,1024]{1,0:T(8,128)(2,1)}, u32[]{:S(2)}) copy-start(bf16[128,1024]{1,0:T(8,128)(2,1)} %copy-done.6) | copy-start | bytes 786436
  101.8 20.5 %copy-start.5 = (bf16[256,1024]{1,0:T(8,128)(2,1)S(1)}, bf16[256,1024]{1,0:T(8,128)(2,1)}, u32[]{:S(2)}) copy-start(bf16[256,1024]{1,0:T(8,128)(2,1)} %copy-done.4) | copy-start | bytes 1572868
  102.7 19.6 %all-to-all-start.2 = ((bf16[8,256,128]{2,1,0:T(8,128)(2,1)}), bf16[8,256,128]{2,1,0:T(8,128)(2,1)S(1)}, u32[]{:S(2)}, u32[]{:S(2)}) async-start(bf16[8,256,128]{2,1,0:T(8,128)(2,1)} %bitcast.7), calls=%async_computation.2 | async-start | bytes 1048576 | tf_op jit(solution)/shard_map/all_to_all | solution.py:168
  108.5 4.3 %collective-permute-start.7 = (bf16[3,128,1024]{2,1,0:T(8,128)(2,1)S(1)}, bf16[3,128,1024]{2,1,0:T(8,128)(2,1)S(1)}, u32[]{:S(2)}, u32[]{:S(2)}) collective-permute-start(bf16[3,128,1024]{2,1,0:T(8,128)(2,1)S(1)} %pad_maximum_fusion.held_ref), channel_id=1, source_target_pairs={{0,8},{8,0},{1,9},{9,1},{2,10},{10,2},{3,11},{11,3},{4,12},{12,4},... | collective-permute-start | bytes 2359304 | tf_op jit(solution)/shard_map/ppermute | solution.py:165
  123.6 30.3 %collective-permute-start.8 = (bf16[128,1024]{1,0:T(8,128)(2,1)S(1)}, bf16[128,1024]{1,0:T(8,128)(2,1)S(1)}, u32[]{:S(2)}, u32[]{:S(2)}) collective-permute-start(bf16[128,1024]{1,0:T(8,128)(2,1)S(1)} %get-tuple-element.16), channel_id=1, source_target_pairs={{0,4},{4,0},{1,5},{5,1},{2,6},{6,2},{3,7},{7,3},{8,12},{12,8},{9,1... | collective-permute-start | bytes 786440 | tf_op jit(solution)/shard_map/ppermute | solution.py:183

commit v6 on v5

--- a/solution.py
+++ b/solution.py
@@ -57,9 +57,20 @@
     )(array, *after)
 
 
-def spread(block, groups):
-    n = len(groups[0])
-    blocks = jnp.broadcast_to(block[None], (n,) + block.shape)
+def copies_kernel(block_ref, after_ref, out_ref):
+    for i in range(out_ref.shape[0]):
+        out_ref[i] = block_ref[...]
+
+
+def spread(block, groups, after):
+    vmem = pl.BlockSpec(memory_space=pltpu.VMEM)
+    blocks = pl.pallas_call(
+        copies_kernel,
+        out_shape=jax.ShapeDtypeStruct((len(groups[0]),) + block.shape, block.dtype),
+        in_specs=[vmem, ANYWHERE],
+        out_specs=vmem,
+        name="copies",
+    )(block, after)
     return lax.all_to_all(blocks, DP, 0, 0, axis_index_groups=groups, tiled=True)
 
 
@@ -95,7 +106,7 @@
         out_ref[g] = jnp.dot(attn, values, preferred_element_type=jnp.float32).astype(jnp.bfloat16)
 
 
-def split_kernel(place_ref, w_ref, after_ref, own_ref, *out_refs):
+def split_kernel(place_ref, w_ref, own_ref, *out_refs):
     column, core = place_ref[0], place_ref[1]
     part, width = out_refs[0].shape
     own_ref[...] = w_ref[:, pl.ds(pl.multiple_of(column * width, width), width)]
@@ -130,8 +141,6 @@
     heads = qkv_weight.reshape(k_rows, 3, C, HD).transpose(2, 0, 1, 3).reshape(C, k_rows, 3 * HD)
     heads = jnp.broadcast_to(heads[None], (ZH,) + heads.shape).reshape(ZH * C, k_rows, 3 * HD)
     heads = lax.all_to_all(heads, ("zh", "c"), 0, 0, tiled=True)
-    first = heads
-    heads = spread(heads, FAR)
 
     column, half, core = lax.axis_index("cb"), lax.axis_index("rg"), lax.axis_index("c")
     depth, columns = out_weight.shape[0], out_weight.shape[1] // CB
@@ -140,15 +149,16 @@
         split_kernel,
         out_shape=[jax.ShapeDtypeStruct((depth, columns), jnp.bfloat16)]
         + [jax.ShapeDtypeStruct((depth // C, columns), jnp.bfloat16)] * (CB - 1),
-        in_specs=[smem, vmem, vmem],
+        in_specs=[smem, vmem],
         out_specs=[vmem] * CB,
         compiler_params=pltpu.CompilerParams(vmem_limit_bytes=24 << 20),
         cost_estimate=pl.CostEstimate(flops=0, bytes_accessed=4 << 20, transcendentals=0),
         name="split",
-    )(jnp.stack([column, core]), out_weight, first)
+    )(jnp.stack([column, core]), out_weight)
     held = [lax.ppermute(block, "cb", [(j, j ^ (i + 1)) for j in range(CB)]) for i, block in enumerate(sent)]
 
-    heads = behind(heads, held[:2]).reshape(XQ, YQ, ZH, C * k_rows, 3 * HD)
+    heads = spread(heads, FAR, held[0])
+    heads = behind(heads, held[1:2]).reshape(XQ, YQ, ZH, C * k_rows, 3 * HD)
     squares = [heads] + [lax.ppermute(heads, DP, pairs) for pairs in NEAR]
     parity = lax.axis_index("x") % 2 * 2 + lax.axis_index("y") % 2
 

time: 167 us -> 170 us (1.018); the launches traced: 167 us -> 167 us
  blocking collectives: 45.3 us -> 11.8 us
  starting transfers between devices: 47.1 us -> 64.9 us
  waiting for transfers between devices: 58.1 us -> 69.8 us
  local copies, waits for them, and re-layouts: 6.49 us -> 8.9 us
  Pallas kernels: 8.07 us -> 9.91 us
    all_to_all x1 -> x0, blocking collectives: 33.5 us -> none  [body(): heads = lax.all_to_all(heads, ('zh', 'c'), 0, 0, tiled=True)]
    all_to_all x0 -> x1, starting transfers between devices: none -> 18.7 us  [body(): heads = lax.all_to_all(heads, ('zh', 'c'), 0, 0, tiled=True)]
    ppermute x3, waiting for transfers between devices: 21.7 us -> 30.5 us  [body(): lax.ppermute(block, 'cb', [(j, j ^ i + 1) for j in range(CB)])]
    unnamed x16 -> x18, local copies, waits for them, and re-layouts: 2.84 us -> 5.75 us
    ppermute x1, starting transfers between devices: 8.54 us -> 6.35 us  [body(): far = lax.ppermute(far, 'rg', [(0, 1), (1, 0)])]
    all_to_all x1, waiting for transfers between devices: 0.01 us -> 2 us  [spread(): lax.all_to_all(blocks, DP, 0, 0, axis_index_groups=groups, tiled=True)]
    pallas_call x0 -> x1, Pallas kernels: none -> 1.84 us  [spread(): pl.pallas_call(copies_kernel, out_shape=jax.ShapeDtypeStruct((len(groups[...]
  transfers between devices with their start and end apart: 11 -> 12, of which waited for: 7 -> 8; matrix products, arithmetic and copies ran while one was open for 1% -> 1% of each run, Pallas kernels for 0% -> 0%
where the time goes in v6:
time: 170 us; the launch traced here: 167 us
  waiting for transfers between devices  69.8 us (41%)
  starting transfers between devices  64.9 us (38%)
  blocking collectives  11.8 us (7%)
  Pallas kernels  9.91 us (6%)
  local copies, waits for them, and re-layouts  8.9 us (5%)
    ppermute x3, waiting for transfers between devices, body(): lax.ppermute(block, 'cb', [(j, j ^ i + 1) for j in range(CB)])  30.5 us
    ppermute x1, waiting for transfers between devices, body(): far = lax.ppermute(far, 'rg', [(0, 1), (1, 0)])  23 us
    all_to_all x1, starting transfers between devices, body(): heads = lax.all_to_all(heads, ('zh', 'c'), 0, 0, tiled=True)  18.7 us
    ppermute x3, starting transfers between devices, body(): lax.ppermute(block, 'cb', [(j, j ^ i + 1) for j in range(CB)])  11.8 us
    all_to_all x1, blocking collectives, body(): summed = lax.all_to_all(summed, 'cb', 0, 0, tiled=True)  11.8 us
    all_to_all x1, starting transfers between devices, spread(): lax.all_to_all(blocks, DP, 0, 0, axis_index_groups=groups, tiled=True)  10.1 us
    all_to_all x1, waiting for transfers between devices, body(): lax.all_to_all(mixed, ('c', 'cb'), 0, 0, tiled=True)  9.53 us
    ppermute x3, starting transfers between devices, body(): squares = [heads] + [lax.ppermute(heads, DP, pairs) for pairs in NEAR]  9.2 us
  transfers between devices with their start and end apart: 12, of which 8 were waited for; matrix products, arithmetic and copies ran while one was open for 1% of the time, Pallas kernels for 0%

profile of v6, /device:TPU:6, one launch (start us, length us, event | category | flops | bytes accessed | tf_op | source)
XLA Modules:
  0.0 166.8 jit_solution(7926971812432243292)
XLA Ops:
  1.6 18.7 %all-to-all-start = ((bf16[4,32,384]{2,1,0:T(8,128)(2,1)}), bf16[4,32,384]{2,1,0:T(8,128)(2,1)S(1)}, u32[]{:S(2)}, u32[]{:S(2)}) async-start(bf16[4,32,384]{2,1,0:T(8,128)(2,1)} %bitcast.5), calls=%async_computation | async-start | bytes 196608 | tf_op jit(solution)/shard_map/all_to_all | solution.py:143
  20.4 1.6 copy-done.2
  23.4 3.4 %collective-permute-start.1 = (bf16[128,1024]{1,0:T(8,128)(2,1)S(1)}, bf16[128,1024]{1,0:T(8,128)(2,1)S(1)}, u32[]{:S(2)}, u32[]{:S(2)}) collective-permute-start(bf16[128,1024]{1,0:T(8,128)(2,1)S(1)} %get-tuple-element.11), channel_id=1, source_target_pairs={{0,1},{1,0},{2,3},{3,2},{4,5},{5,4},{6,7},{7,6},{8,9},{9,8},{10,11... | collective-permute-start | bytes 786440 | tf_op jit(solution)/shard_map/ppermute | solution.py:158
  26.8 9.4 %collective-permute-done.1.after_ref = bf16[128,1024]{1,0:T(8,128)(2,1)S(1)} collective-permute-done((bf16[128,1024]{1,0:T(8,128)(2,1)S(1)}, bf16[128,1024]{1,0:T(8,128)(2,1)S(1)}, u32[]{:S(2)}, u32[]{:S(2)}) %collective-permute-start.1) | collective-permute-done | bytes 262176 | tf_op jit(solution)/shard_map/ppermute | solution.py:158
  37.5 1.8 %copies.1 = bf16[8,4,32,384]{3,2,1,0:T(8,128)(2,1)} custom-call(bf16[4,32,384]{2,1,0:T(8,128)(2,1)} %copy-done.8, bf16[128,1024]{1,0:T(8,128)(2,1)} %copy-done.6), custom_call_target="tpu_custom_call" | custom-call | tf_op jit(solution)/shard_map/copies/pallas_call | solution.py:67
  39.3 10.1 %all-to-all-start.1 = ((bf16[8,4,32,384]{3,2,1,0:T(8,128)(2,1)}), bf16[8,4,32,384]{3,2,1,0:T(8,128)(2,1)S(1)}, u32[]{:S(2)}, u32[]{:S(2)}) async-start(bf16[8,4,32,384]{3,2,1,0:T(8,128)(2,1)} %copies.1), calls=%async_computation.1 | async-start | bytes 1572864 | tf_op jit(solution)/shard_map/all_to_all | solution.py:74
  49.4 1.9 %collective-permute-start = (bf16[256,4096]{1,0:T(8,128)(2,1)S(1)}, bf16[256,4096]{1,0:T(8,128)(2,1)}, u32[]{:S(2)}, u32[]{:S(2)}) collective-permute-start(bf16[256,4096]{1,0:T(8,128)(2,1)S(1)} %copy-done.3), channel_id=1, source_target_pairs={{0,8},{8,0},{1,9},{9,1},{2,10},{10,2},{3,11},{11,3},{4,12},{12,4},... | collective-permute-start | bytes 6291464 | tf_op jit(solution)/shard_map/ppermute | solution.py:139
  51.3 3.2 %collective-permute-start.2 = (bf16[128,1024]{1,0:T(8,128)(2,1)S(1)}, bf16[128,1024]{1,0:T(8,128)(2,1)}, u32[]{:S(2)}, u32[]{:S(2)}) collective-permute-start(bf16[128,1024]{1,0:T(8,128)(2,1)S(1)} %get-tuple-element.12), channel_id=1, source_target_pairs={{0,2},{1,3},{2,0},{3,1},{4,6},{5,7},{6,4},{7,5},{8,10},{9,11},{10,... | collective-permute-start | bytes 786440 | tf_op jit(solution)/shard_map/ppermute | solution.py:158
  54.6 14.0 %collective-permute-done.2.refs_1_ = bf16[128,1024]{1,0:T(8,128)(2,1)} collective-permute-done((bf16[128,1024]{1,0:T(8,128)(2,1)S(1)}, bf16[128,1024]{1,0:T(8,128)(2,1)}, u32[]{:S(2)}, u32[]{:S(2)}) %collective-permute-start.2) | collective-permute-done | bytes 262176 | tf_op jit(solution)/shard_map/ppermute | solution.py:158
  68.5 2.0 %all-to-all-done.1.refs_0_ = bf16[8,4,32,384]{3,2,1,0:T(8,128)(2,1)S(1)} async-done(((bf16[8,4,32,384]{3,2,1,0:T(8,128)(2,1)}), bf16[8,4,32,384]{3,2,1,0:T(8,128)(2,1)S(1)}, u32[]{:S(2)}, u32[]{:S(2)}) %all-to-all-start.1) | async-done | bytes 786464 | tf_op jit(solution)/shard_map/all_to_all | solution.py:74
  71.4 1.9 %collective-permute-start.3 = (bf16[2,4,2,64,384]{4,3,2,1,0:T(8,128)(2,1)}, bf16[2,4,2,64,384]{4,3,2,1,0:T(8,128)(2,1)S(1)}, u32[]{:S(2)}, u32[]{:S(2)}) collective-permute-start(bf16[2,4,2,64,384]{4,3,2,1,0:T(8,128)(2,1)} %bitcast.20), channel_id=1, source_target_pairs={{0,16},{8,120},{16,0},{24,40},{32,48},{40,24},{48,32},{56,72},{64,... | collective-permute-start | bytes 2359304 | tf_op jit(solution)/shard_map/ppermute | solution.py:162
  73.3 2.7 %collective-permute-start.4 = (bf16[2,4,2,64,384]{4,3,2,1,0:T(8,128)(2,1)}, bf16[2,4,2,64,384]{4,3,2,1,0:T(8,128)(2,1)}, u32[]{:S(2)}, u32[]{:S(2)}) collective-permute-start(bf16[2,4,2,64,384]{4,3,2,1,0:T(8,128)(2,1)} %bitcast.21), channel_id=1, source_target_pairs={{0,128},{8,392},{16,144},{24,408},{32,160},{40,424},{48,176},{56,4... | collective-permute-start | bytes 2359304 | tf_op jit(solution)/shard_map/ppermute | solution.py:162
  76.1 4.6 %collective-permute-start.5 = (bf16[2,4,2,64,384]{4,3,2,1,0:T(8,128)(2,1)}, bf16[2,4,2,64,384]{4,3,2,1,0:T(8,128)(2,1)}, u32[]{:S(2)}, u32[]{:S(2)}) collective-permute-start(bf16[2,4,2,64,384]{4,3,2,1,0:T(8,128)(2,1)} %bitcast.22), channel_id=1, source_target_pairs={{0,144},{8,504},{16,128},{24,424},{32,176},{40,408},{48,160},{56,4... | collective-permute-start | bytes 2359304 | tf_op jit(solution)/shard_map/ppermute | solution.py:162
  80.7 5.2 %collective-permute-start.6 = (bf16[128,1024]{1,0:T(8,128)(2,1)S(1)}, bf16[128,1024]{1,0:T(8,128)(2,1)S(1)}, u32[]{:S(2)}, u32[]{:S(2)}) collective-permute-start(bf16[128,1024]{1,0:T(8,128)(2,1)S(1)} %get-tuple-element.13), channel_id=1, source_target_pairs={{0,3},{1,2},{2,1},{3,0},{4,7},{5,6},{6,5},{7,4},{8,11},{9,10},{10,... | collective-permute-start | bytes 786440 | tf_op jit(solution)/shard_map/ppermute | solution.py:158
  85.8 7.2 %collective-permute-done.6.refs_4_ = bf16[128,1024]{1,0:T(8,128)(2,1)S(1)} collective-permute-done((bf16[128,1024]{1,0:T(8,128)(2,1)S(1)}, bf16[128,1024]{1,0:T(8,128)(2,1)S(1)}, u32[]{:S(2)}, u32[]{:S(2)}) %collective-permute-start.6) | collective-permute-done | bytes 262176 | tf_op jit(solution)/shard_map/ppermute | solution.py:158
  93.0 3.0 %collective-permute-done.4.refs_2_ = bf16[2,4,2,64,384]{4,3,2,1,0:T(8,128)(2,1)} collective-permute-done((bf16[2,4,2,64,384]{4,3,2,1,0:T(8,128)(2,1)}, bf16[2,4,2,64,384]{4,3,2,1,0:T(8,128)(2,1)}, u32[]{:S(2)}, u32[]{:S(2)}) %collective-permute-start.4) | collective-permute-done | bytes 786464 | tf_op jit(solution)/shard_map/ppermute | solution.py:162
  97.1 6.1 %attend.1 = bf16[2,256,128]{2,1,0:T(8,128)(2,1)S(1)} custom-call(s32[1]{0:T(128)} %bitcast.3.place_ref, bf16[256,4096]{1,0:T(8,128)(2,1)S(1)} %copy-done.3, bf16[256,4096]{1,0:T(8,128)(2,1)} %collective-permute-done.other_ref, bf16[2,4,2,64,384]{4,3,2,1,0:T(8,128)(2,1)S(1)} %bitcast.23, bf16[2,4,2,64,384]{4,3,2,1,0:T(8,128)(2,1)S(1)} %collective-permute-done.3.refs_1_, ...), custom_call_target="tpu_custom_call" | custom-call | flops 1610612736 | bytes 8388608 | tf_op jit(solution)/shard_map/attend/pallas_call | solution.py:165
  104.2 4.5 %all-to-all-start.2 = ((bf16[8,256,128]{2,1,0:T(8,128)(2,1)}), bf16[8,256,128]{2,1,0:T(8,128)(2,1)S(1)}, u32[]{:S(2)}, u32[]{:S(2)}) async-start(bf16[8,256,128]{2,1,0:T(8,128)(2,1)} %bitcast.7), calls=%async_computation.2 | async-start | bytes 1048576 | tf_op jit(solution)/shard_map/all_to_all | solution.py:178
  109.7 2.4 %collective-permute-start.7 = (bf16[3,128,1024]{2,1,0:T(8,128)(2,1)S(1)}, bf16[3,128,1024]{2,1,0:T(8,128)(2,1)S(1)}, u32[]{:S(2)}, u32[]{:S(2)}) collective-permute-start(bf16[3,128,1024]{2,1,0:T(8,128)(2,1)S(1)} %pad_maximum_fusion.held_ref), channel_id=1, source_target_pairs={{0,8},{8,0},{1,9},{9,1},{2,10},{10,2},{3,11},{11,3},{4,12},{12,4},... | collective-permute-start | bytes 2359304 | tf_op jit(solution)/shard_map/ppermute | solution.py:175
  112.2 1.8 %collective-permute-done.7.partner_ref = bf16[3,128,1024]{2,1,0:T(8,128)(2,1)S(1)} collective-permute-done((bf16[3,128,1024]{2,1,0:T(8,128)(2,1)S(1)}, bf16[3,128,1024]{2,1,0:T(8,128)(2,1)S(1)}, u32[]{:S(2)}, u32[]{:S(2)}) %collective-permute-start.7) | collective-permute-done | bytes 786464 | tf_op jit(solution)/shard_map/ppermute | solution.py:175
  114.0 9.5 %all-to-all-done.2 = bf16[8,256,128]{2,1,0:T(8,128)(2,1)S(1)} async-done(((bf16[8,256,128]{2,1,0:T(8,128)(2,1)}), bf16[8,256,128]{2,1,0:T(8,128)(2,1)S(1)}, u32[]{:S(2)}, u32[]{:S(2)}) %all-to-all-start.2) | async-done | bytes 524320 | tf_op jit(solution)/shard_map/all_to_all | solution.py:178
  124.9 6.3 %collective-permute-start.8 = (bf16[128,1024]{1,0:T(8,128)(2,1)S(1)}, bf16[128,1024]{1,0:T(8,128)(2,1)S(1)}, u32[]{:S(2)}, u32[]{:S(2)}) collective-permute-start(bf16[128,1024]{1,0:T(8,128)(2,1)S(1)} %get-tuple-element.16), channel_id=1, source_target_pairs={{0,4},{4,0},{1,5},{5,1},{2,6},{6,2},{3,7},{7,3},{8,12},{12,8},{9,1... | collective-permute-start | bytes 786440 | tf_op jit(solution)/shard_map/ppermute | solution.py:193
  131.3 23.0 %collective-permute-done.8 = bf16[128,1024]{1,0:T(8,128)(2,1)S(1)} collective-permute-done((bf16[128,1024]{1,0:T(8,128)(2,1)S(1)}, bf16[128,1024]{1,0:T(8,128)(2,1)S(1)}, u32[]{:S(2)}, u32[]{:S(2)}) %collective-permute-start.8) | collective-permute-done | bytes 262176 | tf_op jit(solution)/shard_map/ppermute | solution.py:193
  154.3 11.8 %all_to_all.20 = bf16[4,32,1024]{2,1,0:T(8,128)(2,1)S(1)} all-to-all(bf16[4,32,1024]{2,1,0:T(8,128)(2,1)S(1)} %bitcast.27), channel_id=1, replica_groups=mesh['zh'=2,'x'=4,'y'=8,'c'=2,'rg'=2,'cb'=4] {'cb'}, dimensions={0} | all-to-all | bytes 524288 | tf_op jit(solution)/shard_map/all_to_all | solution.py:196
  (35 shorter events, 10.6 us)
Async XLA Ops:
  1.6 34.6 %all-to-all-start = ((bf16[4,32,384]{2,1,0:T(8,128)(2,1)}), bf16[4,32,384]{2,1,0:T(8,128)(2,1)S(1)}, u32[]{:S(2)}, u32[]{:S(2)}) async-start(bf16[4,32,384]{2,1,0:T(8,128)(2,1)} %bitcast.5), calls=%async_computation | async-start | bytes 196608 | tf_op jit(solution)/shard_map/all_to_all | solution.py:143
  20.4 1.6 copy-start.2
  22.0 27.4 %copy-start.3 = (bf16[256,4096]{1,0:T(8,128)(2,1)S(1)}, bf16[256,4096]{1,0:T(8,128)(2,1)}, u32[]{:S(2)}) copy-start(bf16[256,4096]{1,0:T(8,128)(2,1)} %own_ref.1) | copy-start | bytes 6291460
  22.6 0.8 copy-start.4
  23.4 12.8 %collective-permute-start.1 = (bf16[128,1024]{1,0:T(8,128)(2,1)S(1)}, bf16[128,1024]{1,0:T(8,128)(2,1)S(1)}, u32[]{:S(2)}, u32[]{:S(2)}) collective-permute-start(bf16[128,1024]{1,0:T(8,128)(2,1)S(1)} %get-tuple-element.11), channel_id=1, source_target_pairs={{0,1},{1,0},{2,3},{3,2},{4,5},{5,4},{6,7},{7,6},{8,9},{9,8},{10,11... | collective-permute-start | bytes 786440 | tf_op jit(solution)/shard_map/ppermute | solution.py:158
  36.1 0.7 copy-start.6
  36.8 0.6 copy-start.8
  39.3 31.2 %all-to-all-start.1 = ((bf16[8,4,32,384]{3,2,1,0:T(8,128)(2,1)}), bf16[8,4,32,384]{3,2,1,0:T(8,128)(2,1)S(1)}, u32[]{:S(2)}, u32[]{:S(2)}) async-start(bf16[8,4,32,384]{3,2,1,0:T(8,128)(2,1)} %copies.1), calls=%async_computation.1 | async-start | bytes 1572864 | tf_op jit(solution)/shard_map/all_to_all | solution.py:74
  49.4 43.6 %collective-permute-start = (bf16[256,4096]{1,0:T(8,128)(2,1)S(1)}, bf16[256,4096]{1,0:T(8,128)(2,1)}, u32[]{:S(2)}, u32[]{:S(2)}) collective-permute-start(bf16[256,4096]{1,0:T(8,128)(2,1)S(1)} %copy-done.3), channel_id=1, source_target_pairs={{0,8},{8,0},{1,9},{9,1},{2,10},{10,2},{3,11},{11,3},{4,12},{12,4},... | collective-permute-start | bytes 6291464 | tf_op jit(solution)/shard_map/ppermute | solution.py:139
  51.3 17.2 %collective-permute-start.2 = (bf16[128,1024]{1,0:T(8,128)(2,1)S(1)}, bf16[128,1024]{1,0:T(8,128)(2,1)}, u32[]{:S(2)}, u32[]{:S(2)}) collective-permute-start(bf16[128,1024]{1,0:T(8,128)(2,1)S(1)} %get-tuple-element.12), channel_id=1, source_target_pairs={{0,2},{1,3},{2,0},{3,1},{4,6},{5,7},{6,4},{7,5},{8,10},{9,11},{10,... | collective-permute-start | bytes 786440 | tf_op jit(solution)/shard_map/ppermute | solution.py:158
  70.5 0.9 copy-start
  71.4 21.6 %collective-permute-start.3 = (bf16[2,4,2,64,384]{4,3,2,1,0:T(8,128)(2,1)}, bf16[2,4,2,64,384]{4,3,2,1,0:T(8,128)(2,1)S(1)}, u32[]{:S(2)}, u32[]{:S(2)}) collective-permute-start(bf16[2,4,2,64,384]{4,3,2,1,0:T(8,128)(2,1)} %bitcast.20), channel_id=1, source_target_pairs={{0,16},{8,120},{16,0},{24,40},{32,48},{40,24},{48,32},{56,72},{64,... | collective-permute-start | bytes 2359304 | tf_op jit(solution)/shard_map/ppermute | solution.py:162
  73.3 22.6 %collective-permute-start.4 = (bf16[2,4,2,64,384]{4,3,2,1,0:T(8,128)(2,1)}, bf16[2,4,2,64,384]{4,3,2,1,0:T(8,128)(2,1)}, u32[]{:S(2)}, u32[]{:S(2)}) collective-permute-start(bf16[2,4,2,64,384]{4,3,2,1,0:T(8,128)(2,1)} %bitcast.21), channel_id=1, source_target_pairs={{0,128},{8,392},{16,144},{24,408},{32,160},{40,424},{48,176},{56,4... | collective-permute-start | bytes 2359304 | tf_op jit(solution)/shard_map/ppermute | solution.py:162
  76.1 19.9 %collective-permute-start.5 = (bf16[2,4,2,64,384]{4,3,2,1,0:T(8,128)(2,1)}, bf16[2,4,2,64,384]{4,3,2,1,0:T(8,128)(2,1)}, u32[]{:S(2)}, u32[]{:S(2)}) collective-permute-start(bf16[2,4,2,64,384]{4,3,2,1,0:T(8,128)(2,1)} %bitcast.22), channel_id=1, source_target_pairs={{0,144},{8,504},{16,128},{24,424},{32,176},{40,408},{48,160},{56,4... | collective-permute-start | bytes 2359304 | tf_op jit(solution)/shard_map/ppermute | solution.py:162
  80.7 12.4 %collective-permute-start.6 = (bf16[128,1024]{1,0:T(8,128)(2,1)S(1)}, bf16[128,1024]{1,0:T(8,128)(2,1)S(1)}, u32[]{:S(2)}, u32[]{:S(2)}) collective-permute-start(bf16[128,1024]{1,0:T(8,128)(2,1)S(1)} %get-tuple-element.13), channel_id=1, source_target_pairs={{0,3},{1,2},{2,1},{3,0},{4,7},{5,6},{6,5},{7,4},{8,11},{9,10},{10,... | collective-permute-start | bytes 786440 | tf_op jit(solution)/shard_map/ppermute | solution.py:158
  96.0 1.1 copy-start.1
  103.2 5.5 %copy-start.7 = (bf16[128,1024]{1,0:T(8,128)(2,1)S(1)}, bf16[128,1024]{1,0:T(8,128)(2,1)}, u32[]{:S(2)}) copy-start(bf16[128,1024]{1,0:T(8,128)(2,1)} %copy-done.6) | copy-start | bytes 786436
  103.2 20.3 %copy-start.5 = (bf16[256,1024]{1,0:T(8,128)(2,1)S(1)}, bf16[256,1024]{1,0:T(8,128)(2,1)}, u32[]{:S(2)}) copy-start(bf16[256,1024]{1,0:T(8,128)(2,1)} %copy-done.4) | copy-start | bytes 1572868
  104.2 19.4 %all-to-all-start.2 = ((bf16[8,256,128]{2,1,0:T(8,128)(2,1)}), bf16[8,256,128]{2,1,0:T(8,128)(2,1)S(1)}, u32[]{:S(2)}, u32[]{:S(2)}) async-start(bf16[8,256,128]{2,1,0:T(8,128)(2,1)} %bitcast.7), calls=%async_computation.2 | async-start | bytes 1048576 | tf_op jit(solution)/shard_map/all_to_all | solution.py:178
  109.7 4.3 %collective-permute-start.7 = (bf16[3,128,1024]{2,1,0:T(8,128)(2,1)S(1)}, bf16[3,128,1024]{2,1,0:T(8,128)(2,1)S(1)}, u32[]{:S(2)}, u32[]{:S(2)}) collective-permute-start(bf16[3,128,1024]{2,1,0:T(8,128)(2,1)S(1)} %pad_maximum_fusion.held_ref), channel_id=1, source_target_pairs={{0,8},{8,0},{1,9},{9,1},{2,10},{10,2},{3,11},{11,3},{4,12},{12,4},... | collective-permute-start | bytes 2359304 | tf_op jit(solution)/shard_map/ppermute | solution.py:175
  124.9 29.3 %collective-permute-start.8 = (bf16[128,1024]{1,0:T(8,128)(2,1)S(1)}, bf16[128,1024]{1,0:T(8,128)(2,1)S(1)}, u32[]{:S(2)}, u32[]{:S(2)}) collective-permute-start(bf16[128,1024]{1,0:T(8,128)(2,1)S(1)} %get-tuple-element.16), channel_id=1, source_target_pairs={{0,4},{4,0},{1,5},{5,1},{2,6},{6,2},{3,7},{7,3},{8,12},{12,8},{9,1... | collective-permute-start | bytes 786440 | tf_op jit(solution)/shard_map/ppermute | solution.py:193

commit v7 on v5

--- a/solution.py
+++ b/solution.py
@@ -39,7 +39,7 @@
     ]
     for dx, dy in ((0, 1), (1, 0), (1, 1))
 ]
-ANYWHERE = pl.BlockSpec(memory_space=pl.ANY)
+ANYWHERE = pl.BlockSpec(memory_space=pltpu.HBM)
 
 
 def behind_kernel(*refs):
@@ -65,7 +65,7 @@
 
 def attend_kernel(place_ref, own_ref, other_ref, *refs):
     w_refs, (out_ref, held_ref, sems) = refs[:4], refs[5:]
-    me = place_ref[0]
+    me, core = place_ref[0], place_ref[1]
     for i, w_ref in enumerate(w_refs):
         pltpu.make_async_copy(w_ref, held_ref.at[me ^ i], sems.at[i]).start()
     span = Y * held_ref.shape[4]
@@ -92,7 +92,9 @@
         ) * (1.0 / math.sqrt(HD))
         raised = jnp.exp(scores - jnp.max(scores, axis=-1, keepdims=True))
         attn = (raised / jnp.sum(raised, axis=-1, keepdims=True)).astype(jnp.bfloat16)
-        out_ref[g] = jnp.dot(attn, values, preferred_element_type=jnp.float32).astype(jnp.bfloat16)
+        mixed = jnp.dot(attn, values, preferred_element_type=jnp.float32).astype(jnp.bfloat16)
+        for cb in range(CB):
+            out_ref[(core ^ g) * CB + cb] = mixed
 
 
 def split_kernel(place_ref, w_ref, after_ref, own_ref, *out_refs):
@@ -105,21 +107,18 @@
         out_ref[...] = w_ref[rows, pl.ds(start, width)]
 
 
-def project_kernel(place_ref, mixed_ref, own_ref, held_ref, partner_ref, far_ref, near_ref):
-    column, half, core = place_ref[0], place_ref[1], place_ref[2]
-    rows = far_ref.shape[0]
-    for out_ref, start in ((far_ref, (1 - half) * rows), (near_ref, half * rows)):
-        span = pl.ds(pl.multiple_of(start, rows), rows)
-        mixed = jnp.concatenate([mixed_ref[c, column, span] for c in range(C)], axis=1)
-        term = jnp.dot(mixed, own_ref[...], preferred_element_type=jnp.float32).astype(jnp.bfloat16)
-        total = term.astype(jnp.float32)
-        for i in range(CB - 1):
-            block = column ^ (i + 1)
-            mixed = jnp.concatenate([mixed_ref[core, block, span], mixed_ref[1 - core, block, span]], axis=1)
-            weight = jnp.concatenate([held_ref[i], partner_ref[i]], axis=0)
-            term = jnp.dot(mixed, weight, preferred_element_type=jnp.float32).astype(jnp.bfloat16)
-            total += term.astype(jnp.float32)
-        out_ref[...] = total.astype(out_ref.dtype)
+def project_kernel(place_ref, mixed_ref, own_ref, held_ref, partner_ref, out_ref):
+    column, core = place_ref[0], place_ref[1]
+    mixed = jnp.concatenate([mixed_ref[c, column] for c in range(C)], axis=1)
+    term = jnp.dot(mixed, own_ref[...], preferred_element_type=jnp.float32).astype(jnp.bfloat16)
+    total = term.astype(jnp.float32)
+    for i in range(CB - 1):
+        block = column ^ (i + 1)
+        mixed = jnp.concatenate([mixed_ref[core, block], mixed_ref[1 - core, block]], axis=1)
+        weight = jnp.concatenate([held_ref[i], partner_ref[i]], axis=0)
+        term = jnp.dot(mixed, weight, preferred_element_type=jnp.float32).astype(jnp.bfloat16)
+        total += term.astype(jnp.float32)
+    out_ref[...] = total.astype(out_ref.dtype)
 
 
 def body(tokens, qkv_weight, out_weight):
@@ -133,7 +132,7 @@
     first = heads
     heads = spread(heads, FAR)
 
-    column, half, core = lax.axis_index("cb"), lax.axis_index("rg"), lax.axis_index("c")
+    column, core = lax.axis_index("cb"), lax.axis_index("c")
     depth, columns = out_weight.shape[0], out_weight.shape[1] // CB
     smem, vmem = pl.BlockSpec(memory_space=pltpu.SMEM), pl.BlockSpec(memory_space=pltpu.VMEM)
     own_weight, *sent = pl.pallas_call(
@@ -154,37 +153,31 @@
 
     mixed = pl.pallas_call(
         attend_kernel,
-        out_shape=jax.ShapeDtypeStruct((2, rows, HD), jnp.bfloat16),
+        out_shape=jax.ShapeDtypeStruct((C * CB, rows, HD), jnp.bfloat16),
         in_specs=[smem] + [vmem] * 2 + [ANYWHERE] * 5,
         scratch_shapes=[pltpu.VMEM((4,) + heads.shape, jnp.bfloat16), pltpu.SemaphoreType.DMA((4,))],
         compiler_params=pltpu.CompilerParams(vmem_limit_bytes=48 << 20),
         cost_estimate=pl.CostEstimate(flops=2 * 2 * rows * width * 3 * HD, bytes_accessed=8 << 20, transcendentals=0),
         name="attend",
-    )(parity[None], tokens, other, *squares, held[2])
+    )(jnp.stack([parity, core]), tokens, other, *squares, held[2])
     held = jnp.stack(held)
     partner = lax.ppermute(held, "c", [(0, 1), (1, 0)])
-    mixed = jnp.where(core == 0, mixed, mixed[::-1])
-    mixed = jnp.broadcast_to(mixed[:, None], (C, CB, rows, HD)).reshape(C * CB, rows, HD)
     mixed = lax.all_to_all(mixed, ("c", "cb"), 0, 0, tiled=True).reshape(C, CB, rows, HD)
 
-    part = rows // RG
-    far, near = pl.pallas_call(
+    summed = pl.pallas_call(
         project_kernel,
-        out_shape=[
-            jax.ShapeDtypeStruct((part, columns), jnp.bfloat16),
-            jax.ShapeDtypeStruct((part, columns), jnp.float32),
-        ],
+        out_shape=jax.ShapeDtypeStruct((rows, columns), jnp.bfloat16),
         in_specs=[smem] + [vmem] * 4,
-        out_specs=[vmem] * 2,
+        out_specs=vmem,
         compiler_params=pltpu.CompilerParams(vmem_limit_bytes=24 << 20),
         cost_estimate=pl.CostEstimate(flops=2 * rows * CB * C * HD * columns, bytes_accessed=4 << 20, transcendentals=0),
         name="project",
-    )(jnp.stack([column, half, core]), mixed, own_weight, held, partner)
-    far = lax.ppermute(far, "rg", [(0, 1), (1, 0)])
-    summed = (near + far.astype(jnp.float32)).astype(jnp.bfloat16)
-    summed = summed.reshape(CB, part // CB, columns)
-    summed = lax.all_to_all(summed, "cb", 0, 0, tiled=True)
-    return summed.transpose(1, 0, 2).reshape(part // CB, CB * columns)
+    )(jnp.stack([column, core]), mixed, own_weight, held, partner)
+    part = rows // (RG * CB)
+    summed = lax.all_to_all(summed.reshape(RG * CB, part, columns), MP, 0, 0, tiled=True)
+    summed = summed.reshape(RG, CB, part, columns).astype(jnp.float32)
+    summed = (summed[0] + summed[1]).astype(jnp.bfloat16)
+    return summed.transpose(1, 0, 2).reshape(part, CB * columns)
 
 
 def solution(mesh):

time: 167 us -> 162 us (0.970)
  blocking collectives: 45.3 us -> 70.5 us
  waiting for transfers between devices: 58.1 us -> 36.4 us
  starting transfers between devices: 47.1 us -> 38.7 us
    all_to_all x1, blocking collectives: 11.8 us -> 37 us  [body(): lax.all_to_all(summed.reshape(RG * CB, part, columns), MP, 0, 0, tiled=True)]
    ppermute x1 -> x0, waiting for transfers between devices: 21.8 us -> none  [body(): far = lax.ppermute(far, 'rg', [(0, 1), (1, 0)])]
    ppermute x1 -> x0, starting transfers between devices: 8.54 us -> none  [body(): far = lax.ppermute(far, 'rg', [(0, 1), (1, 0)])]
  transfers between devices with their start and end apart: 11 -> 10, of which waited for: 7 -> 6; matrix products, arithmetic and copies ran while one was open for 1% -> 1% of each run, Pallas kernels for 0% -> 0%
where the time goes in v7:
time: 162 us
  blocking collectives  70.5 us (44%)
  starting transfers between devices  38.7 us (24%)
  waiting for transfers between devices  36.4 us (22%)
  Pallas kernels  8.92 us (6%)
  local copies, waits for them, and re-layouts  5.62 us (3%)
    all_to_all x1, blocking collectives, body(): lax.all_to_all(summed.reshape(RG * CB, part, columns), MP, 0, 0, tiled=True)  37 us
    all_to_all x1, blocking collectives, body(): heads = lax.all_to_all(heads, ('zh', 'c'), 0, 0, tiled=True)  33.5 us
    ppermute x3, waiting for transfers between devices, body(): lax.ppermute(block, 'cb', [(j, j ^ i + 1) for j in range(CB)])  21.6 us
    ppermute x3, starting transfers between devices, body(): lax.ppermute(block, 'cb', [(j, j ^ i + 1) for j in range(CB)])  10.2 us
    all_to_all x1, starting transfers between devices, spread(): lax.all_to_all(blocks, DP, 0, 0, axis_index_groups=groups, tiled=True)  10.1 us
    all_to_all x1, waiting for transfers between devices, body(): lax.all_to_all(mixed, ('c', 'cb'), 0, 0, tiled=True)  9.53 us
    ppermute x3, starting transfers between devices, body(): squares = [heads] + [lax.ppermute(heads, DP, pairs) for pairs in NEAR]  9.2 us
    pallas_call x1, Pallas kernels, body(): pl.pallas_call(attend_kernel, out_shape=jax.ShapeDtypeStruct((C * CB, row...  6.99 us
  transfers between devices with their start and end apart: 10, of which 6 were waited for; matrix products, arithmetic and copies ran while one was open for 1% of the time, Pallas kernels for 0%

profile of v7, /device:TPU:6, one launch (start us, length us, event | category | flops | bytes accessed | tf_op | source)
XLA Modules:
  0.0 161.6 jit_solution(14408959569960301155)
XLA Ops:
  0.0 1.0 reshape.29
  1.1 33.5 %all_to_all.20.after_ref = bf16[4,32,384]{2,1,0:T(8,128)(2,1)S(1)} all-to-all(bf16[4,32,384]{2,1,0:T(8,128)(2,1)S(1)} %bitcast.27), channel_id=1, replica_groups=mesh['zh'=2,'x'=4,'y'=8,'c'=2,'rg'=2,'cb'=4] {'zh','c'}, dimensions={0} | all-to-all | bytes 196608 | tf_op jit(solution)/shard_map/all_to_all | solution.py:131
  34.6 1.0 broadcast_in_dim.15
  35.6 10.1 %all-to-all-start.1 = ((bf16[8,4,32,384]{3,2,1,0:T(8,128)(2,1)}), bf16[8,4,32,384]{3,2,1,0:T(8,128)(2,1)S(1)}, u32[]{:S(2)}, u32[]{:S(2)}) async-start(bf16[8,4,32,384]{3,2,1,0:T(8,128)(2,1)} %broadcast_in_dim.15), calls=%async_computation.1 | async-start | bytes 1572864 | tf_op jit(solution)/shard_map/all_to_all | solution.py:63
  45.6 1.9 %collective-permute-start = (bf16[256,4096]{1,0:T(8,128)(2,1)}, bf16[256,4096]{1,0:T(8,128)(2,1)}, u32[]{:S(2)}, u32[]{:S(2)}) collective-permute-start(bf16[256,4096]{1,0:T(8,128)(2,1)} %own_ref.1), channel_id=1, source_target_pairs={{0,8},{8,0},{1,9},{9,1},{2,10},{10,2},{3,11},{11,3},{4,12},{12,4},... | collective-permute-start | bytes 6291464 | tf_op jit(solution)/shard_map/ppermute | solution.py:127
  49.1 2.0 %collective-permute-start.1 = (bf16[128,1024]{1,0:T(8,128)(2,1)S(1)}, bf16[128,1024]{1,0:T(8,128)(2,1)S(1)}, u32[]{:S(2)}, u32[]{:S(2)}) collective-permute-start(bf16[128,1024]{1,0:T(8,128)(2,1)S(1)} %get-tuple-element.9), channel_id=1, source_target_pairs={{0,1},{1,0},{2,3},{3,2},{4,5},{5,4},{6,7},{7,6},{8,9},{9,8},{10,11... | collective-permute-start | bytes 786440 | tf_op jit(solution)/shard_map/ppermute | solution.py:148
  51.1 3.8 %collective-permute-start.2 = (bf16[128,1024]{1,0:T(8,128)(2,1)S(1)}, bf16[128,1024]{1,0:T(8,128)(2,1)}, u32[]{:S(2)}, u32[]{:S(2)}) collective-permute-start(bf16[128,1024]{1,0:T(8,128)(2,1)S(1)} %get-tuple-element.10), channel_id=1, source_target_pairs={{0,2},{1,3},{2,0},{3,1},{4,6},{5,7},{6,4},{7,5},{8,10},{9,11},{10,... | collective-permute-start | bytes 786440 | tf_op jit(solution)/shard_map/ppermute | solution.py:148
  54.9 8.5 %collective-permute-done.1.refs_1_ = bf16[128,1024]{1,0:T(8,128)(2,1)S(1)} collective-permute-done((bf16[128,1024]{1,0:T(8,128)(2,1)S(1)}, bf16[128,1024]{1,0:T(8,128)(2,1)S(1)}, u32[]{:S(2)}, u32[]{:S(2)}) %collective-permute-start.1) | collective-permute-done | bytes 262176 | tf_op jit(solution)/shard_map/ppermute | solution.py:148
  63.5 5.0 %collective-permute-done.2.refs_2_ = bf16[128,1024]{1,0:T(8,128)(2,1)} collective-permute-done((bf16[128,1024]{1,0:T(8,128)(2,1)S(1)}, bf16[128,1024]{1,0:T(8,128)(2,1)}, u32[]{:S(2)}, u32[]{:S(2)}) %collective-permute-start.2) | collective-permute-done | bytes 262176 | tf_op jit(solution)/shard_map/ppermute | solution.py:148
  69.3 2.6 %collective-permute-start.3 = (bf16[2,4,2,64,384]{4,3,2,1,0:T(8,128)(2,1)}, bf16[2,4,2,64,384]{4,3,2,1,0:T(8,128)(2,1)S(1)}, u32[]{:S(2)}, u32[]{:S(2)}) collective-permute-start(bf16[2,4,2,64,384]{4,3,2,1,0:T(8,128)(2,1)} %bitcast.19), channel_id=1, source_target_pairs={{0,16},{8,120},{16,0},{24,40},{32,48},{40,24},{48,32},{56,72},{64,... | collective-permute-start | bytes 2359304 | tf_op jit(solution)/shard_map/ppermute | solution.py:151
  71.9 2.7 %collective-permute-start.4 = (bf16[2,4,2,64,384]{4,3,2,1,0:T(8,128)(2,1)}, bf16[2,4,2,64,384]{4,3,2,1,0:T(8,128)(2,1)}, u32[]{:S(2)}, u32[]{:S(2)}) collective-permute-start(bf16[2,4,2,64,384]{4,3,2,1,0:T(8,128)(2,1)} %bitcast.20), channel_id=1, source_target_pairs={{0,128},{8,392},{16,144},{24,408},{32,160},{40,424},{48,176},{56,4... | collective-permute-start | bytes 2359304 | tf_op jit(solution)/shard_map/ppermute | solution.py:151
  74.7 3.9 %collective-permute-start.5 = (bf16[2,4,2,64,384]{4,3,2,1,0:T(8,128)(2,1)}, bf16[2,4,2,64,384]{4,3,2,1,0:T(8,128)(2,1)}, u32[]{:S(2)}, u32[]{:S(2)}) collective-permute-start(bf16[2,4,2,64,384]{4,3,2,1,0:T(8,128)(2,1)} %bitcast.21), channel_id=1, source_target_pairs={{0,144},{8,504},{16,128},{24,424},{32,176},{40,408},{48,160},{56,4... | collective-permute-start | bytes 2359304 | tf_op jit(solution)/shard_map/ppermute | solution.py:151
  78.5 4.4 %collective-permute-start.6 = (bf16[128,1024]{1,0:T(8,128)(2,1)S(1)}, bf16[128,1024]{1,0:T(8,128)(2,1)S(1)}, u32[]{:S(2)}, u32[]{:S(2)}) collective-permute-start(bf16[128,1024]{1,0:T(8,128)(2,1)S(1)} %get-tuple-element.11), channel_id=1, source_target_pairs={{0,3},{1,2},{2,1},{3,0},{4,7},{5,6},{6,5},{7,4},{8,11},{9,10},{10,... | collective-permute-start | bytes 786440 | tf_op jit(solution)/shard_map/ppermute | solution.py:148
  83.1 8.1 %collective-permute-done.6.refs_4_ = bf16[128,1024]{1,0:T(8,128)(2,1)S(1)} collective-permute-done((bf16[128,1024]{1,0:T(8,128)(2,1)S(1)}, bf16[128,1024]{1,0:T(8,128)(2,1)S(1)}, u32[]{:S(2)}, u32[]{:S(2)}) %collective-permute-start.6) | collective-permute-done | bytes 262176 | tf_op jit(solution)/shard_map/ppermute | solution.py:148
  91.2 3.3 %collective-permute-done.4.refs_2_ = bf16[2,4,2,64,384]{4,3,2,1,0:T(8,128)(2,1)} collective-permute-done((bf16[2,4,2,64,384]{4,3,2,1,0:T(8,128)(2,1)}, bf16[2,4,2,64,384]{4,3,2,1,0:T(8,128)(2,1)}, u32[]{:S(2)}, u32[]{:S(2)}) %collective-permute-start.4) | collective-permute-done | bytes 786464 | tf_op jit(solution)/shard_map/ppermute | solution.py:151
  94.5 1.1 copy-done.1
  95.7 7.0 %attend.1 = bf16[8,256,128]{2,1,0:T(8,128)(2,1)} custom-call(s32[2]{0:T(128)S(1)} %pad_add_fusion.1.place_ref, bf16[256,4096]{1,0:T(8,128)(2,1)S(1)} %copy-done.3, bf16[256,4096]{1,0:T(8,128)(2,1)} %collective-permute-done.other_ref, bf16[2,4,2,64,384]{4,3,2,1,0:T(8,128)(2,1)S(1)} %bitcast.22, ...), custom_call_target="tpu_custom_call" | custom-call | flops 1610612736 | bytes 8388608 | tf_op jit(solution)/shard_map/attend/pallas_call | solution.py:154
  102.7 4.8 %all-to-all-start.2 = ((bf16[8,256,128]{2,1,0:T(8,128)(2,1)}), bf16[8,256,128]{2,1,0:T(8,128)(2,1)S(1)}, u32[]{:S(2)}, u32[]{:S(2)}) async-start(bf16[8,256,128]{2,1,0:T(8,128)(2,1)} %attend.1), calls=%async_computation.2 | async-start | bytes 1048576 | tf_op jit(solution)/shard_map/all_to_all | solution.py:165
  107.5 1.0 pad_maximum_fusion.held_ref
  108.6 2.4 %collective-permute-start.7 = (bf16[3,128,1024]{2,1,0:T(8,128)(2,1)S(1)}, bf16[3,128,1024]{2,1,0:T(8,128)(2,1)S(1)}, u32[]{:S(2)}, u32[]{:S(2)}) collective-permute-start(bf16[3,128,1024]{2,1,0:T(8,128)(2,1)S(1)} %pad_maximum_fusion.held_ref), channel_id=1, source_target_pairs={{0,8},{8,0},{1,9},{9,1},{2,10},{10,2},{3,11},{11,3},{4,12},{12,4},... | collective-permute-start | bytes 2359304 | tf_op jit(solution)/shard_map/ppermute | solution.py:164
  111.0 1.9 %collective-permute-done.7.partner_ref = bf16[3,128,1024]{2,1,0:T(8,128)(2,1)S(1)} collective-permute-done((bf16[3,128,1024]{2,1,0:T(8,128)(2,1)S(1)}, bf16[3,128,1024]{2,1,0:T(8,128)(2,1)S(1)}, u32[]{:S(2)}, u32[]{:S(2)}) %collective-permute-start.7) | collective-permute-done | bytes 786464 | tf_op jit(solution)/shard_map/ppermute | solution.py:164
  112.9 9.5 %all-to-all-done.2 = bf16[8,256,128]{2,1,0:T(8,128)(2,1)S(1)} async-done(((bf16[8,256,128]{2,1,0:T(8,128)(2,1)}), bf16[8,256,128]{2,1,0:T(8,128)(2,1)S(1)}, u32[]{:S(2)}, u32[]{:S(2)}) %all-to-all-start.2) | async-done | bytes 524320 | tf_op jit(solution)/shard_map/all_to_all | solution.py:165
  122.4 1.3 project.1
  123.7 37.0 %all_to_all.21 = bf16[8,32,1024]{2,1,0:T(8,128)(2,1)S(1)} all-to-all(bf16[8,32,1024]{2,1,0:T(8,128)(2,1)S(1)} %bitcast.24), channel_id=1, replica_groups=mesh['zh'=2,'x'=4,'y'=8,'c'=2,'rg'=2,'cb'=4] {'rg','cb'}, dimensions={0} | all-to-all | bytes 1048576 | tf_op jit(solution)/shard_map/all_to_all | solution.py:177
  (29 shorter events, 3.5 us)
Async XLA Ops:
  0.0 47.6 %copy-start.2 = (bf16[256,4096]{1,0:T(8,128)(2,1)S(1)}, bf16[256,4096]{1,0:T(8,128)(2,1)}, u32[]{:S(2)}) copy-start(bf16[256,4096]{1,0:T(8,128)(2,1)} %w_ref.1) | copy-start | bytes 6291460
  35.6 32.8 %all-to-all-start.1 = ((bf16[8,4,32,384]{3,2,1,0:T(8,128)(2,1)}), bf16[8,4,32,384]{3,2,1,0:T(8,128)(2,1)S(1)}, u32[]{:S(2)}, u32[]{:S(2)}) async-start(bf16[8,4,32,384]{3,2,1,0:T(8,128)(2,1)} %broadcast_in_dim.15), calls=%async_computation.1 | async-start | bytes 1572864 | tf_op jit(solution)/shard_map/all_to_all | solution.py:63
  45.6 45.6 %collective-permute-start = (bf16[256,4096]{1,0:T(8,128)(2,1)}, bf16[256,4096]{1,0:T(8,128)(2,1)}, u32[]{:S(2)}, u32[]{:S(2)}) collective-permute-start(bf16[256,4096]{1,0:T(8,128)(2,1)} %own_ref.1), channel_id=1, source_target_pairs={{0,8},{8,0},{1,9},{9,1},{2,10},{10,2},{3,11},{11,3},{4,12},{12,4},... | collective-permute-start | bytes 6291464 | tf_op jit(solution)/shard_map/ppermute | solution.py:127
  48.3 0.8 copy-start.4
  49.1 45.4 %copy-start.3 = (bf16[256,4096]{1,0:T(8,128)(2,1)S(1)}, bf16[256,4096]{1,0:T(8,128)(2,1)}, u32[]{:S(2)}) copy-start(bf16[256,4096]{1,0:T(8,128)(2,1)} %own_ref.1) | copy-start | bytes 6291460
  49.1 14.4 %collective-permute-start.1 = (bf16[128,1024]{1,0:T(8,128)(2,1)S(1)}, bf16[128,1024]{1,0:T(8,128)(2,1)S(1)}, u32[]{:S(2)}, u32[]{:S(2)}) collective-permute-start(bf16[128,1024]{1,0:T(8,128)(2,1)S(1)} %get-tuple-element.9), channel_id=1, source_target_pairs={{0,1},{1,0},{2,3},{3,2},{4,5},{5,4},{6,7},{7,6},{8,9},{9,8},{10,11... | collective-permute-start | bytes 786440 | tf_op jit(solution)/shard_map/ppermute | solution.py:148
  51.1 17.3 %collective-permute-start.2 = (bf16[128,1024]{1,0:T(8,128)(2,1)S(1)}, bf16[128,1024]{1,0:T(8,128)(2,1)}, u32[]{:S(2)}, u32[]{:S(2)}) collective-permute-start(bf16[128,1024]{1,0:T(8,128)(2,1)S(1)} %get-tuple-element.10), channel_id=1, source_target_pairs={{0,2},{1,3},{2,0},{3,1},{4,6},{5,7},{6,4},{7,5},{8,10},{9,11},{10,... | collective-permute-start | bytes 786440 | tf_op jit(solution)/shard_map/ppermute | solution.py:148
  63.5 5.0 %copy-start.6 = (bf16[128,1024]{1,0:T(8,128)(2,1)}, bf16[128,1024]{1,0:T(8,128)(2,1)S(1)}, u32[]{:S(2)}) copy-start(bf16[128,1024]{1,0:T(8,128)(2,1)S(1)} %collective-permute-done.1.refs_1_) | copy-start | bytes 786436
  68.4 0.9 copy-start
  69.3 21.9 %collective-permute-start.3 = (bf16[2,4,2,64,384]{4,3,2,1,0:T(8,128)(2,1)}, bf16[2,4,2,64,384]{4,3,2,1,0:T(8,128)(2,1)S(1)}, u32[]{:S(2)}, u32[]{:S(2)}) collective-permute-start(bf16[2,4,2,64,384]{4,3,2,1,0:T(8,128)(2,1)} %bitcast.19), channel_id=1, source_target_pairs={{0,16},{8,120},{16,0},{24,40},{32,48},{40,24},{48,32},{56,72},{64,... | collective-permute-start | bytes 2359304 | tf_op jit(solution)/shard_map/ppermute | solution.py:151
  71.9 22.6 %collective-permute-start.4 = (bf16[2,4,2,64,384]{4,3,2,1,0:T(8,128)(2,1)}, bf16[2,4,2,64,384]{4,3,2,1,0:T(8,128)(2,1)}, u32[]{:S(2)}, u32[]{:S(2)}) collective-permute-start(bf16[2,4,2,64,384]{4,3,2,1,0:T(8,128)(2,1)} %bitcast.20), channel_id=1, source_target_pairs={{0,128},{8,392},{16,144},{24,408},{32,160},{40,424},{48,176},{56,4... | collective-permute-start | bytes 2359304 | tf_op jit(solution)/shard_map/ppermute | solution.py:151
  74.7 19.9 %collective-permute-start.5 = (bf16[2,4,2,64,384]{4,3,2,1,0:T(8,128)(2,1)}, bf16[2,4,2,64,384]{4,3,2,1,0:T(8,128)(2,1)}, u32[]{:S(2)}, u32[]{:S(2)}) collective-permute-start(bf16[2,4,2,64,384]{4,3,2,1,0:T(8,128)(2,1)} %bitcast.21), channel_id=1, source_target_pairs={{0,144},{8,504},{16,128},{24,424},{32,176},{40,408},{48,160},{56,4... | collective-permute-start | bytes 2359304 | tf_op jit(solution)/shard_map/ppermute | solution.py:151
  78.5 12.6 %collective-permute-start.6 = (bf16[128,1024]{1,0:T(8,128)(2,1)S(1)}, bf16[128,1024]{1,0:T(8,128)(2,1)S(1)}, u32[]{:S(2)}, u32[]{:S(2)}) collective-permute-start(bf16[128,1024]{1,0:T(8,128)(2,1)S(1)} %get-tuple-element.11), channel_id=1, source_target_pairs={{0,3},{1,2},{2,1},{3,0},{4,7},{5,6},{6,5},{7,4},{8,11},{9,10},{10,... | collective-permute-start | bytes 786440 | tf_op jit(solution)/shard_map/ppermute | solution.py:148
  94.5 1.1 copy-start.1
  95.7 11.8 %copy-start.7 = (bf16[128,1024]{1,0:T(8,128)(2,1)S(1)}, bf16[128,1024]{1,0:T(8,128)(2,1)}, u32[]{:S(2)}) copy-start(bf16[128,1024]{1,0:T(8,128)(2,1)} %copy-done.6) | copy-start | bytes 786436
  102.7 19.7 %copy-start.5 = (bf16[256,1024]{1,0:T(8,128)(2,1)S(1)}, bf16[256,1024]{1,0:T(8,128)(2,1)}, u32[]{:S(2)}) copy-start(bf16[256,1024]{1,0:T(8,128)(2,1)} %copy-done.4) | copy-start | bytes 1572868
  102.7 19.7 %all-to-all-start.2 = ((bf16[8,256,128]{2,1,0:T(8,128)(2,1)}), bf16[8,256,128]{2,1,0:T(8,128)(2,1)S(1)}, u32[]{:S(2)}, u32[]{:S(2)}) async-start(bf16[8,256,128]{2,1,0:T(8,128)(2,1)} %attend.1), calls=%async_computation.2 | async-start | bytes 1048576 | tf_op jit(solution)/shard_map/all_to_all | solution.py:165
  108.6 4.3 %collective-permute-start.7 = (bf16[3,128,1024]{2,1,0:T(8,128)(2,1)S(1)}, bf16[3,128,1024]{2,1,0:T(8,128)(2,1)S(1)}, u32[]{:S(2)}, u32[]{:S(2)}) collective-permute-start(bf16[3,128,1024]{2,1,0:T(8,128)(2,1)S(1)} %pad_maximum_fusion.held_ref), channel_id=1, source_target_pairs={{0,8},{8,0},{1,9},{9,1},{2,10},{10,2},{3,11},{11,3},{4,12},{12,4},... | collective-permute-start | bytes 2359304 | tf_op jit(solution)/shard_map/ppermute | solution.py:164

commit v8 on v7

--- a/solution.py
+++ b/solution.py
@@ -107,8 +107,9 @@
         out_ref[...] = w_ref[rows, pl.ds(start, width)]
 
 
-def project_kernel(place_ref, mixed_ref, own_ref, held_ref, partner_ref, out_ref):
-    column, core = place_ref[0], place_ref[1]
+def project_kernel(place_ref, mixed_ref, own_ref, held_ref, partner_ref, *refs):
+    out_refs, sum_ref = refs[:-1], refs[-1]
+    column, core, spot = place_ref[0], place_ref[1], place_ref[2]
     mixed = jnp.concatenate([mixed_ref[c, column] for c in range(C)], axis=1)
     term = jnp.dot(mixed, own_ref[...], preferred_element_type=jnp.float32).astype(jnp.bfloat16)
     total = term.astype(jnp.float32)
@@ -118,7 +119,18 @@
         weight = jnp.concatenate([held_ref[i], partner_ref[i]], axis=0)
         term = jnp.dot(mixed, weight, preferred_element_type=jnp.float32).astype(jnp.bfloat16)
         total += term.astype(jnp.float32)
-    out_ref[...] = total.astype(out_ref.dtype)
+    sum_ref[...] = total.astype(sum_ref.dtype)
+    part = out_refs[0].shape[0]
+    for i, out_ref in enumerate(out_refs):
+        out_ref[...] = sum_ref[pl.ds(pl.multiple_of((spot ^ i) * part, part), part)]
+
+
+def add_kernel(place_ref, *refs):
+    in_refs, out_ref = refs[:-1], refs[-1]
+    width = in_refs[0].shape[1]
+    for i in range(CB):
+        total = in_refs[i][...].astype(jnp.float32) + in_refs[CB + i][...].astype(jnp.float32)
+        out_ref[:, pl.ds(pl.multiple_of((place_ref[0] ^ i) * width, width), width)] = total.astype(out_ref.dtype)
 
 
 def body(tokens, qkv_weight, out_weight):
@@ -164,20 +176,27 @@
     partner = lax.ppermute(held, "c", [(0, 1), (1, 0)])
     mixed = lax.all_to_all(mixed, ("c", "cb"), 0, 0, tiled=True).reshape(C, CB, rows, HD)
 
-    summed = pl.pallas_call(
+    n_mp = RG * CB
+    part = rows // n_mp
+    spot = jnp.stack([column, core, lax.axis_index("rg") * CB + column])
+    sums = pl.pallas_call(
         project_kernel,
-        out_shape=jax.ShapeDtypeStruct((rows, columns), jnp.bfloat16),
+        out_shape=[jax.ShapeDtypeStruct((part, columns), jnp.bfloat16)] * n_mp,
         in_specs=[smem] + [vmem] * 4,
-        out_specs=vmem,
+        out_specs=[vmem] * n_mp,
+        scratch_shapes=[pltpu.VMEM((rows, columns), jnp.bfloat16)],
         compiler_params=pltpu.CompilerParams(vmem_limit_bytes=24 << 20),
         cost_estimate=pl.CostEstimate(flops=2 * rows * CB * C * HD * columns, bytes_accessed=4 << 20, transcendentals=0),
         name="project",
-    )(jnp.stack([column, core]), mixed, own_weight, held, partner)
-    part = rows // (RG * CB)
-    summed = lax.all_to_all(summed.reshape(RG * CB, part, columns), MP, 0, 0, tiled=True)
-    summed = summed.reshape(RG, CB, part, columns).astype(jnp.float32)
-    summed = (summed[0] + summed[1]).astype(jnp.bfloat16)
-    return summed.transpose(1, 0, 2).reshape(part, CB * columns)
+    )(spot, mixed, own_weight, held, partner)
+    sums = [sums[0]] + [lax.ppermute(sums[i], MP, [(j, j ^ i) for j in range(n_mp)]) for i in range(1, n_mp)]
+    return pl.pallas_call(
+        add_kernel,
+        out_shape=jax.ShapeDtypeStruct((part, CB * columns), jnp.bfloat16),
+        in_specs=[smem] + [vmem] * n_mp,
+        out_specs=vmem,
+        name="add",
+    )(column[None], *sums)
 
 
 def solution(mesh):

time: 162 us -> 168 us (1.037)
  blocking collectives: 70.5 us -> 33.5 us
  starting transfers between devices: 38.7 us -> 70.8 us
  waiting for transfers between devices: 36.4 us -> 44.3 us
  Pallas kernels: 8.92 us -> 10.8 us
    all_to_all x1 -> x0, blocking collectives: 37 us -> none  [body(): lax.all_to_all(summed.reshape(RG * CB, part, columns), MP, 0, 0, tiled=True)]
    ppermute x0 -> x7, starting transfers between devices: none -> 32.1 us  [body(): lax.ppermute(sums[i], MP, [(j, j ^ i) for j in range(n_mp)])]
    ppermute x0 -> x7, waiting for transfers between devices: none -> 8.07 us  [body(): lax.ppermute(sums[i], MP, [(j, j ^ i) for j in range(n_mp)])]
    pallas_call x1 -> x2, Pallas kernels: 1.29 us -> 3.13 us  [the longest x1 1.82 us: body(): pl.pallas_call(add_kernel, out_shape=jax.ShapeDtypeStruct((part, CB * col...]
    unnamed x16 -> x32, local copies, waits for them, and re-layouts: 2.85 us -> 4.07 us
  transfers between devices with their start and end apart: 10 -> 17, of which waited for: 6 -> 8; matrix products, arithmetic and copies ran while one was open for 1% -> 1% of each run, Pallas kernels for 0% -> 0%
where the time goes in v8:
time: 168 us; the launch traced here: 167 us
  starting transfers between devices  70.8 us (42%)
  waiting for transfers between devices  44.3 us (26%)
  blocking collectives  33.5 us (20%)
  Pallas kernels  10.8 us (6%)
  local copies, waits for them, and re-layouts  6.12 us (4%)
    all_to_all x1, blocking collectives, body(): heads = lax.all_to_all(heads, ('zh', 'c'), 0, 0, tiled=True)  33.5 us
    ppermute x7, starting transfers between devices, body(): lax.ppermute(sums[i], MP, [(j, j ^ i) for j in range(n_mp)])  32.1 us
    ppermute x3, waiting for transfers between devices, body(): lax.ppermute(block, 'cb', [(j, j ^ i + 1) for j in range(CB)])  21.6 us
    ppermute x3, starting transfers between devices, body(): lax.ppermute(block, 'cb', [(j, j ^ i + 1) for j in range(CB)])  10.2 us
    all_to_all x1, starting transfers between devices, spread(): lax.all_to_all(blocks, DP, 0, 0, axis_index_groups=groups, tiled=True)  10.1 us
    all_to_all x1, waiting for transfers between devices, body(): lax.all_to_all(mixed, ('c', 'cb'), 0, 0, tiled=True)  9.53 us
    ppermute x3, starting transfers between devices, body(): squares = [heads] + [lax.ppermute(heads, DP, pairs) for pairs in NEAR]  9.2 us
    ppermute x7, waiting for transfers between devices, body(): lax.ppermute(sums[i], MP, [(j, j ^ i) for j in range(n_mp)])  8.07 us
  transfers between devices with their start and end apart: 17, of which 8 were waited for; matrix products, arithmetic and copies ran while one was open for 1% of the time, Pallas kernels for 0%

profile of v8, /device:TPU:6, one launch (start us, length us, event | category | flops | bytes accessed | tf_op | source)
XLA Modules:
  0.0 167.1 jit_solution(13845416888303857048)
XLA Ops:
  1.1 33.5 %all_to_all.15.after_ref = bf16[4,32,384]{2,1,0:T(8,128)(2,1)S(1)} all-to-all(bf16[4,32,384]{2,1,0:T(8,128)(2,1)S(1)} %bitcast.22), channel_id=1, replica_groups=mesh['zh'=2,'x'=4,'y'=8,'c'=2,'rg'=2,'cb'=4] {'zh','c'}, dimensions={0} | all-to-all | bytes 196608 | tf_op jit(solution)/shard_map/all_to_all | solution.py:143
  35.6 10.1 %all-to-all-start.1 = ((bf16[8,4,32,384]{3,2,1,0:T(8,128)(2,1)}), bf16[8,4,32,384]{3,2,1,0:T(8,128)(2,1)S(1)}, u32[]{:S(2)}, u32[]{:S(2)}) async-start(bf16[8,4,32,384]{3,2,1,0:T(8,128)(2,1)} %broadcast_in_dim.19), calls=%async_computation.1 | async-start | bytes 1572864 | tf_op jit(solution)/shard_map/all_to_all | solution.py:63
  45.6 1.9 %collective-permute-start = (bf16[256,4096]{1,0:T(8,128)(2,1)}, bf16[256,4096]{1,0:T(8,128)(2,1)}, u32[]{:S(2)}, u32[]{:S(2)}) collective-permute-start(bf16[256,4096]{1,0:T(8,128)(2,1)} %own_ref.1), channel_id=1, source_target_pairs={{0,8},{8,0},{1,9},{9,1},{2,10},{10,2},{3,11},{11,3},{4,12},{12,4},... | collective-permute-start | bytes 6291464 | tf_op jit(solution)/shard_map/ppermute | solution.py:139
  49.1 2.0 %collective-permute-start.1 = (bf16[128,1024]{1,0:T(8,128)(2,1)S(1)}, bf16[128,1024]{1,0:T(8,128)(2,1)S(1)}, u32[]{:S(2)}, u32[]{:S(2)}) collective-permute-start(bf16[128,1024]{1,0:T(8,128)(2,1)S(1)} %get-tuple-element.17), channel_id=1, source_target_pairs={{0,1},{1,0},{2,3},{3,2},{4,5},{5,4},{6,7},{7,6},{8,9},{9,8},{10,11... | collective-permute-start | bytes 786440 | tf_op jit(solution)/shard_map/ppermute | solution.py:160
  51.1 3.8 %collective-permute-start.2 = (bf16[128,1024]{1,0:T(8,128)(2,1)S(1)}, bf16[128,1024]{1,0:T(8,128)(2,1)}, u32[]{:S(2)}, u32[]{:S(2)}) collective-permute-start(bf16[128,1024]{1,0:T(8,128)(2,1)S(1)} %get-tuple-element.18), channel_id=1, source_target_pairs={{0,2},{1,3},{2,0},{3,1},{4,6},{5,7},{6,4},{7,5},{8,10},{9,11},{10,... | collective-permute-start | bytes 786440 | tf_op jit(solution)/shard_map/ppermute | solution.py:160
  54.9 8.5 %collective-permute-done.1.refs_1_ = bf16[128,1024]{1,0:T(8,128)(2,1)S(1)} collective-permute-done((bf16[128,1024]{1,0:T(8,128)(2,1)S(1)}, bf16[128,1024]{1,0:T(8,128)(2,1)S(1)}, u32[]{:S(2)}, u32[]{:S(2)}) %collective-permute-start.1) | collective-permute-done | bytes 262176 | tf_op jit(solution)/shard_map/ppermute | solution.py:160
  63.4 5.0 %collective-permute-done.2.refs_2_ = bf16[128,1024]{1,0:T(8,128)(2,1)} collective-permute-done((bf16[128,1024]{1,0:T(8,128)(2,1)S(1)}, bf16[128,1024]{1,0:T(8,128)(2,1)}, u32[]{:S(2)}, u32[]{:S(2)}) %collective-permute-start.2) | collective-permute-done | bytes 262176 | tf_op jit(solution)/shard_map/ppermute | solution.py:160
  69.3 2.6 %collective-permute-start.3 = (bf16[2,4,2,64,384]{4,3,2,1,0:T(8,128)(2,1)}, bf16[2,4,2,64,384]{4,3,2,1,0:T(8,128)(2,1)S(1)}, u32[]{:S(2)}, u32[]{:S(2)}) collective-permute-start(bf16[2,4,2,64,384]{4,3,2,1,0:T(8,128)(2,1)} %bitcast.15), channel_id=1, source_target_pairs={{0,16},{8,120},{16,0},{24,40},{32,48},{40,24},{48,32},{56,72},{64,... | collective-permute-start | bytes 2359304 | tf_op jit(solution)/shard_map/ppermute | solution.py:163
  71.9 2.7 %collective-permute-start.4 = (bf16[2,4,2,64,384]{4,3,2,1,0:T(8,128)(2,1)}, bf16[2,4,2,64,384]{4,3,2,1,0:T(8,128)(2,1)}, u32[]{:S(2)}, u32[]{:S(2)}) collective-permute-start(bf16[2,4,2,64,384]{4,3,2,1,0:T(8,128)(2,1)} %bitcast.16), channel_id=1, source_target_pairs={{0,128},{8,392},{16,144},{24,408},{32,160},{40,424},{48,176},{56,4... | collective-permute-start | bytes 2359304 | tf_op jit(solution)/shard_map/ppermute | solution.py:163
  74.6 3.9 %collective-permute-start.5 = (bf16[2,4,2,64,384]{4,3,2,1,0:T(8,128)(2,1)}, bf16[2,4,2,64,384]{4,3,2,1,0:T(8,128)(2,1)}, u32[]{:S(2)}, u32[]{:S(2)}) collective-permute-start(bf16[2,4,2,64,384]{4,3,2,1,0:T(8,128)(2,1)} %bitcast.17), channel_id=1, source_target_pairs={{0,144},{8,504},{16,128},{24,424},{32,176},{40,408},{48,160},{56,4... | collective-permute-start | bytes 2359304 | tf_op jit(solution)/shard_map/ppermute | solution.py:163
  78.5 4.4 %collective-permute-start.6 = (bf16[128,1024]{1,0:T(8,128)(2,1)S(1)}, bf16[128,1024]{1,0:T(8,128)(2,1)S(1)}, u32[]{:S(2)}, u32[]{:S(2)}) collective-permute-start(bf16[128,1024]{1,0:T(8,128)(2,1)S(1)} %get-tuple-element.19), channel_id=1, source_target_pairs={{0,3},{1,2},{2,1},{3,0},{4,7},{5,6},{6,5},{7,4},{8,11},{9,10},{10,... | collective-permute-start | bytes 786440 | tf_op jit(solution)/shard_map/ppermute | solution.py:160
  83.1 8.1 %collective-permute-done.6.refs_4_ = bf16[128,1024]{1,0:T(8,128)(2,1)S(1)} collective-permute-done((bf16[128,1024]{1,0:T(8,128)(2,1)S(1)}, bf16[128,1024]{1,0:T(8,128)(2,1)S(1)}, u32[]{:S(2)}, u32[]{:S(2)}) %collective-permute-start.6) | collective-permute-done | bytes 262176 | tf_op jit(solution)/shard_map/ppermute | solution.py:160
  91.2 3.3 %collective-permute-done.4.refs_2_ = bf16[2,4,2,64,384]{4,3,2,1,0:T(8,128)(2,1)} collective-permute-done((bf16[2,4,2,64,384]{4,3,2,1,0:T(8,128)(2,1)}, bf16[2,4,2,64,384]{4,3,2,1,0:T(8,128)(2,1)}, u32[]{:S(2)}, u32[]{:S(2)}) %collective-permute-start.4) | collective-permute-done | bytes 786464 | tf_op jit(solution)/shard_map/ppermute | solution.py:163
  95.7 7.0 %attend.1 = bf16[8,256,128]{2,1,0:T(8,128)(2,1)} custom-call(s32[2]{0:T(128)S(1)} %pad_add_fusion.1.place_ref, bf16[256,4096]{1,0:T(8,128)(2,1)S(1)} %copy-done.3, bf16[256,4096]{1,0:T(8,128)(2,1)} %collective-permute-done.other_ref, bf16[2,4,2,64,384]{4,3,2,1,0:T(8,128)(2,1)S(1)} %bitcast.18, ...), custom_call_target="tpu_custom_call" | custom-call | flops 1610612736 | bytes 8388608 | tf_op jit(solution)/shard_map/attend/pallas_call | solution.py:166
  102.7 4.8 %all-to-all-start.2 = ((bf16[8,256,128]{2,1,0:T(8,128)(2,1)}), bf16[8,256,128]{2,1,0:T(8,128)(2,1)S(1)}, u32[]{:S(2)}, u32[]{:S(2)}) async-start(bf16[8,256,128]{2,1,0:T(8,128)(2,1)} %attend.1), calls=%async_computation.2 | async-start | bytes 1048576 | tf_op jit(solution)/shard_map/all_to_all | solution.py:177
  108.6 2.4 %collective-permute-start.7 = (bf16[3,128,1024]{2,1,0:T(8,128)(2,1)S(1)}, bf16[3,128,1024]{2,1,0:T(8,128)(2,1)S(1)}, u32[]{:S(2)}, u32[]{:S(2)}) collective-permute-start(bf16[3,128,1024]{2,1,0:T(8,128)(2,1)S(1)} %pad_maximum_fusion.held_ref), channel_id=1, source_target_pairs={{0,8},{8,0},{1,9},{9,1},{2,10},{10,2},{3,11},{11,3},{4,12},{12,4},... | collective-permute-start | bytes 2359304 | tf_op jit(solution)/shard_map/ppermute | solution.py:176
  112.9 9.5 %all-to-all-done.2 = bf16[8,256,128]{2,1,0:T(8,128)(2,1)S(1)} async-done(((bf16[8,256,128]{2,1,0:T(8,128)(2,1)}), bf16[8,256,128]{2,1,0:T(8,128)(2,1)S(1)}, u32[]{:S(2)}, u32[]{:S(2)}) %all-to-all-start.2) | async-done | bytes 524320 | tf_op jit(solution)/shard_map/all_to_all | solution.py:177
  126.3 2.8 %collective-permute-start.9 = (bf16[32,1024]{1,0:T(8,128)(2,1)S(1)}, bf16[32,1024]{1,0:T(8,128)(2,1)S(1)}, u32[]{:S(2)}, u32[]{:S(2)}) collective-permute-start(bf16[32,1024]{1,0:T(8,128)(2,1)S(1)} %get-tuple-element.23), channel_id=1, source_target_pairs={{0,2},{1,3},{2,0},{3,1},{4,6},{5,7},{6,4},{7,5},{8,10},{9,11},{10,... | collective-permute-start | bytes 196616 | tf_op jit(solution)/shard_map/ppermute | solution.py:192
  129.1 5.4 %collective-permute-start.10 = (bf16[32,1024]{1,0:T(8,128)(2,1)S(1)}, bf16[32,1024]{1,0:T(8,128)(2,1)S(1)}, u32[]{:S(2)}, u32[]{:S(2)}) collective-permute-start(bf16[32,1024]{1,0:T(8,128)(2,1)S(1)} %get-tuple-element.24), channel_id=1, source_target_pairs={{0,3},{1,2},{2,1},{3,0},{4,7},{5,6},{6,5},{7,4},{8,11},{9,10},{10,... | collective-permute-start | bytes 196616 | tf_op jit(solution)/shard_map/ppermute | solution.py:192
  134.5 8.5 %collective-permute-start.11 = (bf16[32,1024]{1,0:T(8,128)(2,1)S(1)}, bf16[32,1024]{1,0:T(8,128)(2,1)S(1)}, u32[]{:S(2)}, u32[]{:S(2)}) collective-permute-start(bf16[32,1024]{1,0:T(8,128)(2,1)S(1)} %get-tuple-element.25), channel_id=1, source_target_pairs={{0,4},{1,5},{2,6},{3,7},{4,0},{5,1},{6,2},{7,3},{8,12},{9,13},{10,... | collective-permute-start | bytes 196616 | tf_op jit(solution)/shard_map/ppermute | solution.py:192
  143.0 1.9 %collective-permute-start.12 = (bf16[32,1024]{1,0:T(8,128)(2,1)S(1)}, bf16[32,1024]{1,0:T(8,128)(2,1)S(1)}, u32[]{:S(2)}, u32[]{:S(2)}) collective-permute-start(bf16[32,1024]{1,0:T(8,128)(2,1)S(1)} %get-tuple-element.26), channel_id=1, source_target_pairs={{0,5},{1,4},{2,7},{3,6},{4,1},{5,0},{6,3},{7,2},{8,13},{9,12},{10,... | collective-permute-start | bytes 196616 | tf_op jit(solution)/shard_map/ppermute | solution.py:192
  145.0 6.7 %collective-permute-start.13 = (bf16[32,1024]{1,0:T(8,128)(2,1)S(1)}, bf16[32,1024]{1,0:T(8,128)(2,1)S(1)}, u32[]{:S(2)}, u32[]{:S(2)}) collective-permute-start(bf16[32,1024]{1,0:T(8,128)(2,1)S(1)} %get-tuple-element.27), channel_id=1, source_target_pairs={{0,6},{1,7},{2,4},{3,5},{4,2},{5,3},{6,0},{7,1},{8,14},{9,15},{10,... | collective-permute-start | bytes 196616 | tf_op jit(solution)/shard_map/ppermute | solution.py:192
  151.7 4.8 %collective-permute-start.14 = (bf16[32,1024]{1,0:T(8,128)(2,1)S(1)}, bf16[32,1024]{1,0:T(8,128)(2,1)S(1)}, u32[]{:S(2)}, u32[]{:S(2)}) collective-permute-start(bf16[32,1024]{1,0:T(8,128)(2,1)S(1)} %get-tuple-element.28), channel_id=1, source_target_pairs={{0,7},{1,6},{2,5},{3,4},{4,3},{5,2},{6,1},{7,0},{8,15},{9,14},{10,... | collective-permute-start | bytes 196616 | tf_op jit(solution)/shard_map/ppermute | solution.py:192
  157.7 7.0 %collective-permute-done.14.refs_7_ = bf16[32,1024]{1,0:T(8,128)(2,1)S(1)} collective-permute-done((bf16[32,1024]{1,0:T(8,128)(2,1)S(1)}, bf16[32,1024]{1,0:T(8,128)(2,1)S(1)}, u32[]{:S(2)}, u32[]{:S(2)}) %collective-permute-start.14) | collective-permute-done | bytes 65568 | tf_op jit(solution)/shard_map/ppermute | solution.py:192
  (57 shorter events, 16.0 us)
Async XLA Ops:
  0.0 47.6 %copy-start.2 = (bf16[256,4096]{1,0:T(8,128)(2,1)S(1)}, bf16[256,4096]{1,0:T(8,128)(2,1)}, u32[]{:S(2)}) copy-start(bf16[256,4096]{1,0:T(8,128)(2,1)} %w_ref.1) | copy-start | bytes 6291460
  35.6 32.8 %all-to-all-start.1 = ((bf16[8,4,32,384]{3,2,1,0:T(8,128)(2,1)}), bf16[8,4,32,384]{3,2,1,0:T(8,128)(2,1)S(1)}, u32[]{:S(2)}, u32[]{:S(2)}) async-start(bf16[8,4,32,384]{3,2,1,0:T(8,128)(2,1)} %broadcast_in_dim.19), calls=%async_computation.1 | async-start | bytes 1572864 | tf_op jit(solution)/shard_map/all_to_all | solution.py:63
  45.6 45.5 %collective-permute-start = (bf16[256,4096]{1,0:T(8,128)(2,1)}, bf16[256,4096]{1,0:T(8,128)(2,1)}, u32[]{:S(2)}, u32[]{:S(2)}) collective-permute-start(bf16[256,4096]{1,0:T(8,128)(2,1)} %own_ref.1), channel_id=1, source_target_pairs={{0,8},{8,0},{1,9},{9,1},{2,10},{10,2},{3,11},{11,3},{4,12},{12,4},... | collective-permute-start | bytes 6291464 | tf_op jit(solution)/shard_map/ppermute | solution.py:139
  49.1 45.4 %copy-start.3 = (bf16[256,4096]{1,0:T(8,128)(2,1)S(1)}, bf16[256,4096]{1,0:T(8,128)(2,1)}, u32[]{:S(2)}) copy-start(bf16[256,4096]{1,0:T(8,128)(2,1)} %own_ref.1) | copy-start | bytes 6291460
  49.1 14.4 %collective-permute-start.1 = (bf16[128,1024]{1,0:T(8,128)(2,1)S(1)}, bf16[128,1024]{1,0:T(8,128)(2,1)S(1)}, u32[]{:S(2)}, u32[]{:S(2)}) collective-permute-start(bf16[128,1024]{1,0:T(8,128)(2,1)S(1)} %get-tuple-element.17), channel_id=1, source_target_pairs={{0,1},{1,0},{2,3},{3,2},{4,5},{5,4},{6,7},{7,6},{8,9},{9,8},{10,11... | collective-permute-start | bytes 786440 | tf_op jit(solution)/shard_map/ppermute | solution.py:160
  51.1 17.3 %collective-permute-start.2 = (bf16[128,1024]{1,0:T(8,128)(2,1)S(1)}, bf16[128,1024]{1,0:T(8,128)(2,1)}, u32[]{:S(2)}, u32[]{:S(2)}) collective-permute-start(bf16[128,1024]{1,0:T(8,128)(2,1)S(1)} %get-tuple-element.18), channel_id=1, source_target_pairs={{0,2},{1,3},{2,0},{3,1},{4,6},{5,7},{6,4},{7,5},{8,10},{9,11},{10,... | collective-permute-start | bytes 786440 | tf_op jit(solution)/shard_map/ppermute | solution.py:160
  69.3 21.9 %collective-permute-start.3 = (bf16[2,4,2,64,384]{4,3,2,1,0:T(8,128)(2,1)}, bf16[2,4,2,64,384]{4,3,2,1,0:T(8,128)(2,1)S(1)}, u32[]{:S(2)}, u32[]{:S(2)}) collective-permute-start(bf16[2,4,2,64,384]{4,3,2,1,0:T(8,128)(2,1)} %bitcast.15), channel_id=1, source_target_pairs={{0,16},{8,120},{16,0},{24,40},{32,48},{40,24},{48,32},{56,72},{64,... | collective-permute-start | bytes 2359304 | tf_op jit(solution)/shard_map/ppermute | solution.py:163
  71.9 22.6 %collective-permute-start.4 = (bf16[2,4,2,64,384]{4,3,2,1,0:T(8,128)(2,1)}, bf16[2,4,2,64,384]{4,3,2,1,0:T(8,128)(2,1)}, u32[]{:S(2)}, u32[]{:S(2)}) collective-permute-start(bf16[2,4,2,64,384]{4,3,2,1,0:T(8,128)(2,1)} %bitcast.16), channel_id=1, source_target_pairs={{0,128},{8,392},{16,144},{24,408},{32,160},{40,424},{48,176},{56,4... | collective-permute-start | bytes 2359304 | tf_op jit(solution)/shard_map/ppermute | solution.py:163
  74.6 19.9 %collective-permute-start.5 = (bf16[2,4,2,64,384]{4,3,2,1,0:T(8,128)(2,1)}, bf16[2,4,2,64,384]{4,3,2,1,0:T(8,128)(2,1)}, u32[]{:S(2)}, u32[]{:S(2)}) collective-permute-start(bf16[2,4,2,64,384]{4,3,2,1,0:T(8,128)(2,1)} %bitcast.17), channel_id=1, source_target_pairs={{0,144},{8,504},{16,128},{24,424},{32,176},{40,408},{48,160},{56,4... | collective-permute-start | bytes 2359304 | tf_op jit(solution)/shard_map/ppermute | solution.py:163
  78.5 12.6 %collective-permute-start.6 = (bf16[128,1024]{1,0:T(8,128)(2,1)S(1)}, bf16[128,1024]{1,0:T(8,128)(2,1)S(1)}, u32[]{:S(2)}, u32[]{:S(2)}) collective-permute-start(bf16[128,1024]{1,0:T(8,128)(2,1)S(1)} %get-tuple-element.19), channel_id=1, source_target_pairs={{0,3},{1,2},{2,1},{3,0},{4,7},{5,6},{6,5},{7,4},{8,11},{9,10},{10,... | collective-permute-start | bytes 786440 | tf_op jit(solution)/shard_map/ppermute | solution.py:160
  95.7 11.8 %copy-start.8 = (bf16[128,1024]{1,0:T(8,128)(2,1)S(1)}, bf16[128,1024]{1,0:T(8,128)(2,1)}, u32[]{:S(2)}) copy-start(bf16[128,1024]{1,0:T(8,128)(2,1)} %copy-done.7) | copy-start | bytes 786436
  102.7 19.7 %copy-start.5 = (bf16[256,1024]{1,0:T(8,128)(2,1)S(1)}, bf16[256,1024]{1,0:T(8,128)(2,1)}, u32[]{:S(2)}) copy-start(bf16[256,1024]{1,0:T(8,128)(2,1)} %copy-done.4) | copy-start | bytes 1572868
  102.7 19.7 %all-to-all-start.2 = ((bf16[8,256,128]{2,1,0:T(8,128)(2,1)}), bf16[8,256,128]{2,1,0:T(8,128)(2,1)S(1)}, u32[]{:S(2)}, u32[]{:S(2)}) async-start(bf16[8,256,128]{2,1,0:T(8,128)(2,1)} %attend.1), calls=%async_computation.2 | async-start | bytes 1048576 | tf_op jit(solution)/shard_map/all_to_all | solution.py:177
  108.6 4.3 %collective-permute-start.7 = (bf16[3,128,1024]{2,1,0:T(8,128)(2,1)S(1)}, bf16[3,128,1024]{2,1,0:T(8,128)(2,1)S(1)}, u32[]{:S(2)}, u32[]{:S(2)}) collective-permute-start(bf16[3,128,1024]{2,1,0:T(8,128)(2,1)S(1)} %pad_maximum_fusion.held_ref), channel_id=1, source_target_pairs={{0,8},{8,0},{1,9},{9,1},{2,10},{10,2},{3,11},{11,3},{4,12},{12,4},... | collective-permute-start | bytes 2359304 | tf_op jit(solution)/shard_map/ppermute | solution.py:176
  124.3 20.6 %collective-permute-start.8 = (bf16[32,1024]{1,0:T(8,128)(2,1)S(1)}, bf16[32,1024]{1,0:T(8,128)(2,1)S(1)}, u32[]{:S(2)}, u32[]{:S(2)}) collective-permute-start(bf16[32,1024]{1,0:T(8,128)(2,1)S(1)} %get-tuple-element.22), channel_id=1, source_target_pairs={{0,1},{1,0},{2,3},{3,2},{4,5},{5,4},{6,7},{7,6},{8,9},{9,8},{10,11... | collective-permute-start | bytes 196616 | tf_op jit(solution)/shard_map/ppermute | solution.py:192
  126.3 25.4 %collective-permute-start.9 = (bf16[32,1024]{1,0:T(8,128)(2,1)S(1)}, bf16[32,1024]{1,0:T(8,128)(2,1)S(1)}, u32[]{:S(2)}, u32[]{:S(2)}) collective-permute-start(bf16[32,1024]{1,0:T(8,128)(2,1)S(1)} %get-tuple-element.23), channel_id=1, source_target_pairs={{0,2},{1,3},{2,0},{3,1},{4,6},{5,7},{6,4},{7,5},{8,10},{9,11},{10,... | collective-permute-start | bytes 196616 | tf_op jit(solution)/shard_map/ppermute | solution.py:192
  129.1 27.5 %collective-permute-start.10 = (bf16[32,1024]{1,0:T(8,128)(2,1)S(1)}, bf16[32,1024]{1,0:T(8,128)(2,1)S(1)}, u32[]{:S(2)}, u32[]{:S(2)}) collective-permute-start(bf16[32,1024]{1,0:T(8,128)(2,1)S(1)} %get-tuple-element.24), channel_id=1, source_target_pairs={{0,3},{1,2},{2,1},{3,0},{4,7},{5,6},{6,5},{7,4},{8,11},{9,10},{10,... | collective-permute-start | bytes 196616 | tf_op jit(solution)/shard_map/ppermute | solution.py:192
  134.5 22.1 %collective-permute-start.11 = (bf16[32,1024]{1,0:T(8,128)(2,1)S(1)}, bf16[32,1024]{1,0:T(8,128)(2,1)S(1)}, u32[]{:S(2)}, u32[]{:S(2)}) collective-permute-start(bf16[32,1024]{1,0:T(8,128)(2,1)S(1)} %get-tuple-element.25), channel_id=1, source_target_pairs={{0,4},{1,5},{2,6},{3,7},{4,0},{5,1},{6,2},{7,3},{8,12},{9,13},{10,... | collective-permute-start | bytes 196616 | tf_op jit(solution)/shard_map/ppermute | solution.py:192
  143.0 14.7 %collective-permute-start.12 = (bf16[32,1024]{1,0:T(8,128)(2,1)S(1)}, bf16[32,1024]{1,0:T(8,128)(2,1)S(1)}, u32[]{:S(2)}, u32[]{:S(2)}) collective-permute-start(bf16[32,1024]{1,0:T(8,128)(2,1)S(1)} %get-tuple-element.26), channel_id=1, source_target_pairs={{0,5},{1,4},{2,7},{3,6},{4,1},{5,0},{6,3},{7,2},{8,13},{9,12},{10,... | collective-permute-start | bytes 196616 | tf_op jit(solution)/shard_map/ppermute | solution.py:192
  144.9 19.7 %copy-start.9 = (bf16[32,1024]{1,0:T(8,128)(2,1)}, bf16[32,1024]{1,0:T(8,128)(2,1)S(1)}, u32[]{:S(2)}) copy-start(bf16[32,1024]{1,0:T(8,128)(2,1)S(1)} %collective-permute-done.8.refs_1_) | copy-start | bytes 196612
  145.0 12.7 %collective-permute-start.13 = (bf16[32,1024]{1,0:T(8,128)(2,1)S(1)}, bf16[32,1024]{1,0:T(8,128)(2,1)S(1)}, u32[]{:S(2)}, u32[]{:S(2)}) collective-permute-start(bf16[32,1024]{1,0:T(8,128)(2,1)S(1)} %get-tuple-element.27), channel_id=1, source_target_pairs={{0,6},{1,7},{2,4},{3,5},{4,2},{5,3},{6,0},{7,1},{8,14},{9,15},{10,... | collective-permute-start | bytes 196616 | tf_op jit(solution)/shard_map/ppermute | solution.py:192
  151.7 13.0 %copy-start.10 = (bf16[32,1024]{1,0:T(8,128)(2,1)}, bf16[32,1024]{1,0:T(8,128)(2,1)S(1)}, u32[]{:S(2)}) copy-start(bf16[32,1024]{1,0:T(8,128)(2,1)S(1)} %collective-permute-done.9.refs_2_) | copy-start | bytes 196612
  151.7 13.0 %collective-permute-start.14 = (bf16[32,1024]{1,0:T(8,128)(2,1)S(1)}, bf16[32,1024]{1,0:T(8,128)(2,1)S(1)}, u32[]{:S(2)}, u32[]{:S(2)}) collective-permute-start(bf16[32,1024]{1,0:T(8,128)(2,1)S(1)} %get-tuple-element.28), channel_id=1, source_target_pairs={{0,7},{1,6},{2,5},{3,4},{4,3},{5,2},{6,1},{7,0},{8,15},{9,14},{10,... | collective-permute-start | bytes 196616 | tf_op jit(solution)/shard_map/ppermute | solution.py:192
  156.6 8.1 %copy-start.11 = (bf16[32,1024]{1,0:T(8,128)(2,1)}, bf16[32,1024]{1,0:T(8,128)(2,1)S(1)}, u32[]{:S(2)}) copy-start(bf16[32,1024]{1,0:T(8,128)(2,1)S(1)} %collective-permute-done.10.refs_3_) | copy-start | bytes 196612
  (9 other events, 31.2 us)

commit v9 on v7

--- a/solution.py
+++ b/solution.py
@@ -66,13 +66,18 @@
 def attend_kernel(place_ref, own_ref, other_ref, *refs):
     w_refs, (out_ref, held_ref, sems) = refs[:4], refs[5:]
     me, core = place_ref[0], place_ref[1]
-    for i, w_ref in enumerate(w_refs):
-        pltpu.make_async_copy(w_ref, held_ref.at[me ^ i], sems.at[i]).start()
+    for i in range(1, 4):
+        pltpu.make_async_copy(w_refs[i], held_ref.at[me ^ i], sems.at[me ^ i]).start()
+    held_ref[me] = w_refs[0][...]
     span = Y * held_ref.shape[4]
     totals = [None, None]
     for px in range(2):
         for slot in (2 * px, 2 * px + 1):
-            pltpu.make_async_copy(w_refs[0], held_ref.at[slot], sems.at[me ^ slot]).wait()
+
+            @pl.when(slot != me)
+            def _():
+                pltpu.make_async_copy(w_refs[1], held_ref.at[slot], sems.at[slot]).wait()
+
         for zh in range(ZH):
             for xq in range(XQ):
                 weight = jnp.concatenate(
@@ -97,28 +102,42 @@
             out_ref[(core ^ g) * CB + cb] = mixed
 
 
-def split_kernel(place_ref, w_ref, after_ref, own_ref, *out_refs):
+def split_kernel(place_ref, w_ref, *refs):
     column, core = place_ref[0], place_ref[1]
+    out_refs = refs[1:]
     part, width = out_refs[0].shape
-    own_ref[...] = w_ref[:, pl.ds(pl.multiple_of(column * width, width), width)]
     rows = pl.ds(pl.multiple_of(core * part, part), part)
     for i, out_ref in enumerate(out_refs):
         start = pl.multiple_of((column ^ (i + 1)) * width, width)
         out_ref[...] = w_ref[rows, pl.ds(start, width)]
 
 
-def project_kernel(place_ref, mixed_ref, own_ref, held_ref, partner_ref, out_ref):
+def project_kernel(place_ref, mixed_ref, w_ref, held_ref, partner_ref, out_ref, own_ref, sem):
     column, core = place_ref[0], place_ref[1]
-    mixed = jnp.concatenate([mixed_ref[c, column] for c in range(C)], axis=1)
-    term = jnp.dot(mixed, own_ref[...], preferred_element_type=jnp.float32).astype(jnp.bfloat16)
-    total = term.astype(jnp.float32)
+    width = own_ref.shape[1]
+    fetch = pltpu.make_async_copy(
+        w_ref.at[:, pl.ds(pl.multiple_of(column * width, width), width)], own_ref, sem
+    )
+    fetch.start()
+    total = None
     for i in range(CB - 1):
         block = column ^ (i + 1)
         mixed = jnp.concatenate([mixed_ref[core, block], mixed_ref[1 - core, block]], axis=1)
         weight = jnp.concatenate([held_ref[i], partner_ref[i]], axis=0)
         term = jnp.dot(mixed, weight, preferred_element_type=jnp.float32).astype(jnp.bfloat16)
-        total += term.astype(jnp.float32)
-    out_ref[...] = total.astype(out_ref.dtype)
+        wide = term.astype(jnp.float32)
+        total = wide if total is None else total + wide
+    fetch.wait()
+    mixed = jnp.concatenate([mixed_ref[c, column] for c in range(C)], axis=1)
+    term = jnp.dot(mixed, own_ref[...], preferred_element_type=jnp.float32).astype(jnp.bfloat16)
+    out_ref[...] = (total + term.astype(jnp.float32)).astype(out_ref.dtype)
+
+
+def add_kernel(sums_ref, out_ref):
+    width = sums_ref.shape[3]
+    for cb in range(CB):
+        total = sums_ref[0, cb].astype(jnp.float32) + sums_ref[1, cb].astype(jnp.float32)
+        out_ref[:, cb * width : (cb + 1) * width] = total.astype(out_ref.dtype)
 
 
 def body(tokens, qkv_weight, out_weight):
@@ -135,26 +154,27 @@
     column, core = lax.axis_index("cb"), lax.axis_index("c")
     depth, columns = out_weight.shape[0], out_weight.shape[1] // CB
     smem, vmem = pl.BlockSpec(memory_space=pltpu.SMEM), pl.BlockSpec(memory_space=pltpu.VMEM)
-    own_weight, *sent = pl.pallas_call(
+    sent = pl.pallas_call(
         split_kernel,
-        out_shape=[jax.ShapeDtypeStruct((depth, columns), jnp.bfloat16)]
-        + [jax.ShapeDtypeStruct((depth // C, columns), jnp.bfloat16)] * (CB - 1),
+        out_shape=[jax.ShapeDtypeStruct((depth // C, columns), jnp.bfloat16)] * (CB - 1),
         in_specs=[smem, vmem, vmem],
-        out_specs=[vmem] * CB,
+        out_specs=[vmem] * (CB - 1),
         compiler_params=pltpu.CompilerParams(vmem_limit_bytes=24 << 20),
         cost_estimate=pl.CostEstimate(flops=0, bytes_accessed=4 << 20, transcendentals=0),
         name="split",
     )(jnp.stack([column, core]), out_weight, first)
     held = [lax.ppermute(block, "cb", [(j, j ^ (i + 1)) for j in range(CB)]) for i, block in enumerate(sent)]
 
-    heads = behind(heads, held[:2]).reshape(XQ, YQ, ZH, C * k_rows, 3 * HD)
-    squares = [heads] + [lax.ppermute(heads, DP, pairs) for pairs in NEAR]
+    shape = (XQ, YQ, ZH, C * k_rows, 3 * HD)
+    sent = behind(heads, held[:2]).reshape(shape)
+    heads = heads.reshape(shape)
+    squares = [heads] + [lax.ppermute(sent, DP, pairs) for pairs in NEAR]
     parity = lax.axis_index("x") % 2 * 2 + lax.axis_index("y") % 2
 
     mixed = pl.pallas_call(
         attend_kernel,
         out_shape=jax.ShapeDtypeStruct((C * CB, rows, HD), jnp.bfloat16),
-        in_specs=[smem] + [vmem] * 2 + [ANYWHERE] * 5,
+        in_specs=[smem] + [vmem] * 3 + [ANYWHERE] * 4,
         scratch_shapes=[pltpu.VMEM((4,) + heads.shape, jnp.bfloat16), pltpu.SemaphoreType.DMA((4,))],
         compiler_params=pltpu.CompilerParams(vmem_limit_bytes=48 << 20),
         cost_estimate=pl.CostEstimate(flops=2 * 2 * rows * width * 3 * HD, bytes_accessed=8 << 20, transcendentals=0),
@@ -167,17 +187,22 @@
     summed = pl.pallas_call(
         project_kernel,
         out_shape=jax.ShapeDtypeStruct((rows, columns), jnp.bfloat16),
-        in_specs=[smem] + [vmem] * 4,
+        in_specs=[smem, vmem, ANYWHERE, vmem, vmem],
         out_specs=vmem,
+        scratch_shapes=[pltpu.VMEM((depth, columns), jnp.bfloat16), pltpu.SemaphoreType.DMA(())],
         compiler_params=pltpu.CompilerParams(vmem_limit_bytes=24 << 20),
         cost_estimate=pl.CostEstimate(flops=2 * rows * CB * C * HD * columns, bytes_accessed=4 << 20, transcendentals=0),
         name="project",
-    )(jnp.stack([column, core]), mixed, own_weight, held, partner)
+    )(jnp.stack([column, core]), mixed, out_weight, held, partner)
     part = rows // (RG * CB)
     summed = lax.all_to_all(summed.reshape(RG * CB, part, columns), MP, 0, 0, tiled=True)
-    summed = summed.reshape(RG, CB, part, columns).astype(jnp.float32)
-    summed = (summed[0] + summed[1]).astype(jnp.bfloat16)
-    return summed.transpose(1, 0, 2).reshape(part, CB * columns)
+    return pl.pallas_call(
+        add_kernel,
+        out_shape=jax.ShapeDtypeStruct((part, CB * columns), jnp.bfloat16),
+        in_specs=[vmem],
+        out_specs=vmem,
+        name="add",
+    )(summed.reshape(RG, CB, part, columns))
 
 
 def solution(mesh):

time: 162 us -> 164 us (1.012)
  Pallas kernels: 8.92 us -> 11.8 us
  waiting for transfers between devices: 36.4 us -> 34.6 us
    ppermute x3, waiting for transfers between devices: 21.6 us -> 10.2 us  [body(): lax.ppermute(block, 'cb', [(j, j ^ i + 1) for j in range(CB)])]
    all_to_all x1, waiting for transfers between devices: 0.01 us -> 10.7 us  [spread(): lax.all_to_all(blocks, DP, 0, 0, axis_index_groups=groups, tiled=True)]
    pallas_call x1 -> x2, Pallas kernels: 0.63 us -> 3.19 us  [the longest x1 1.81 us: body(): pl.pallas_call(add_kernel, out_shape=jax.ShapeDtypeStruct((part, CB * col...]
    unnamed x16 -> x13, local copies, waits for them, and re-layouts: 2.85 us -> 4.51 us
  transfers between devices with their start and end apart: 10 -> 10, of which waited for: 6 -> 6; matrix products, arithmetic and copies ran while one was open for 1% -> 1% of each run, Pallas kernels for 0% -> 1%
where the time goes in v9:
time: 164 us; the launch traced here: 163 us
  blocking collectives  70.6 us (43%)
  starting transfers between devices  38.4 us (23%)
  waiting for transfers between devices  34.6 us (21%)
  Pallas kernels  11.8 us (7%)
  local copies, waits for them, and re-layouts  6.57 us (4%)
    all_to_all x1, blocking collectives, body(): lax.all_to_all(summed.reshape(RG * CB, part, columns), MP, 0, 0, tiled=True)  37.1 us
    all_to_all x1, blocking collectives, body(): heads = lax.all_to_all(heads, ('zh', 'c'), 0, 0, tiled=True)  33.5 us
    all_to_all x1, waiting for transfers between devices, spread(): lax.all_to_all(blocks, DP, 0, 0, axis_index_groups=groups, tiled=True)  10.7 us
    ppermute x3, waiting for transfers between devices, body(): lax.ppermute(block, 'cb', [(j, j ^ i + 1) for j in range(CB)])  10.2 us
    ppermute x3, starting transfers between devices, body(): lax.ppermute(block, 'cb', [(j, j ^ i + 1) for j in range(CB)])  10.1 us
    all_to_all x1, starting transfers between devices, spread(): lax.all_to_all(blocks, DP, 0, 0, axis_index_groups=groups, tiled=True)  10.1 us
    ppermute x3, starting transfers between devices, body(): squares = [heads] + [lax.ppermute(sent, DP, pairs) for pairs in NEAR]  9.21 us
    all_to_all x1, waiting for transfers between devices, body(): lax.all_to_all(mixed, ('c', 'cb'), 0, 0, tiled=True)  8.48 us
  transfers between devices with their start and end apart: 10, of which 6 were waited for; matrix products, arithmetic and copies ran while one was open for 1% of the time, Pallas kernels for 1%

profile of v9, /device:TPU:6, one launch (start us, length us, event | category | flops | bytes accessed | tf_op | source)
XLA Modules:
  0.0 163.5 jit_solution(9991530899635645074)
XLA Ops:
  1.1 33.5 %all_to_all.20.refs_0_ = bf16[4,32,384]{2,1,0:T(8,128)(2,1)S(1)} all-to-all(bf16[4,32,384]{2,1,0:T(8,128)(2,1)S(1)} %bitcast.26), channel_id=1, replica_groups=mesh['zh'=2,'x'=4,'y'=8,'c'=2,'rg'=2,'cb'=4] {'zh','c'}, dimensions={0} | all-to-all | bytes 196608 | tf_op jit(solution)/shard_map/all_to_all | solution.py:150
  35.6 10.1 %all-to-all-start.1 = ((bf16[8,4,32,384]{3,2,1,0:T(8,128)(2,1)}), bf16[8,4,32,384]{3,2,1,0:T(8,128)(2,1)S(1)}, u32[]{:S(2)}, u32[]{:S(2)}) async-start(bf16[8,4,32,384]{3,2,1,0:T(8,128)(2,1)} %broadcast_in_dim.15), calls=%async_computation.1 | async-start | bytes 1572864 | tf_op jit(solution)/shard_map/all_to_all | solution.py:63
  45.7 1.9 %collective-permute-start = (bf16[256,4096]{1,0:T(8,128)(2,1)}, bf16[256,4096]{1,0:T(8,128)(2,1)}, u32[]{:S(2)}, u32[]{:S(2)}) collective-permute-start(bf16[256,4096]{1,0:T(8,128)(2,1)} %own_ref.1), channel_id=1, source_target_pairs={{0,8},{8,0},{1,9},{9,1},{2,10},{10,2},{3,11},{11,3},{4,12},{12,4},... | collective-permute-start | bytes 6291464 | tf_op jit(solution)/shard_map/ppermute | solution.py:146
  47.7 1.4 split.1
  49.0 1.9 %collective-permute-start.1 = (bf16[128,1024]{1,0:T(8,128)(2,1)}, bf16[128,1024]{1,0:T(8,128)(2,1)S(1)}, u32[]{:S(2)}, u32[]{:S(2)}) collective-permute-start(bf16[128,1024]{1,0:T(8,128)(2,1)} %get-tuple-element.8), channel_id=1, source_target_pairs={{0,1},{1,0},{2,3},{3,2},{4,5},{5,4},{6,7},{7,6},{8,9},{9,8},{10,11... | collective-permute-start | bytes 786440 | tf_op jit(solution)/shard_map/ppermute | solution.py:166
  51.0 3.8 %collective-permute-start.2 = (bf16[128,1024]{1,0:T(8,128)(2,1)}, bf16[128,1024]{1,0:T(8,128)(2,1)}, u32[]{:S(2)}, u32[]{:S(2)}) collective-permute-start(bf16[128,1024]{1,0:T(8,128)(2,1)} %get-tuple-element.9), channel_id=1, source_target_pairs={{0,2},{1,3},{2,0},{3,1},{4,6},{5,7},{6,4},{7,5},{8,10},{9,11},{10,... | collective-permute-start | bytes 786440 | tf_op jit(solution)/shard_map/ppermute | solution.py:166
  54.7 10.7 %all-to-all-done.1 = bf16[8,4,32,384]{3,2,1,0:T(8,128)(2,1)S(1)} async-done(((bf16[8,4,32,384]{3,2,1,0:T(8,128)(2,1)}), bf16[8,4,32,384]{3,2,1,0:T(8,128)(2,1)S(1)}, u32[]{:S(2)}, u32[]{:S(2)}) %all-to-all-start.1) | async-done | bytes 786464 | tf_op jit(solution)/shard_map/all_to_all | solution.py:63
  66.3 2.1 %collective-permute-done.2.refs_2_ = bf16[128,1024]{1,0:T(8,128)(2,1)} collective-permute-done((bf16[128,1024]{1,0:T(8,128)(2,1)}, bf16[128,1024]{1,0:T(8,128)(2,1)}, u32[]{:S(2)}, u32[]{:S(2)}) %collective-permute-start.2) | collective-permute-done | bytes 262176 | tf_op jit(solution)/shard_map/ppermute | solution.py:166
  68.4 2.6 %collective-permute-start.3 = (bf16[2,4,2,64,384]{4,3,2,1,0:T(8,128)(2,1)}, bf16[2,4,2,64,384]{4,3,2,1,0:T(8,128)(2,1)}, u32[]{:S(2)}, u32[]{:S(2)}) collective-permute-start(bf16[2,4,2,64,384]{4,3,2,1,0:T(8,128)(2,1)} %bitcast.21), channel_id=1, source_target_pairs={{0,16},{8,120},{16,0},{24,40},{32,48},{40,24},{48,32},{56,72},{64,... | collective-permute-start | bytes 2359304 | tf_op jit(solution)/shard_map/ppermute | solution.py:171
  71.0 2.7 %collective-permute-start.4 = (bf16[2,4,2,64,384]{4,3,2,1,0:T(8,128)(2,1)}, bf16[2,4,2,64,384]{4,3,2,1,0:T(8,128)(2,1)}, u32[]{:S(2)}, u32[]{:S(2)}) collective-permute-start(bf16[2,4,2,64,384]{4,3,2,1,0:T(8,128)(2,1)} %bitcast.22), channel_id=1, source_target_pairs={{0,128},{8,392},{16,144},{24,408},{32,160},{40,424},{48,176},{56,4... | collective-permute-start | bytes 2359304 | tf_op jit(solution)/shard_map/ppermute | solution.py:171
  73.8 3.9 %collective-permute-start.5 = (bf16[2,4,2,64,384]{4,3,2,1,0:T(8,128)(2,1)}, bf16[2,4,2,64,384]{4,3,2,1,0:T(8,128)(2,1)}, u32[]{:S(2)}, u32[]{:S(2)}) collective-permute-start(bf16[2,4,2,64,384]{4,3,2,1,0:T(8,128)(2,1)} %bitcast.23), channel_id=1, source_target_pairs={{0,144},{8,504},{16,128},{24,424},{32,176},{40,408},{48,160},{56,4... | collective-permute-start | bytes 2359304 | tf_op jit(solution)/shard_map/ppermute | solution.py:171
  77.7 4.4 %collective-permute-start.6 = (bf16[128,1024]{1,0:T(8,128)(2,1)S(1)}, bf16[128,1024]{1,0:T(8,128)(2,1)S(1)}, u32[]{:S(2)}, u32[]{:S(2)}) collective-permute-start(bf16[128,1024]{1,0:T(8,128)(2,1)S(1)} %get-tuple-element.10), channel_id=1, source_target_pairs={{0,3},{1,2},{2,1},{3,0},{4,7},{5,6},{6,5},{7,4},{8,11},{9,10},{10,... | collective-permute-start | bytes 786440 | tf_op jit(solution)/shard_map/ppermute | solution.py:166
  82.2 8.1 %collective-permute-done.6.refs_4_ = bf16[128,1024]{1,0:T(8,128)(2,1)S(1)} collective-permute-done((bf16[128,1024]{1,0:T(8,128)(2,1)S(1)}, bf16[128,1024]{1,0:T(8,128)(2,1)S(1)}, u32[]{:S(2)}, u32[]{:S(2)}) %collective-permute-start.6) | collective-permute-done | bytes 262176 | tf_op jit(solution)/shard_map/ppermute | solution.py:166
  90.3 3.3 %collective-permute-done.4.refs_2_ = bf16[2,4,2,64,384]{4,3,2,1,0:T(8,128)(2,1)} collective-permute-done((bf16[2,4,2,64,384]{4,3,2,1,0:T(8,128)(2,1)}, bf16[2,4,2,64,384]{4,3,2,1,0:T(8,128)(2,1)}, u32[]{:S(2)}, u32[]{:S(2)}) %collective-permute-start.4) | collective-permute-done | bytes 786464 | tf_op jit(solution)/shard_map/ppermute | solution.py:171
  93.7 1.6 copy-done.1
  95.2 7.1 %attend.1 = bf16[8,256,128]{2,1,0:T(8,128)(2,1)} custom-call(s32[2]{0:T(128)S(1)} %pad_add_fusion.1.place_ref, bf16[256,4096]{1,0:T(8,128)(2,1)S(1)} %copy-done.1, bf16[256,4096]{1,0:T(8,128)(2,1)} %collective-permute-done.other_ref, bf16[2,4,2,64,384]{4,3,2,1,0:T(8,128)(2,1)S(1)} %bitcast.17, bf16[2,4,2,64,384]{4,3,2,1,0:T(8,128)(2,1)} %collective-permute-done.3.refs_1_, ...), custom_call_target="tpu_custom_call" | custom-call | flops 1610612736 | bytes 8388608 | tf_op jit(solution)/shard_map/attend/pallas_call | solution.py:174
  102.4 4.7 %all-to-all-start.2 = ((bf16[8,256,128]{2,1,0:T(8,128)(2,1)}), bf16[8,256,128]{2,1,0:T(8,128)(2,1)S(1)}, u32[]{:S(2)}, u32[]{:S(2)}) async-start(bf16[8,256,128]{2,1,0:T(8,128)(2,1)} %attend.1), calls=%async_computation.2 | async-start | bytes 1048576 | tf_op jit(solution)/shard_map/all_to_all | solution.py:185
  107.1 1.2 pad_maximum_fusion.held_ref
  108.3 2.4 %collective-permute-start.7 = (bf16[3,128,1024]{2,1,0:T(8,128)(2,1)S(1)}, bf16[3,128,1024]{2,1,0:T(8,128)(2,1)S(1)}, u32[]{:S(2)}, u32[]{:S(2)}) collective-permute-start(bf16[3,128,1024]{2,1,0:T(8,128)(2,1)S(1)} %pad_maximum_fusion.held_ref), channel_id=1, source_target_pairs={{0,8},{8,0},{1,9},{9,1},{2,10},{10,2},{3,11},{11,3},{4,12},{12,4},... | collective-permute-start | bytes 2359304 | tf_op jit(solution)/shard_map/ppermute | solution.py:184
  110.7 1.9 %collective-permute-done.7.partner_ref = bf16[3,128,1024]{2,1,0:T(8,128)(2,1)S(1)} collective-permute-done((bf16[3,128,1024]{2,1,0:T(8,128)(2,1)S(1)}, bf16[3,128,1024]{2,1,0:T(8,128)(2,1)S(1)}, u32[]{:S(2)}, u32[]{:S(2)}) %collective-permute-start.7) | collective-permute-done | bytes 786464 | tf_op jit(solution)/shard_map/ppermute | solution.py:184
  113.5 8.5 %all-to-all-done.2 = bf16[8,256,128]{2,1,0:T(8,128)(2,1)S(1)} async-done(((bf16[8,256,128]{2,1,0:T(8,128)(2,1)}), bf16[8,256,128]{2,1,0:T(8,128)(2,1)S(1)}, u32[]{:S(2)}, u32[]{:S(2)}) %all-to-all-start.2) | async-done | bytes 524320 | tf_op jit(solution)/shard_map/all_to_all | solution.py:185
  123.1 1.5 project.1
  124.6 37.1 %all_to_all.21 = bf16[8,32,1024]{2,1,0:T(8,128)(2,1)} all-to-all(bf16[8,32,1024]{2,1,0:T(8,128)(2,1)S(1)} %bitcast.19), channel_id=1, replica_groups=mesh['zh'=2,'x'=4,'y'=8,'c'=2,'rg'=2,'cb'=4] {'rg','cb'}, dimensions={0} | all-to-all | bytes 1048576 | tf_op jit(solution)/shard_map/all_to_all | solution.py:198
  161.7 1.8 %add.18 = bf16[32,4096]{1,0:T(8,128)(2,1)} custom-call(bf16[2,4,32,1024]{3,2,1,0:T(8,128)(2,1)} %bitcast.24), custom_call_target="tpu_custom_call" | custom-call | tf_op jit(solution)/shard_map/add/pallas_call | solution.py:199
  (24 shorter events, 5.1 us)
Async XLA Ops:
  0.0 47.7 %copy-start = (bf16[256,4096]{1,0:T(8,128)(2,1)S(1)}, bf16[256,4096]{1,0:T(8,128)(2,1)}, u32[]{:S(2)}) copy-start(bf16[256,4096]{1,0:T(8,128)(2,1)} %w_ref.3) | copy-start | bytes 6291460
  35.6 29.9 %all-to-all-start.1 = ((bf16[8,4,32,384]{3,2,1,0:T(8,128)(2,1)}), bf16[8,4,32,384]{3,2,1,0:T(8,128)(2,1)S(1)}, u32[]{:S(2)}, u32[]{:S(2)}) async-start(bf16[8,4,32,384]{3,2,1,0:T(8,128)(2,1)} %broadcast_in_dim.15), calls=%async_computation.1 | async-start | bytes 1572864 | tf_op jit(solution)/shard_map/all_to_all | solution.py:63
  45.7 44.7 %collective-permute-start = (bf16[256,4096]{1,0:T(8,128)(2,1)}, bf16[256,4096]{1,0:T(8,128)(2,1)}, u32[]{:S(2)}, u32[]{:S(2)}) collective-permute-start(bf16[256,4096]{1,0:T(8,128)(2,1)} %own_ref.1), channel_id=1, source_target_pairs={{0,8},{8,0},{1,9},{9,1},{2,10},{10,2},{3,11},{11,3},{4,12},{12,4},... | collective-permute-start | bytes 6291464 | tf_op jit(solution)/shard_map/ppermute | solution.py:146
  49.0 17.3 %collective-permute-start.1 = (bf16[128,1024]{1,0:T(8,128)(2,1)}, bf16[128,1024]{1,0:T(8,128)(2,1)S(1)}, u32[]{:S(2)}, u32[]{:S(2)}) collective-permute-start(bf16[128,1024]{1,0:T(8,128)(2,1)} %get-tuple-element.8), channel_id=1, source_target_pairs={{0,1},{1,0},{2,3},{3,2},{4,5},{5,4},{6,7},{7,6},{8,9},{9,8},{10,11... | collective-permute-start | bytes 786440 | tf_op jit(solution)/shard_map/ppermute | solution.py:166
  51.0 17.5 %collective-permute-start.2 = (bf16[128,1024]{1,0:T(8,128)(2,1)}, bf16[128,1024]{1,0:T(8,128)(2,1)}, u32[]{:S(2)}, u32[]{:S(2)}) collective-permute-start(bf16[128,1024]{1,0:T(8,128)(2,1)} %get-tuple-element.9), channel_id=1, source_target_pairs={{0,2},{1,3},{2,0},{3,1},{4,6},{5,7},{6,4},{7,5},{8,10},{9,11},{10,... | collective-permute-start | bytes 786440 | tf_op jit(solution)/shard_map/ppermute | solution.py:166
  66.3 2.1 %copy-start.5 = (bf16[128,1024]{1,0:T(8,128)(2,1)}, bf16[128,1024]{1,0:T(8,128)(2,1)S(1)}, u32[]{:S(2)}) copy-start(bf16[128,1024]{1,0:T(8,128)(2,1)S(1)} %collective-permute-done.1.refs_1_) | copy-start | bytes 786436
  68.4 21.9 %collective-permute-start.3 = (bf16[2,4,2,64,384]{4,3,2,1,0:T(8,128)(2,1)}, bf16[2,4,2,64,384]{4,3,2,1,0:T(8,128)(2,1)}, u32[]{:S(2)}, u32[]{:S(2)}) collective-permute-start(bf16[2,4,2,64,384]{4,3,2,1,0:T(8,128)(2,1)} %bitcast.21), channel_id=1, source_target_pairs={{0,16},{8,120},{16,0},{24,40},{32,48},{40,24},{48,32},{56,72},{64,... | collective-permute-start | bytes 2359304 | tf_op jit(solution)/shard_map/ppermute | solution.py:171
  71.0 22.6 %collective-permute-start.4 = (bf16[2,4,2,64,384]{4,3,2,1,0:T(8,128)(2,1)}, bf16[2,4,2,64,384]{4,3,2,1,0:T(8,128)(2,1)}, u32[]{:S(2)}, u32[]{:S(2)}) collective-permute-start(bf16[2,4,2,64,384]{4,3,2,1,0:T(8,128)(2,1)} %bitcast.22), channel_id=1, source_target_pairs={{0,128},{8,392},{16,144},{24,408},{32,160},{40,424},{48,176},{56,4... | collective-permute-start | bytes 2359304 | tf_op jit(solution)/shard_map/ppermute | solution.py:171
  73.8 19.9 %collective-permute-start.5 = (bf16[2,4,2,64,384]{4,3,2,1,0:T(8,128)(2,1)}, bf16[2,4,2,64,384]{4,3,2,1,0:T(8,128)(2,1)}, u32[]{:S(2)}, u32[]{:S(2)}) collective-permute-start(bf16[2,4,2,64,384]{4,3,2,1,0:T(8,128)(2,1)} %bitcast.23), channel_id=1, source_target_pairs={{0,144},{8,504},{16,128},{24,424},{32,176},{40,408},{48,160},{56,4... | collective-permute-start | bytes 2359304 | tf_op jit(solution)/shard_map/ppermute | solution.py:171
  77.7 12.6 %collective-permute-start.6 = (bf16[128,1024]{1,0:T(8,128)(2,1)S(1)}, bf16[128,1024]{1,0:T(8,128)(2,1)S(1)}, u32[]{:S(2)}, u32[]{:S(2)}) collective-permute-start(bf16[128,1024]{1,0:T(8,128)(2,1)S(1)} %get-tuple-element.10), channel_id=1, source_target_pairs={{0,3},{1,2},{2,1},{3,0},{4,7},{5,6},{6,5},{7,4},{8,11},{9,10},{10,... | collective-permute-start | bytes 786440 | tf_op jit(solution)/shard_map/ppermute | solution.py:166
  90.3 12.0 %copy-start.2 = (bf16[128,1024]{1,0:T(8,128)(2,1)}, bf16[128,1024]{1,0:T(8,128)(2,1)S(1)}, u32[]{:S(2)}) copy-start(bf16[128,1024]{1,0:T(8,128)(2,1)S(1)} %collective-permute-done.6.refs_4_) | copy-start | bytes 786436
  93.7 1.6 copy-start.1
  102.4 19.6 %all-to-all-start.2 = ((bf16[8,256,128]{2,1,0:T(8,128)(2,1)}), bf16[8,256,128]{2,1,0:T(8,128)(2,1)S(1)}, u32[]{:S(2)}, u32[]{:S(2)}) async-start(bf16[8,256,128]{2,1,0:T(8,128)(2,1)} %attend.1), calls=%async_computation.2 | async-start | bytes 1048576 | tf_op jit(solution)/shard_map/all_to_all | solution.py:185
  108.3 4.3 %collective-permute-start.7 = (bf16[3,128,1024]{2,1,0:T(8,128)(2,1)S(1)}, bf16[3,128,1024]{2,1,0:T(8,128)(2,1)S(1)}, u32[]{:S(2)}, u32[]{:S(2)}) collective-permute-start(bf16[3,128,1024]{2,1,0:T(8,128)(2,1)S(1)} %pad_maximum_fusion.held_ref), channel_id=1, source_target_pairs={{0,8},{8,0},{1,9},{9,1},{2,10},{10,2},{3,11},{11,3},{4,12},{12,4},... | collective-permute-start | bytes 2359304 | tf_op jit(solution)/shard_map/ppermute | solution.py:184
  112.6 0.9 copy-start.3
  121.9 1.1 copy-start.4

commit v10 on v7

--- a/solution.py
+++ b/solution.py
@@ -63,8 +63,15 @@
     return lax.all_to_all(blocks, DP, 0, 0, axis_index_groups=groups, tiled=True)
 
 
+def cut_kernel(w_ref, out_ref):
+    for i in range(out_ref.shape[0]):
+        c = i % C
+        for part in range(3):
+            out_ref[i, :, part * HD : (part + 1) * HD] = w_ref[part, :, c * HD : (c + 1) * HD]
+
+
 def attend_kernel(place_ref, own_ref, other_ref, *refs):
-    w_refs, (out_ref, held_ref, sems) = refs[:4], refs[5:]
+    w_refs, (out_ref, held_ref, sems) = refs[:4], refs[6:]
     me, core = place_ref[0], place_ref[1]
     for i, w_ref in enumerate(w_refs):
         pltpu.make_async_copy(w_ref, held_ref.at[me ^ i], sems.at[i]).start()
@@ -126,8 +133,13 @@
     k_rows = qkv_weight.shape[0]
     other = lax.ppermute(tokens, "c", [(0, 1), (1, 0)])
 
-    heads = qkv_weight.reshape(k_rows, 3, C, HD).transpose(2, 0, 1, 3).reshape(C, k_rows, 3 * HD)
-    heads = jnp.broadcast_to(heads[None], (ZH,) + heads.shape).reshape(ZH * C, k_rows, 3 * HD)
+    heads = pl.pallas_call(
+        cut_kernel,
+        out_shape=jax.ShapeDtypeStruct((ZH * C, k_rows, 3 * HD), jnp.bfloat16),
+        in_specs=[pl.BlockSpec(memory_space=pltpu.VMEM)],
+        out_specs=pl.BlockSpec(memory_space=pltpu.VMEM),
+        name="cut",
+    )(qkv_weight.transpose(1, 0, 2))
     heads = lax.all_to_all(heads, ("zh", "c"), 0, 0, tiled=True)
     first = heads
     heads = spread(heads, FAR)
@@ -147,19 +159,19 @@
     )(jnp.stack([column, core]), out_weight, first)
     held = [lax.ppermute(block, "cb", [(j, j ^ (i + 1)) for j in range(CB)]) for i, block in enumerate(sent)]
 
-    heads = behind(heads, held[:2]).reshape(XQ, YQ, ZH, C * k_rows, 3 * HD)
+    heads = behind(heads, held[1:2]).reshape(XQ, YQ, ZH, C * k_rows, 3 * HD)
     squares = [heads] + [lax.ppermute(heads, DP, pairs) for pairs in NEAR]
     parity = lax.axis_index("x") % 2 * 2 + lax.axis_index("y") % 2
 
     mixed = pl.pallas_call(
         attend_kernel,
         out_shape=jax.ShapeDtypeStruct((C * CB, rows, HD), jnp.bfloat16),
-        in_specs=[smem] + [vmem] * 2 + [ANYWHERE] * 5,
+        in_specs=[smem] + [vmem] * 2 + [ANYWHERE] * 6,
         scratch_shapes=[pltpu.VMEM((4,) + heads.shape, jnp.bfloat16), pltpu.SemaphoreType.DMA((4,))],
         compiler_params=pltpu.CompilerParams(vmem_limit_bytes=48 << 20),
         cost_estimate=pl.CostEstimate(flops=2 * 2 * rows * width * 3 * HD, bytes_accessed=8 << 20, transcendentals=0),
         name="attend",
-    )(jnp.stack([parity, core]), tokens, other, *squares, held[2])
+    )(jnp.stack([parity, core]), tokens, other, *squares, held[0], held[2])
     held = jnp.stack(held)
     partner = lax.ppermute(held, "c", [(0, 1), (1, 0)])
     mixed = lax.all_to_all(mixed, ("c", "cb"), 0, 0, tiled=True).reshape(C, CB, rows, HD)

time: 162 us -> 170 us (1.049)
  waiting for transfers between devices: 36.4 us -> 42.2 us
    ppermute x3, waiting for transfers between devices: 21.6 us -> 29.8 us  [body(): lax.ppermute(block, 'cb', [(j, j ^ i + 1) for j in range(CB)])]
    ppermute x3, waiting for transfers between devices: 3.33 us -> 0.01 us  [body(): squares = [heads] + [lax.ppermute(heads, DP, pairs) for pairs in NEAR]]
    unnamed x16 -> x18, local copies, waits for them, and re-layouts: 2.85 us -> 4.89 us
  transfers between devices with their start and end apart: 10 -> 10, of which waited for: 6 -> 5; matrix products, arithmetic and copies ran while one was open for 1% -> 0% of each run, Pallas kernels for 0% -> 0%
where the time goes in v10:
time: 170 us; the launch traced here: 168 us
  blocking collectives  69.2 us (41%)
  waiting for transfers between devices  42.2 us (25%)
  starting transfers between devices  39.5 us (23%)
  Pallas kernels  9.86 us (6%)
  local copies, waits for them, and re-layouts  6.59 us (4%)
    all_to_all x1, blocking collectives, body(): lax.all_to_all(summed.reshape(RG * CB, part, columns), MP, 0, 0, tiled=True)  35.5 us
    all_to_all x1, blocking collectives, body(): heads = lax.all_to_all(heads, ('zh', 'c'), 0, 0, tiled=True)  33.7 us
    ppermute x3, waiting for transfers between devices, body(): lax.ppermute(block, 'cb', [(j, j ^ i + 1) for j in range(CB)])  29.8 us
    all_to_all x1, waiting for transfers between devices, body(): lax.all_to_all(mixed, ('c', 'cb'), 0, 0, tiled=True)  10.5 us
    all_to_all x1, starting transfers between devices, spread(): lax.all_to_all(blocks, DP, 0, 0, axis_index_groups=groups, tiled=True)  10.1 us
    ppermute x3, starting transfers between devices, body(): lax.ppermute(block, 'cb', [(j, j ^ i + 1) for j in range(CB)])  9.75 us
    ppermute x3, starting transfers between devices, body(): squares = [heads] + [lax.ppermute(heads, DP, pairs) for pairs in NEAR]  9.2 us
    pallas_call x1, Pallas kernels, body(): pl.pallas_call(attend_kernel, out_shape=jax.ShapeDtypeStruct((C * CB, row...  6.33 us
  transfers between devices with their start and end apart: 10, of which 5 were waited for; matrix products, arithmetic and copies ran while one was open for 0% of the time, Pallas kernels for 0%

profile of v10, /device:TPU:6, one launch (start us, length us, event | category | flops | bytes accessed | tf_op | source)
XLA Modules:
  0.0 167.9 jit_solution(3242906806828846798)
XLA Ops:
  0.0 1.6 cut.1
  1.6 33.7 %all_to_all.20.after_ref = bf16[4,32,384]{2,1,0:T(8,128)(2,1)S(1)} all-to-all(bf16[4,32,384]{2,1,0:T(8,128)(2,1)} %cut.1), channel_id=1, replica_groups=mesh['zh'=2,'x'=4,'y'=8,'c'=2,'rg'=2,'cb'=4] {'zh','c'}, dimensions={0} | all-to-all | bytes 196608 | tf_op jit(solution)/shard_map/all_to_all | solution.py:143
  35.3 1.0 broadcast_in_dim.2
  36.3 10.1 %all-to-all-start.1 = ((bf16[8,4,32,384]{3,2,1,0:T(8,128)(2,1)}), bf16[8,4,32,384]{3,2,1,0:T(8,128)(2,1)S(1)}, u32[]{:S(2)}, u32[]{:S(2)}) async-start(bf16[8,4,32,384]{3,2,1,0:T(8,128)(2,1)} %broadcast_in_dim.2), calls=%async_computation.1 | async-start | bytes 1572864 | tf_op jit(solution)/shard_map/all_to_all | solution.py:63
  46.4 1.9 %collective-permute-start = (bf16[256,4096]{1,0:T(8,128)(2,1)}, bf16[256,4096]{1,0:T(8,128)(2,1)}, u32[]{:S(2)}, u32[]{:S(2)}) collective-permute-start(bf16[256,4096]{1,0:T(8,128)(2,1)} %own_ref.1), channel_id=1, source_target_pairs={{0,8},{8,0},{1,9},{9,1},{2,10},{10,2},{3,11},{11,3},{4,12},{12,4},... | collective-permute-start | bytes 6291464 | tf_op jit(solution)/shard_map/ppermute | solution.py:134
  49.0 0.8 copy-done.3
  51.2 3.2 %collective-permute-start.1 = (bf16[128,1024]{1,0:T(8,128)(2,1)S(1)}, bf16[128,1024]{1,0:T(8,128)(2,1)S(1)}, u32[]{:S(2)}, u32[]{:S(2)}) collective-permute-start(bf16[128,1024]{1,0:T(8,128)(2,1)S(1)} %get-tuple-element.9), channel_id=1, source_target_pairs={{0,2},{1,3},{2,0},{3,1},{4,6},{5,7},{6,4},{7,5},{8,10},{9,11},{10,... | collective-permute-start | bytes 786440 | tf_op jit(solution)/shard_map/ppermute | solution.py:160
  54.4 12.8 %collective-permute-done.1.refs_1_ = bf16[128,1024]{1,0:T(8,128)(2,1)S(1)} collective-permute-done((bf16[128,1024]{1,0:T(8,128)(2,1)S(1)}, bf16[128,1024]{1,0:T(8,128)(2,1)S(1)}, u32[]{:S(2)}, u32[]{:S(2)}) %collective-permute-start.1) | collective-permute-done | bytes 262176 | tf_op jit(solution)/shard_map/ppermute | solution.py:160
  67.9 0.9 copy-done
  68.8 2.6 %collective-permute-start.2 = (bf16[2,4,2,64,384]{4,3,2,1,0:T(8,128)(2,1)}, bf16[2,4,2,64,384]{4,3,2,1,0:T(8,128)(2,1)S(1)}, u32[]{:S(2)}, u32[]{:S(2)}) collective-permute-start(bf16[2,4,2,64,384]{4,3,2,1,0:T(8,128)(2,1)} %bitcast.14), channel_id=1, source_target_pairs={{0,16},{8,120},{16,0},{24,40},{32,48},{40,24},{48,32},{56,72},{64,... | collective-permute-start | bytes 2359304 | tf_op jit(solution)/shard_map/ppermute | solution.py:163
  71.4 2.7 %collective-permute-start.3 = (bf16[2,4,2,64,384]{4,3,2,1,0:T(8,128)(2,1)}, bf16[2,4,2,64,384]{4,3,2,1,0:T(8,128)(2,1)S(1)}, u32[]{:S(2)}, u32[]{:S(2)}) collective-permute-start(bf16[2,4,2,64,384]{4,3,2,1,0:T(8,128)(2,1)} %bitcast.15), channel_id=1, source_target_pairs={{0,128},{8,392},{16,144},{24,408},{32,160},{40,424},{48,176},{56,4... | collective-permute-start | bytes 2359304 | tf_op jit(solution)/shard_map/ppermute | solution.py:163
  74.1 3.9 %collective-permute-start.4 = (bf16[2,4,2,64,384]{4,3,2,1,0:T(8,128)(2,1)}, bf16[2,4,2,64,384]{4,3,2,1,0:T(8,128)(2,1)S(1)}, u32[]{:S(2)}, u32[]{:S(2)}) collective-permute-start(bf16[2,4,2,64,384]{4,3,2,1,0:T(8,128)(2,1)} %bitcast.16), channel_id=1, source_target_pairs={{0,144},{8,504},{16,128},{24,424},{32,176},{40,408},{48,160},{56,4... | collective-permute-start | bytes 2359304 | tf_op jit(solution)/shard_map/ppermute | solution.py:163
  78.0 1.9 %collective-permute-start.5 = (bf16[128,1024]{1,0:T(8,128)(2,1)}, bf16[128,1024]{1,0:T(8,128)(2,1)S(1)}, u32[]{:S(2)}, u32[]{:S(2)}) collective-permute-start(bf16[128,1024]{1,0:T(8,128)(2,1)} %copy-done.6), channel_id=1, source_target_pairs={{0,1},{1,0},{2,3},{3,2},{4,5},{5,4},{6,7},{7,6},{8,9},{9,8},{10,11... | collective-permute-start | bytes 786440 | tf_op jit(solution)/shard_map/ppermute | solution.py:160
  80.0 8.7 %collective-permute-done.5.refs_4_ = bf16[128,1024]{1,0:T(8,128)(2,1)S(1)} collective-permute-done((bf16[128,1024]{1,0:T(8,128)(2,1)}, bf16[128,1024]{1,0:T(8,128)(2,1)S(1)}, u32[]{:S(2)}, u32[]{:S(2)}) %collective-permute-start.5) | collective-permute-done | bytes 262176 | tf_op jit(solution)/shard_map/ppermute | solution.py:160
  88.7 4.6 %collective-permute-start.6 = (bf16[128,1024]{1,0:T(8,128)(2,1)}, bf16[128,1024]{1,0:T(8,128)(2,1)S(1)}, u32[]{:S(2)}, u32[]{:S(2)}) collective-permute-start(bf16[128,1024]{1,0:T(8,128)(2,1)} %copy-done.5), channel_id=1, source_target_pairs={{0,3},{1,2},{2,1},{3,0},{4,7},{5,6},{6,5},{7,4},{8,11},{9,10},{10,... | collective-permute-start | bytes 786440 | tf_op jit(solution)/shard_map/ppermute | solution.py:160
  93.4 8.3 %collective-permute-done.6.refs_5_ = bf16[128,1024]{1,0:T(8,128)(2,1)S(1)} collective-permute-done((bf16[128,1024]{1,0:T(8,128)(2,1)}, bf16[128,1024]{1,0:T(8,128)(2,1)S(1)}, u32[]{:S(2)}, u32[]{:S(2)}) %collective-permute-start.6) | collective-permute-done | bytes 262176 | tf_op jit(solution)/shard_map/ppermute | solution.py:160
  101.7 1.1 copy-done.1
  102.8 6.3 %attend.1 = bf16[8,256,128]{2,1,0:T(8,128)(2,1)} custom-call(s32[2]{0:T(128)S(1)} %pad_add_fusion.1.place_ref, bf16[256,4096]{1,0:T(8,128)(2,1)} %own_ref.1, bf16[256,4096]{1,0:T(8,128)(2,1)} %collective-permute-done.other_ref, bf16[2,4,2,64,384]{4,3,2,1,0:T(8,128)(2,1)S(1)} %bitcast.17, bf16[2,4,2,64,384]{4,3,2,1,0:T(8,128)(2,1)S(1)} %collective-permute-done.2.refs_1_, ...), custom_call_target="tpu_custom_call" | custom-call | flops 1610612736 | bytes 8388608 | tf_op jit(solution)/shard_map/attend/pallas_call | solution.py:166
  109.2 6.2 %all-to-all-start.2 = ((bf16[8,256,128]{2,1,0:T(8,128)(2,1)}), bf16[8,256,128]{2,1,0:T(8,128)(2,1)S(1)}, u32[]{:S(2)}, u32[]{:S(2)}) async-start(bf16[8,256,128]{2,1,0:T(8,128)(2,1)} %attend.1), calls=%async_computation.2 | async-start | bytes 1048576 | tf_op jit(solution)/shard_map/all_to_all | solution.py:177
  115.5 2.4 %collective-permute-start.7 = (bf16[3,128,1024]{2,1,0:T(8,128)(2,1)S(1)}, bf16[3,128,1024]{2,1,0:T(8,128)(2,1)S(1)}, u32[]{:S(2)}, u32[]{:S(2)}) collective-permute-start(bf16[3,128,1024]{2,1,0:T(8,128)(2,1)S(1)} %pad_maximum_fusion.held_ref), channel_id=1, source_target_pairs={{0,8},{8,0},{1,9},{9,1},{2,10},{10,2},{3,11},{11,3},{4,12},{12,4},... | collective-permute-start | bytes 2359304 | tf_op jit(solution)/shard_map/ppermute | solution.py:176
  117.9 1.9 %collective-permute-done.7.partner_ref = bf16[3,128,1024]{2,1,0:T(8,128)(2,1)S(1)} collective-permute-done((bf16[3,128,1024]{2,1,0:T(8,128)(2,1)S(1)}, bf16[3,128,1024]{2,1,0:T(8,128)(2,1)S(1)}, u32[]{:S(2)}, u32[]{:S(2)}) %collective-permute-start.7) | collective-permute-done | bytes 786464 | tf_op jit(solution)/shard_map/ppermute | solution.py:176
  119.8 10.5 %all-to-all-done.2 = bf16[8,256,128]{2,1,0:T(8,128)(2,1)S(1)} async-done(((bf16[8,256,128]{2,1,0:T(8,128)(2,1)}), bf16[8,256,128]{2,1,0:T(8,128)(2,1)S(1)}, u32[]{:S(2)}, u32[]{:S(2)}) %all-to-all-start.2) | async-done | bytes 524320 | tf_op jit(solution)/shard_map/all_to_all | solution.py:177
  130.2 1.3 project.1
  131.5 35.5 %all_to_all.21 = bf16[8,32,1024]{2,1,0:T(8,128)(2,1)S(1)} all-to-all(bf16[8,32,1024]{2,1,0:T(8,128)(2,1)S(1)} %bitcast.19), channel_id=1, replica_groups=mesh['zh'=2,'x'=4,'y'=8,'c'=2,'rg'=2,'cb'=4] {'rg','cb'}, dimensions={0} | all-to-all | bytes 1048576 | tf_op jit(solution)/shard_map/all_to_all | solution.py:189
  (28 shorter events, 3.9 us)
Async XLA Ops:
  0.0 48.4 %copy-start.2 = (bf16[256,4096]{1,0:T(8,128)(2,1)S(1)}, bf16[256,4096]{1,0:T(8,128)(2,1)}, u32[]{:S(2)}) copy-start(bf16[256,4096]{1,0:T(8,128)(2,1)} %w_ref.1) | copy-start | bytes 6291460
  36.3 30.9 %all-to-all-start.1 = ((bf16[8,4,32,384]{3,2,1,0:T(8,128)(2,1)}), bf16[8,4,32,384]{3,2,1,0:T(8,128)(2,1)S(1)}, u32[]{:S(2)}, u32[]{:S(2)}) async-start(bf16[8,4,32,384]{3,2,1,0:T(8,128)(2,1)} %broadcast_in_dim.2), calls=%async_computation.1 | async-start | bytes 1572864 | tf_op jit(solution)/shard_map/all_to_all | solution.py:63
  46.4 55.3 %collective-permute-start = (bf16[256,4096]{1,0:T(8,128)(2,1)}, bf16[256,4096]{1,0:T(8,128)(2,1)}, u32[]{:S(2)}, u32[]{:S(2)}) collective-permute-start(bf16[256,4096]{1,0:T(8,128)(2,1)} %own_ref.1), channel_id=1, source_target_pairs={{0,8},{8,0},{1,9},{9,1},{2,10},{10,2},{3,11},{11,3},{4,12},{12,4},... | collective-permute-start | bytes 6291464 | tf_op jit(solution)/shard_map/ppermute | solution.py:134
  49.0 0.8 copy-start.3
  49.8 0.7 copy-start.5
  50.5 0.7 copy-start.6
  51.2 16.0 %collective-permute-start.1 = (bf16[128,1024]{1,0:T(8,128)(2,1)S(1)}, bf16[128,1024]{1,0:T(8,128)(2,1)S(1)}, u32[]{:S(2)}, u32[]{:S(2)}) collective-permute-start(bf16[128,1024]{1,0:T(8,128)(2,1)S(1)} %get-tuple-element.9), channel_id=1, source_target_pairs={{0,2},{1,3},{2,0},{3,1},{4,6},{5,7},{6,4},{7,5},{8,10},{9,11},{10,... | collective-permute-start | bytes 786440 | tf_op jit(solution)/shard_map/ppermute | solution.py:160
  67.2 0.7 copy-start.7
  67.9 0.9 copy-start
  68.8 32.8 %collective-permute-start.2 = (bf16[2,4,2,64,384]{4,3,2,1,0:T(8,128)(2,1)}, bf16[2,4,2,64,384]{4,3,2,1,0:T(8,128)(2,1)S(1)}, u32[]{:S(2)}, u32[]{:S(2)}) collective-permute-start(bf16[2,4,2,64,384]{4,3,2,1,0:T(8,128)(2,1)} %bitcast.14), channel_id=1, source_target_pairs={{0,16},{8,120},{16,0},{24,40},{32,48},{40,24},{48,32},{56,72},{64,... | collective-permute-start | bytes 2359304 | tf_op jit(solution)/shard_map/ppermute | solution.py:163
  71.4 30.3 %collective-permute-start.3 = (bf16[2,4,2,64,384]{4,3,2,1,0:T(8,128)(2,1)}, bf16[2,4,2,64,384]{4,3,2,1,0:T(8,128)(2,1)S(1)}, u32[]{:S(2)}, u32[]{:S(2)}) collective-permute-start(bf16[2,4,2,64,384]{4,3,2,1,0:T(8,128)(2,1)} %bitcast.15), channel_id=1, source_target_pairs={{0,128},{8,392},{16,144},{24,408},{32,160},{40,424},{48,176},{56,4... | collective-permute-start | bytes 2359304 | tf_op jit(solution)/shard_map/ppermute | solution.py:163
  74.1 27.5 %collective-permute-start.4 = (bf16[2,4,2,64,384]{4,3,2,1,0:T(8,128)(2,1)}, bf16[2,4,2,64,384]{4,3,2,1,0:T(8,128)(2,1)S(1)}, u32[]{:S(2)}, u32[]{:S(2)}) collective-permute-start(bf16[2,4,2,64,384]{4,3,2,1,0:T(8,128)(2,1)} %bitcast.16), channel_id=1, source_target_pairs={{0,144},{8,504},{16,128},{24,424},{32,176},{40,408},{48,160},{56,4... | collective-permute-start | bytes 2359304 | tf_op jit(solution)/shard_map/ppermute | solution.py:163
  78.0 10.6 %collective-permute-start.5 = (bf16[128,1024]{1,0:T(8,128)(2,1)}, bf16[128,1024]{1,0:T(8,128)(2,1)S(1)}, u32[]{:S(2)}, u32[]{:S(2)}) collective-permute-start(bf16[128,1024]{1,0:T(8,128)(2,1)} %copy-done.6), channel_id=1, source_target_pairs={{0,1},{1,0},{2,3},{3,2},{4,5},{5,4},{6,7},{7,6},{8,9},{9,8},{10,11... | collective-permute-start | bytes 786440 | tf_op jit(solution)/shard_map/ppermute | solution.py:160
  88.7 13.0 %collective-permute-start.6 = (bf16[128,1024]{1,0:T(8,128)(2,1)}, bf16[128,1024]{1,0:T(8,128)(2,1)S(1)}, u32[]{:S(2)}, u32[]{:S(2)}) collective-permute-start(bf16[128,1024]{1,0:T(8,128)(2,1)} %copy-done.5), channel_id=1, source_target_pairs={{0,3},{1,2},{2,1},{3,0},{4,7},{5,6},{6,5},{7,4},{8,11},{9,10},{10,... | collective-permute-start | bytes 786440 | tf_op jit(solution)/shard_map/ppermute | solution.py:160
  101.7 1.1 copy-start.1
  102.8 12.6 %copy-start.8 = (bf16[128,1024]{1,0:T(8,128)(2,1)S(1)}, bf16[128,1024]{1,0:T(8,128)(2,1)}, u32[]{:S(2)}) copy-start(bf16[128,1024]{1,0:T(8,128)(2,1)} %copy-done.7) | copy-start | bytes 786436
  109.1 21.1 %copy-start.4 = (bf16[256,1024]{1,0:T(8,128)(2,1)S(1)}, bf16[256,1024]{1,0:T(8,128)(2,1)}, u32[]{:S(2)}) copy-start(bf16[256,1024]{1,0:T(8,128)(2,1)} %copy-done.3) | copy-start | bytes 1572868
  109.2 21.1 %all-to-all-start.2 = ((bf16[8,256,128]{2,1,0:T(8,128)(2,1)}), bf16[8,256,128]{2,1,0:T(8,128)(2,1)S(1)}, u32[]{:S(2)}, u32[]{:S(2)}) async-start(bf16[8,256,128]{2,1,0:T(8,128)(2,1)} %attend.1), calls=%async_computation.2 | async-start | bytes 1048576 | tf_op jit(solution)/shard_map/all_to_all | solution.py:177
  115.5 4.3 %collective-permute-start.7 = (bf16[3,128,1024]{2,1,0:T(8,128)(2,1)S(1)}, bf16[3,128,1024]{2,1,0:T(8,128)(2,1)S(1)}, u32[]{:S(2)}, u32[]{:S(2)}) collective-permute-start(bf16[3,128,1024]{2,1,0:T(8,128)(2,1)S(1)} %pad_maximum_fusion.held_ref), channel_id=1, source_target_pairs={{0,8},{8,0},{1,9},{9,1},{2,10},{10,2},{3,11},{11,3},{4,12},{12,4},... | collective-permute-start | bytes 2359304 | tf_op jit(solution)/shard_map/ppermute | solution.py:176

commit v11 on v7

--- a/solution.py
+++ b/solution.py
@@ -63,27 +63,35 @@
     return lax.all_to_all(blocks, DP, 0, 0, axis_index_groups=groups, tiled=True)
 
 
-def attend_kernel(place_ref, own_ref, other_ref, *refs):
-    w_refs, (out_ref, held_ref, sems) = refs[:4], refs[5:]
-    me, core = place_ref[0], place_ref[1]
-    for i, w_ref in enumerate(w_refs):
-        pltpu.make_async_copy(w_ref, held_ref.at[me ^ i], sems.at[i]).start()
+def half_sum(px, even, token_refs, w_refs, held_ref, sems):
+    moves = [pltpu.make_async_copy(w_refs[i], held_ref.at[even ^ i], sems.at[i]) for i in range(2)]
+    for move in moves:
+        move.start()
+    for move in moves:
+        move.wait()
     span = Y * held_ref.shape[4]
     totals = [None, None]
-    for px in range(2):
-        for slot in (2 * px, 2 * px + 1):
-            pltpu.make_async_copy(w_refs[0], held_ref.at[slot], sems.at[me ^ slot]).wait()
-        for zh in range(ZH):
-            for xq in range(XQ):
-                weight = jnp.concatenate(
-                    [held_ref[2 * px + y % 2, xq, y // 2, zh] for y in range(Y)], axis=0
-                )
-                start = (zh * X + 2 * xq + px) * span
-                for g, ref in enumerate((own_ref, other_ref)):
-                    product = jnp.dot(
-                        ref[:, start : start + span], weight, preferred_element_type=jnp.float32
-                    )
-                    totals[g] = product if totals[g] is None else totals[g] + product
+    for zh in range(ZH):
+        for xq in range(XQ):
+            weight = jnp.concatenate([held_ref[y % 2, xq, y // 2, zh] for y in range(Y)], axis=0)
+            start = pl.multiple_of((zh * X + 2 * xq + px) * span, span)
+            for g, ref in enumerate(token_refs):
+                product = jnp.dot(ref[:, pl.ds(start, span)], weight, preferred_element_type=jnp.float32)
+                totals[g] = product if totals[g] is None else totals[g] + product
+    return totals
+
+
+def half_kernel(place_ref, own_ref, other_ref, w0_ref, w1_ref, out_ref, held_ref, sems):
+    me = place_ref[0]
+    totals = half_sum(me // 2, me % 2, (own_ref, other_ref), (w0_ref, w1_ref), held_ref, sems)
+    for g in range(2):
+        out_ref[g] = totals[g]
+
+
+def attend_kernel(place_ref, own_ref, other_ref, half_ref, w0_ref, w1_ref, after_ref, out_ref, held_ref, sems):
+    me, core = place_ref[0], place_ref[1]
+    totals = half_sum(1 - me // 2, me % 2, (own_ref, other_ref), (w0_ref, w1_ref), held_ref, sems)
+    totals = [totals[g] + half_ref[g] for g in range(2)]
     for g in range(2):
         projected = totals[g].astype(jnp.bfloat16)
         queries, key_rows, values = (projected[:, i * HD : (i + 1) * HD] for i in range(3))
@@ -151,15 +159,29 @@
     squares = [heads] + [lax.ppermute(heads, DP, pairs) for pairs in NEAR]
     parity = lax.axis_index("x") % 2 * 2 + lax.axis_index("y") % 2
 
+    spot = jnp.stack([parity, core])
+    scratch = [pltpu.VMEM((2,) + heads.shape, jnp.bfloat16), pltpu.SemaphoreType.DMA((2,))]
+    work = pl.CostEstimate(flops=2 * rows * width * 3 * HD, bytes_accessed=6 << 20, transcendentals=0)
+    half = pl.pallas_call(
+        half_kernel,
+        out_shape=jax.ShapeDtypeStruct((2, rows, 3 * HD), jnp.float32),
+        in_specs=[smem] + [vmem] * 2 + [ANYWHERE] * 2,
+        out_specs=vmem,
+        scratch_shapes=scratch,
+        compiler_params=pltpu.CompilerParams(vmem_limit_bytes=32 << 20),
+        cost_estimate=work,
+        name="half",
+    )(spot, tokens, other, squares[0], squares[1])
     mixed = pl.pallas_call(
         attend_kernel,
         out_shape=jax.ShapeDtypeStruct((C * CB, rows, HD), jnp.bfloat16),
-        in_specs=[smem] + [vmem] * 2 + [ANYWHERE] * 5,
-        scratch_shapes=[pltpu.VMEM((4,) + heads.shape, jnp.bfloat16), pltpu.SemaphoreType.DMA((4,))],
-        compiler_params=pltpu.CompilerParams(vmem_limit_bytes=48 << 20),
-        cost_estimate=pl.CostEstimate(flops=2 * 2 * rows * width * 3 * HD, bytes_accessed=8 << 20, transcendentals=0),
+        in_specs=[smem] + [vmem] * 3 + [ANYWHERE] * 3,
+        out_specs=vmem,
+        scratch_shapes=scratch,
+        compiler_params=pltpu.CompilerParams(vmem_limit_bytes=32 << 20),
+        cost_estimate=work,
         name="attend",
-    )(jnp.stack([parity, core]), tokens, other, *squares, held[2])
+    )(spot, tokens, other, half, squares[2], squares[3], held[2])
     held = jnp.stack(held)
     partner = lax.ppermute(held, "c", [(0, 1), (1, 0)])
     mixed = lax.all_to_all(mixed, ("c", "cb"), 0, 0, tiled=True).reshape(C, CB, rows, HD)

time: 162 us -> 161 us (level)
  waiting for transfers between devices: 36.4 us -> 31 us
  Pallas kernels: 8.92 us -> 11.4 us
    ppermute x3, waiting for transfers between devices: 21.6 us -> 15.9 us  [body(): lax.ppermute(block, 'cb', [(j, j ^ i + 1) for j in range(CB)])]
    pallas_call x0 -> x1, Pallas kernels: none -> 4.09 us  [body(): pl.pallas_call(half_kernel, out_shape=jax.ShapeDtypeStruct((2, rows, 3 *...]
    pallas_call x1, Pallas kernels: 6.99 us -> 5.36 us  [body(): pl.pallas_call(attend_kernel, out_shape=jax.ShapeDtypeStruct((C * CB, row...]
  transfers between devices with their start and end apart: 10 -> 10, of which waited for: 6 -> 7; matrix products, arithmetic and copies ran while one was open for 1% -> 1% of each run, Pallas kernels for 0% -> 3%
where the time goes in v11:
time: 161 us; the launch traced here: 160 us
  blocking collectives  70.5 us (44%)
  starting transfers between devices  38.5 us (24%)
  waiting for transfers between devices  31 us (19%)
  Pallas kernels  11.4 us (7%)
  local copies, waits for them, and re-layouts  7.21 us (4%)
    all_to_all x1, blocking collectives, body(): lax.all_to_all(summed.reshape(RG * CB, part, columns), MP, 0, 0, tiled=True)  37 us
    all_to_all x1, blocking collectives, body(): heads = lax.all_to_all(heads, ('zh', 'c'), 0, 0, tiled=True)  33.5 us
    ppermute x3, waiting for transfers between devices, body(): lax.ppermute(block, 'cb', [(j, j ^ i + 1) for j in range(CB)])  15.9 us
    ppermute x3, starting transfers between devices, body(): lax.ppermute(block, 'cb', [(j, j ^ i + 1) for j in range(CB)])  10.1 us
    all_to_all x1, starting transfers between devices, spread(): lax.all_to_all(blocks, DP, 0, 0, axis_index_groups=groups, tiled=True)  10.1 us
    all_to_all x1, waiting for transfers between devices, body(): lax.all_to_all(mixed, ('c', 'cb'), 0, 0, tiled=True)  9.53 us
    ppermute x3, starting transfers between devices, body(): squares = [heads] + [lax.ppermute(heads, DP, pairs) for pairs in NEAR]  9.2 us
    pallas_call x1, Pallas kernels, body(): pl.pallas_call(attend_kernel, out_shape=jax.ShapeDtypeStruct((C * CB, row...  5.36 us
  transfers between devices with their start and end apart: 10, of which 7 were waited for; matrix products, arithmetic and copies ran while one was open for 1% of the time, Pallas kernels for 3%

profile of v11, /device:TPU:6, one launch (start us, length us, event | category | flops | bytes accessed | tf_op | source)
XLA Modules:
  0.0 160.2 jit_solution(8001136479671022714)
XLA Ops:
  1.1 33.5 %all_to_all.20.after_ref = bf16[4,32,384]{2,1,0:T(8,128)(2,1)S(1)} all-to-all(bf16[4,32,384]{2,1,0:T(8,128)(2,1)S(1)} %bitcast.27), channel_id=1, replica_groups=mesh['zh'=2,'x'=4,'y'=8,'c'=2,'rg'=2,'cb'=4] {'zh','c'}, dimensions={0} | all-to-all | bytes 196608 | tf_op jit(solution)/shard_map/all_to_all | solution.py:139
  35.6 10.1 %all-to-all-start.1 = ((bf16[8,4,32,384]{3,2,1,0:T(8,128)(2,1)}), bf16[8,4,32,384]{3,2,1,0:T(8,128)(2,1)S(1)}, u32[]{:S(2)}, u32[]{:S(2)}) async-start(bf16[8,4,32,384]{3,2,1,0:T(8,128)(2,1)} %broadcast_in_dim.15), calls=%async_computation.1 | async-start | bytes 1572864 | tf_op jit(solution)/shard_map/all_to_all | solution.py:63
  45.6 1.9 %collective-permute-start = (bf16[256,4096]{1,0:T(8,128)(2,1)S(1)}, bf16[256,4096]{1,0:T(8,128)(2,1)}, u32[]{:S(2)}, u32[]{:S(2)}) collective-permute-start(bf16[256,4096]{1,0:T(8,128)(2,1)S(1)} %copy-done), channel_id=1, source_target_pairs={{0,8},{8,0},{1,9},{9,1},{2,10},{10,2},{3,11},{11,3},{4,12},{12,4},... | collective-permute-start | bytes 6291464 | tf_op jit(solution)/shard_map/ppermute | solution.py:135
  47.6 1.6 copy-done.3
  50.7 1.9 %collective-permute-start.1 = (bf16[128,1024]{1,0:T(8,128)(2,1)S(1)}, bf16[128,1024]{1,0:T(8,128)(2,1)S(1)}, u32[]{:S(2)}, u32[]{:S(2)}) collective-permute-start(bf16[128,1024]{1,0:T(8,128)(2,1)S(1)} %get-tuple-element.9), channel_id=1, source_target_pairs={{0,1},{1,0},{2,3},{3,2},{4,5},{5,4},{6,7},{7,6},{8,9},{9,8},{10,11... | collective-permute-start | bytes 786440 | tf_op jit(solution)/shard_map/ppermute | solution.py:156
  52.6 3.8 %collective-permute-start.2 = (bf16[128,1024]{1,0:T(8,128)(2,1)S(1)}, bf16[128,1024]{1,0:T(8,128)(2,1)}, u32[]{:S(2)}, u32[]{:S(2)}) collective-permute-start(bf16[128,1024]{1,0:T(8,128)(2,1)S(1)} %get-tuple-element.10), channel_id=1, source_target_pairs={{0,2},{1,3},{2,0},{3,1},{4,6},{5,7},{6,4},{7,5},{8,10},{9,11},{10,... | collective-permute-start | bytes 786440 | tf_op jit(solution)/shard_map/ppermute | solution.py:156
  56.4 8.5 %collective-permute-done.1.refs_1_ = bf16[128,1024]{1,0:T(8,128)(2,1)S(1)} collective-permute-done((bf16[128,1024]{1,0:T(8,128)(2,1)S(1)}, bf16[128,1024]{1,0:T(8,128)(2,1)S(1)}, u32[]{:S(2)}, u32[]{:S(2)}) %collective-permute-start.1) | collective-permute-done | bytes 262176 | tf_op jit(solution)/shard_map/ppermute | solution.py:156
  64.9 5.0 %collective-permute-done.2.refs_2_ = bf16[128,1024]{1,0:T(8,128)(2,1)} collective-permute-done((bf16[128,1024]{1,0:T(8,128)(2,1)S(1)}, bf16[128,1024]{1,0:T(8,128)(2,1)}, u32[]{:S(2)}, u32[]{:S(2)}) %collective-permute-start.2) | collective-permute-done | bytes 262176 | tf_op jit(solution)/shard_map/ppermute | solution.py:156
  70.8 2.6 %collective-permute-start.3 = (bf16[2,4,2,64,384]{4,3,2,1,0:T(8,128)(2,1)}, bf16[2,4,2,64,384]{4,3,2,1,0:T(8,128)(2,1)}, u32[]{:S(2)}, u32[]{:S(2)}) collective-permute-start(bf16[2,4,2,64,384]{4,3,2,1,0:T(8,128)(2,1)} %bitcast.19), channel_id=1, source_target_pairs={{0,16},{8,120},{16,0},{24,40},{32,48},{40,24},{48,32},{56,72},{64,... | collective-permute-start | bytes 2359304 | tf_op jit(solution)/shard_map/ppermute | solution.py:159
  73.4 2.7 %collective-permute-start.4 = (bf16[2,4,2,64,384]{4,3,2,1,0:T(8,128)(2,1)}, bf16[2,4,2,64,384]{4,3,2,1,0:T(8,128)(2,1)S(1)}, u32[]{:S(2)}, u32[]{:S(2)}) collective-permute-start(bf16[2,4,2,64,384]{4,3,2,1,0:T(8,128)(2,1)} %bitcast.20), channel_id=1, source_target_pairs={{0,128},{8,392},{16,144},{24,408},{32,160},{40,424},{48,176},{56,4... | collective-permute-start | bytes 2359304 | tf_op jit(solution)/shard_map/ppermute | solution.py:159
  76.1 3.9 %collective-permute-start.5 = (bf16[2,4,2,64,384]{4,3,2,1,0:T(8,128)(2,1)}, bf16[2,4,2,64,384]{4,3,2,1,0:T(8,128)(2,1)}, u32[]{:S(2)}, u32[]{:S(2)}) collective-permute-start(bf16[2,4,2,64,384]{4,3,2,1,0:T(8,128)(2,1)} %bitcast.21), channel_id=1, source_target_pairs={{0,144},{8,504},{16,128},{24,424},{32,176},{40,408},{48,160},{56,4... | collective-permute-start | bytes 2359304 | tf_op jit(solution)/shard_map/ppermute | solution.py:159
  80.0 4.4 %collective-permute-start.6 = (bf16[128,1024]{1,0:T(8,128)(2,1)S(1)}, bf16[128,1024]{1,0:T(8,128)(2,1)S(1)}, u32[]{:S(2)}, u32[]{:S(2)}) collective-permute-start(bf16[128,1024]{1,0:T(8,128)(2,1)S(1)} %get-tuple-element.11), channel_id=1, source_target_pairs={{0,3},{1,2},{2,1},{3,0},{4,7},{5,6},{6,5},{7,4},{8,11},{9,10},{10,... | collective-permute-start | bytes 786440 | tf_op jit(solution)/shard_map/ppermute | solution.py:156
  85.0 1.1 copy-done.2
  86.1 4.1 %half.1.half_ref = f32[2,256,384]{2,1,0:T(8,128)S(1)} custom-call(s32[2]{0:T(128)S(1)} %pad_add_fusion.1.place_ref, bf16[256,4096]{1,0:T(8,128)(2,1)S(1)} %copy-done, bf16[256,4096]{1,0:T(8,128)(2,1)} %collective-permute-done.other_ref, bf16[2,4,2,64,384]{4,3,2,1,0:T(8,128)(2,1)S(1)} %bitcast.22, bf16[2,4,2,64,384]{4,3,2,1,0:T(8,128)(2,1)} %collective-permute-done.3.w1_ref), custom_call_target="tpu_custom_call" | custom-call | flops 805306368 | bytes 6291456 | tf_op jit(solution)/shard_map/half/pallas_call | solution.py:165
  90.2 2.5 %collective-permute-done.6.after_ref = bf16[128,1024]{1,0:T(8,128)(2,1)S(1)} collective-permute-done((bf16[128,1024]{1,0:T(8,128)(2,1)S(1)}, bf16[128,1024]{1,0:T(8,128)(2,1)S(1)}, u32[]{:S(2)}, u32[]{:S(2)}) %collective-permute-start.6) | collective-permute-done | bytes 262176 | tf_op jit(solution)/shard_map/ppermute | solution.py:156
  92.7 3.2 %collective-permute-done.4.w0_ref = bf16[2,4,2,64,384]{4,3,2,1,0:T(8,128)(2,1)S(1)} collective-permute-done((bf16[2,4,2,64,384]{4,3,2,1,0:T(8,128)(2,1)}, bf16[2,4,2,64,384]{4,3,2,1,0:T(8,128)(2,1)S(1)}, u32[]{:S(2)}, u32[]{:S(2)}) %collective-permute-start.4) | collective-permute-done | bytes 786464 | tf_op jit(solution)/shard_map/ppermute | solution.py:159
  95.9 5.4 %attend.1 = bf16[8,256,128]{2,1,0:T(8,128)(2,1)} custom-call(s32[2]{0:T(128)S(1)} %pad_add_fusion.1.place_ref, bf16[256,4096]{1,0:T(8,128)(2,1)S(1)} %copy-done, bf16[256,4096]{1,0:T(8,128)(2,1)} %collective-permute-done.other_ref, f32[2,256,384]{2,1,0:T(8,128)S(1)} %half.1.half_ref, bf16[2,4,2,64,384]{4,3,2,1,0:T(8,128)(2,1)S(1)} %collective-permute-done.4.w0_ref, ...), custom_call_target="tpu_custom_call" | custom-call | flops 805306368 | bytes 6291456 | tf_op jit(solution)/shard_map/attend/pallas_call | solution.py:175
  101.3 4.8 %all-to-all-start.2 = ((bf16[8,256,128]{2,1,0:T(8,128)(2,1)}), bf16[8,256,128]{2,1,0:T(8,128)(2,1)S(1)}, u32[]{:S(2)}, u32[]{:S(2)}) async-start(bf16[8,256,128]{2,1,0:T(8,128)(2,1)} %attend.1), calls=%async_computation.2 | async-start | bytes 1048576 | tf_op jit(solution)/shard_map/all_to_all | solution.py:187
  106.1 1.0 pad_maximum_fusion.held_ref
  107.1 2.4 %collective-permute-start.7 = (bf16[3,128,1024]{2,1,0:T(8,128)(2,1)S(1)}, bf16[3,128,1024]{2,1,0:T(8,128)(2,1)S(1)}, u32[]{:S(2)}, u32[]{:S(2)}) collective-permute-start(bf16[3,128,1024]{2,1,0:T(8,128)(2,1)S(1)} %pad_maximum_fusion.held_ref), channel_id=1, source_target_pairs={{0,8},{8,0},{1,9},{9,1},{2,10},{10,2},{3,11},{11,3},{4,12},{12,4},... | collective-permute-start | bytes 2359304 | tf_op jit(solution)/shard_map/ppermute | solution.py:186
  109.6 1.9 %collective-permute-done.7.partner_ref = bf16[3,128,1024]{2,1,0:T(8,128)(2,1)S(1)} collective-permute-done((bf16[3,128,1024]{2,1,0:T(8,128)(2,1)S(1)}, bf16[3,128,1024]{2,1,0:T(8,128)(2,1)S(1)}, u32[]{:S(2)}, u32[]{:S(2)}) %collective-permute-start.7) | collective-permute-done | bytes 786464 | tf_op jit(solution)/shard_map/ppermute | solution.py:186
  111.5 9.5 %all-to-all-done.2 = bf16[8,256,128]{2,1,0:T(8,128)(2,1)S(1)} async-done(((bf16[8,256,128]{2,1,0:T(8,128)(2,1)}), bf16[8,256,128]{2,1,0:T(8,128)(2,1)S(1)}, u32[]{:S(2)}, u32[]{:S(2)}) %all-to-all-start.2) | async-done | bytes 524320 | tf_op jit(solution)/shard_map/all_to_all | solution.py:187
  121.0 1.3 project.1
  122.3 37.0 %all_to_all.21 = bf16[8,32,1024]{2,1,0:T(8,128)(2,1)S(1)} all-to-all(bf16[8,32,1024]{2,1,0:T(8,128)(2,1)S(1)} %bitcast.24), channel_id=1, replica_groups=mesh['zh'=2,'x'=4,'y'=8,'c'=2,'rg'=2,'cb'=4] {'rg','cb'}, dimensions={0} | all-to-all | bytes 1048576 | tf_op jit(solution)/shard_map/all_to_all | solution.py:199
  (30 shorter events, 5.9 us)
Async XLA Ops:
  0.0 45.6 %copy-start = (bf16[256,4096]{1,0:T(8,128)(2,1)S(1)}, bf16[256,4096]{1,0:T(8,128)(2,1)}, u32[]{:S(2)}) copy-start(bf16[256,4096]{1,0:T(8,128)(2,1)} %own_ref.3) | copy-start | bytes 6291460
  35.6 34.3 %all-to-all-start.1 = ((bf16[8,4,32,384]{3,2,1,0:T(8,128)(2,1)}), bf16[8,4,32,384]{3,2,1,0:T(8,128)(2,1)S(1)}, u32[]{:S(2)}, u32[]{:S(2)}) async-start(bf16[8,4,32,384]{3,2,1,0:T(8,128)(2,1)} %broadcast_in_dim.15), calls=%async_computation.1 | async-start | bytes 1572864 | tf_op jit(solution)/shard_map/all_to_all | solution.py:63
  45.6 38.9 %collective-permute-start = (bf16[256,4096]{1,0:T(8,128)(2,1)S(1)}, bf16[256,4096]{1,0:T(8,128)(2,1)}, u32[]{:S(2)}, u32[]{:S(2)}) collective-permute-start(bf16[256,4096]{1,0:T(8,128)(2,1)S(1)} %copy-done), channel_id=1, source_target_pairs={{0,8},{8,0},{1,9},{9,1},{2,10},{10,2},{3,11},{11,3},{4,12},{12,4},... | collective-permute-start | bytes 6291464 | tf_op jit(solution)/shard_map/ppermute | solution.py:135
  47.6 1.6 copy-start.3
  49.9 0.8 copy-start.4
  50.7 14.2 %collective-permute-start.1 = (bf16[128,1024]{1,0:T(8,128)(2,1)S(1)}, bf16[128,1024]{1,0:T(8,128)(2,1)S(1)}, u32[]{:S(2)}, u32[]{:S(2)}) collective-permute-start(bf16[128,1024]{1,0:T(8,128)(2,1)S(1)} %get-tuple-element.9), channel_id=1, source_target_pairs={{0,1},{1,0},{2,3},{3,2},{4,5},{5,4},{6,7},{7,6},{8,9},{9,8},{10,11... | collective-permute-start | bytes 786440 | tf_op jit(solution)/shard_map/ppermute | solution.py:156
  52.6 17.3 %collective-permute-start.2 = (bf16[128,1024]{1,0:T(8,128)(2,1)S(1)}, bf16[128,1024]{1,0:T(8,128)(2,1)}, u32[]{:S(2)}, u32[]{:S(2)}) collective-permute-start(bf16[128,1024]{1,0:T(8,128)(2,1)S(1)} %get-tuple-element.10), channel_id=1, source_target_pairs={{0,2},{1,3},{2,0},{3,1},{4,6},{5,7},{6,4},{7,5},{8,10},{9,11},{10,... | collective-permute-start | bytes 786440 | tf_op jit(solution)/shard_map/ppermute | solution.py:156
  64.9 5.0 %copy-start.6 = (bf16[128,1024]{1,0:T(8,128)(2,1)}, bf16[128,1024]{1,0:T(8,128)(2,1)S(1)}, u32[]{:S(2)}) copy-start(bf16[128,1024]{1,0:T(8,128)(2,1)S(1)} %collective-permute-done.1.refs_1_) | copy-start | bytes 786436
  69.9 0.9 copy-start.1
  70.8 14.2 %collective-permute-start.3 = (bf16[2,4,2,64,384]{4,3,2,1,0:T(8,128)(2,1)}, bf16[2,4,2,64,384]{4,3,2,1,0:T(8,128)(2,1)}, u32[]{:S(2)}, u32[]{:S(2)}) collective-permute-start(bf16[2,4,2,64,384]{4,3,2,1,0:T(8,128)(2,1)} %bitcast.19), channel_id=1, source_target_pairs={{0,16},{8,120},{16,0},{24,40},{32,48},{40,24},{48,32},{56,72},{64,... | collective-permute-start | bytes 2359304 | tf_op jit(solution)/shard_map/ppermute | solution.py:159
  73.4 22.5 %collective-permute-start.4 = (bf16[2,4,2,64,384]{4,3,2,1,0:T(8,128)(2,1)}, bf16[2,4,2,64,384]{4,3,2,1,0:T(8,128)(2,1)S(1)}, u32[]{:S(2)}, u32[]{:S(2)}) collective-permute-start(bf16[2,4,2,64,384]{4,3,2,1,0:T(8,128)(2,1)} %bitcast.20), channel_id=1, source_target_pairs={{0,128},{8,392},{16,144},{24,408},{32,160},{40,424},{48,176},{56,4... | collective-permute-start | bytes 2359304 | tf_op jit(solution)/shard_map/ppermute | solution.py:159
  76.1 19.8 %collective-permute-start.5 = (bf16[2,4,2,64,384]{4,3,2,1,0:T(8,128)(2,1)}, bf16[2,4,2,64,384]{4,3,2,1,0:T(8,128)(2,1)}, u32[]{:S(2)}, u32[]{:S(2)}) collective-permute-start(bf16[2,4,2,64,384]{4,3,2,1,0:T(8,128)(2,1)} %bitcast.21), channel_id=1, source_target_pairs={{0,144},{8,504},{16,128},{24,424},{32,176},{40,408},{48,160},{56,4... | collective-permute-start | bytes 2359304 | tf_op jit(solution)/shard_map/ppermute | solution.py:159
  80.0 12.6 %collective-permute-start.6 = (bf16[128,1024]{1,0:T(8,128)(2,1)S(1)}, bf16[128,1024]{1,0:T(8,128)(2,1)S(1)}, u32[]{:S(2)}, u32[]{:S(2)}) collective-permute-start(bf16[128,1024]{1,0:T(8,128)(2,1)S(1)} %get-tuple-element.11), channel_id=1, source_target_pairs={{0,3},{1,2},{2,1},{3,0},{4,7},{5,6},{6,5},{7,4},{8,11},{9,10},{10,... | collective-permute-start | bytes 786440 | tf_op jit(solution)/shard_map/ppermute | solution.py:156
  85.0 1.1 copy-start.2
  92.7 13.5 %copy-start.7 = (bf16[128,1024]{1,0:T(8,128)(2,1)S(1)}, bf16[128,1024]{1,0:T(8,128)(2,1)}, u32[]{:S(2)}) copy-start(bf16[128,1024]{1,0:T(8,128)(2,1)} %copy-done.6) | copy-start | bytes 786436
  101.3 19.7 %copy-start.5 = (bf16[256,1024]{1,0:T(8,128)(2,1)S(1)}, bf16[256,1024]{1,0:T(8,128)(2,1)}, u32[]{:S(2)}) copy-start(bf16[256,1024]{1,0:T(8,128)(2,1)} %copy-done.4) | copy-start | bytes 1572868
  101.3 19.7 %all-to-all-start.2 = ((bf16[8,256,128]{2,1,0:T(8,128)(2,1)}), bf16[8,256,128]{2,1,0:T(8,128)(2,1)S(1)}, u32[]{:S(2)}, u32[]{:S(2)}) async-start(bf16[8,256,128]{2,1,0:T(8,128)(2,1)} %attend.1), calls=%async_computation.2 | async-start | bytes 1048576 | tf_op jit(solution)/shard_map/all_to_all | solution.py:187
  107.1 4.3 %collective-permute-start.7 = (bf16[3,128,1024]{2,1,0:T(8,128)(2,1)S(1)}, bf16[3,128,1024]{2,1,0:T(8,128)(2,1)S(1)}, u32[]{:S(2)}, u32[]{:S(2)}) collective-permute-start(bf16[3,128,1024]{2,1,0:T(8,128)(2,1)S(1)} %pad_maximum_fusion.held_ref), channel_id=1, source_target_pairs={{0,8},{8,0},{1,9},{9,1},{2,10},{10,2},{3,11},{11,3},{4,12},{12,4},... | collective-permute-start | bytes 2359304 | tf_op jit(solution)/shard_map/ppermute | solution.py:186

commit v12 on v11

--- a/solution.py
+++ b/solution.py
@@ -105,28 +105,35 @@
             out_ref[(core ^ g) * CB + cb] = mixed
 
 
-def split_kernel(place_ref, w_ref, after_ref, own_ref, *out_refs):
+def split_kernel(place_ref, w_ref, *refs):
     column, core = place_ref[0], place_ref[1]
+    out_refs = refs[1:]
     part, width = out_refs[0].shape
-    own_ref[...] = w_ref[:, pl.ds(pl.multiple_of(column * width, width), width)]
     rows = pl.ds(pl.multiple_of(core * part, part), part)
     for i, out_ref in enumerate(out_refs):
         start = pl.multiple_of((column ^ (i + 1)) * width, width)
         out_ref[...] = w_ref[rows, pl.ds(start, width)]
 
 
-def project_kernel(place_ref, mixed_ref, own_ref, held_ref, partner_ref, out_ref):
+def project_kernel(place_ref, mixed_ref, w_ref, held_ref, partner_ref, out_ref, own_ref, sem):
     column, core = place_ref[0], place_ref[1]
-    mixed = jnp.concatenate([mixed_ref[c, column] for c in range(C)], axis=1)
-    term = jnp.dot(mixed, own_ref[...], preferred_element_type=jnp.float32).astype(jnp.bfloat16)
-    total = term.astype(jnp.float32)
+    width = own_ref.shape[1]
+    fetch = pltpu.make_async_copy(
+        w_ref.at[:, pl.ds(pl.multiple_of(column * width, width), width)], own_ref, sem
+    )
+    fetch.start()
+    total = None
     for i in range(CB - 1):
         block = column ^ (i + 1)
         mixed = jnp.concatenate([mixed_ref[core, block], mixed_ref[1 - core, block]], axis=1)
         weight = jnp.concatenate([held_ref[i], partner_ref[i]], axis=0)
         term = jnp.dot(mixed, weight, preferred_element_type=jnp.float32).astype(jnp.bfloat16)
-        total += term.astype(jnp.float32)
-    out_ref[...] = total.astype(out_ref.dtype)
+        wide = term.astype(jnp.float32)
+        total = wide if total is None else total + wide
+    fetch.wait()
+    mixed = jnp.concatenate([mixed_ref[c, column] for c in range(C)], axis=1)
+    term = jnp.dot(mixed, own_ref[...], preferred_element_type=jnp.float32).astype(jnp.bfloat16)
+    out_ref[...] = (total + term.astype(jnp.float32)).astype(out_ref.dtype)
 
 
 def body(tokens, qkv_weight, out_weight):
@@ -143,12 +150,11 @@
     column, core = lax.axis_index("cb"), lax.axis_index("c")
     depth, columns = out_weight.shape[0], out_weight.shape[1] // CB
     smem, vmem = pl.BlockSpec(memory_space=pltpu.SMEM), pl.BlockSpec(memory_space=pltpu.VMEM)
-    own_weight, *sent = pl.pallas_call(
+    sent = pl.pallas_call(
         split_kernel,
-        out_shape=[jax.ShapeDtypeStruct((depth, columns), jnp.bfloat16)]
-        + [jax.ShapeDtypeStruct((depth // C, columns), jnp.bfloat16)] * (CB - 1),
+        out_shape=[jax.ShapeDtypeStruct((depth // C, columns), jnp.bfloat16)] * (CB - 1),
         in_specs=[smem, vmem, vmem],
-        out_specs=[vmem] * CB,
+        out_specs=[vmem] * (CB - 1),
         compiler_params=pltpu.CompilerParams(vmem_limit_bytes=24 << 20),
         cost_estimate=pl.CostEstimate(flops=0, bytes_accessed=4 << 20, transcendentals=0),
         name="split",
@@ -189,12 +195,13 @@
     summed = pl.pallas_call(
         project_kernel,
         out_shape=jax.ShapeDtypeStruct((rows, columns), jnp.bfloat16),
-        in_specs=[smem] + [vmem] * 4,
+        in_specs=[smem, vmem, ANYWHERE, vmem, vmem],
         out_specs=vmem,
+        scratch_shapes=[pltpu.VMEM((depth, columns), jnp.bfloat16), pltpu.SemaphoreType.DMA(())],
         compiler_params=pltpu.CompilerParams(vmem_limit_bytes=24 << 20),
         cost_estimate=pl.CostEstimate(flops=2 * rows * CB * C * HD * columns, bytes_accessed=4 << 20, transcendentals=0),
         name="project",
-    )(jnp.stack([column, core]), mixed, own_weight, held, partner)
+    )(jnp.stack([column, core]), mixed, out_weight, held, partner)
     part = rows // (RG * CB)
     summed = lax.all_to_all(summed.reshape(RG * CB, part, columns), MP, 0, 0, tiled=True)
     summed = summed.reshape(RG, CB, part, columns).astype(jnp.float32)

time: 161 us -> 160 us (level)
  waiting for transfers between devices: 31 us -> 28.5 us
where the time goes in v12:
time: 160 us; the launch traced here: 159 us
  blocking collectives  70.5 us (44%)
  starting transfers between devices  38.4 us (24%)
  waiting for transfers between devices  28.5 us (18%)
  Pallas kernels  11.7 us (7%)
  local copies, waits for them, and re-layouts  8.42 us (5%)
    all_to_all x1, blocking collectives, body(): lax.all_to_all(summed.reshape(RG * CB, part, columns), MP, 0, 0, tiled=True)  37 us
    all_to_all x1, blocking collectives, body(): heads = lax.all_to_all(heads, ('zh', 'c'), 0, 0, tiled=True)  33.5 us
    ppermute x3, waiting for transfers between devices, body(): lax.ppermute(block, 'cb', [(j, j ^ i + 1) for j in range(CB)])  14.4 us
    ppermute x3, starting transfers between devices, body(): lax.ppermute(block, 'cb', [(j, j ^ i + 1) for j in range(CB)])  10.1 us
    all_to_all x1, starting transfers between devices, spread(): lax.all_to_all(blocks, DP, 0, 0, axis_index_groups=groups, tiled=True)  10.1 us
    ppermute x3, starting transfers between devices, body(): squares = [heads] + [lax.ppermute(heads, DP, pairs) for pairs in NEAR]  9.2 us
    all_to_all x1, waiting for transfers between devices, body(): lax.all_to_all(mixed, ('c', 'cb'), 0, 0, tiled=True)  8.49 us
    unnamed x16, local copies, waits for them, and re-layouts  5.65 us
  transfers between devices with their start and end apart: 10, of which 7 were waited for; matrix products, arithmetic and copies ran while one was open for 1% of the time, Pallas kernels for 3%

profile of v12, /device:TPU:6, one launch (start us, length us, event | category | flops | bytes accessed | tf_op | source)
XLA Modules:
  0.0 159.3 jit_solution(2617659442359223315)
XLA Ops:
  1.1 33.5 %all_to_all.20.refs_0_ = bf16[4,32,384]{2,1,0:T(8,128)(2,1)S(1)} all-to-all(bf16[4,32,384]{2,1,0:T(8,128)(2,1)S(1)} %bitcast.27), channel_id=1, replica_groups=mesh['zh'=2,'x'=4,'y'=8,'c'=2,'rg'=2,'cb'=4] {'zh','c'}, dimensions={0} | all-to-all | bytes 196608 | tf_op jit(solution)/shard_map/all_to_all | solution.py:146
  35.6 10.1 %all-to-all-start.1 = ((bf16[8,4,32,384]{3,2,1,0:T(8,128)(2,1)}), bf16[8,4,32,384]{3,2,1,0:T(8,128)(2,1)S(1)}, u32[]{:S(2)}, u32[]{:S(2)}) async-start(bf16[8,4,32,384]{3,2,1,0:T(8,128)(2,1)} %broadcast_in_dim.15), calls=%async_computation.1 | async-start | bytes 1572864 | tf_op jit(solution)/shard_map/all_to_all | solution.py:63
  45.6 1.9 %collective-permute-start = (bf16[256,4096]{1,0:T(8,128)(2,1)}, bf16[256,4096]{1,0:T(8,128)(2,1)}, u32[]{:S(2)}, u32[]{:S(2)}) collective-permute-start(bf16[256,4096]{1,0:T(8,128)(2,1)} %own_ref.3), channel_id=1, source_target_pairs={{0,8},{8,0},{1,9},{9,1},{2,10},{10,2},{3,11},{11,3},{4,12},{12,4},... | collective-permute-start | bytes 6291464 | tf_op jit(solution)/shard_map/ppermute | solution.py:142
  48.3 1.9 %collective-permute-start.1 = (bf16[128,1024]{1,0:T(8,128)(2,1)S(1)}, bf16[128,1024]{1,0:T(8,128)(2,1)S(1)}, u32[]{:S(2)}, u32[]{:S(2)}) collective-permute-start(bf16[128,1024]{1,0:T(8,128)(2,1)S(1)} %get-tuple-element.8), channel_id=1, source_target_pairs={{0,1},{1,0},{2,3},{3,2},{4,5},{5,4},{6,7},{7,6},{8,9},{9,8},{10,11... | collective-permute-start | bytes 786440 | tf_op jit(solution)/shard_map/ppermute | solution.py:162
  50.2 3.8 %collective-permute-start.2 = (bf16[128,1024]{1,0:T(8,128)(2,1)S(1)}, bf16[128,1024]{1,0:T(8,128)(2,1)}, u32[]{:S(2)}, u32[]{:S(2)}) collective-permute-start(bf16[128,1024]{1,0:T(8,128)(2,1)S(1)} %get-tuple-element.9), channel_id=1, source_target_pairs={{0,2},{1,3},{2,0},{3,1},{4,6},{5,7},{6,4},{7,5},{8,10},{9,11},{10,... | collective-permute-start | bytes 786440 | tf_op jit(solution)/shard_map/ppermute | solution.py:162
  54.0 8.5 %collective-permute-done.1.refs_1_ = bf16[128,1024]{1,0:T(8,128)(2,1)S(1)} collective-permute-done((bf16[128,1024]{1,0:T(8,128)(2,1)S(1)}, bf16[128,1024]{1,0:T(8,128)(2,1)S(1)}, u32[]{:S(2)}, u32[]{:S(2)}) %collective-permute-start.1) | collective-permute-done | bytes 262176 | tf_op jit(solution)/shard_map/ppermute | solution.py:162
  62.5 5.0 %collective-permute-done.2.refs_2_ = bf16[128,1024]{1,0:T(8,128)(2,1)} collective-permute-done((bf16[128,1024]{1,0:T(8,128)(2,1)S(1)}, bf16[128,1024]{1,0:T(8,128)(2,1)}, u32[]{:S(2)}, u32[]{:S(2)}) %collective-permute-start.2) | collective-permute-done | bytes 262176 | tf_op jit(solution)/shard_map/ppermute | solution.py:162
  68.4 2.6 %collective-permute-start.3 = (bf16[2,4,2,64,384]{4,3,2,1,0:T(8,128)(2,1)}, bf16[2,4,2,64,384]{4,3,2,1,0:T(8,128)(2,1)}, u32[]{:S(2)}, u32[]{:S(2)}) collective-permute-start(bf16[2,4,2,64,384]{4,3,2,1,0:T(8,128)(2,1)} %bitcast.19), channel_id=1, source_target_pairs={{0,16},{8,120},{16,0},{24,40},{32,48},{40,24},{48,32},{56,72},{64,... | collective-permute-start | bytes 2359304 | tf_op jit(solution)/shard_map/ppermute | solution.py:165
  70.9 2.7 %collective-permute-start.4 = (bf16[2,4,2,64,384]{4,3,2,1,0:T(8,128)(2,1)}, bf16[2,4,2,64,384]{4,3,2,1,0:T(8,128)(2,1)}, u32[]{:S(2)}, u32[]{:S(2)}) collective-permute-start(bf16[2,4,2,64,384]{4,3,2,1,0:T(8,128)(2,1)} %bitcast.20), channel_id=1, source_target_pairs={{0,128},{8,392},{16,144},{24,408},{32,160},{40,424},{48,176},{56,4... | collective-permute-start | bytes 2359304 | tf_op jit(solution)/shard_map/ppermute | solution.py:165
  73.7 3.9 %collective-permute-start.5 = (bf16[2,4,2,64,384]{4,3,2,1,0:T(8,128)(2,1)}, bf16[2,4,2,64,384]{4,3,2,1,0:T(8,128)(2,1)}, u32[]{:S(2)}, u32[]{:S(2)}) collective-permute-start(bf16[2,4,2,64,384]{4,3,2,1,0:T(8,128)(2,1)} %bitcast.21), channel_id=1, source_target_pairs={{0,144},{8,504},{16,128},{24,424},{32,176},{40,408},{48,160},{56,4... | collective-permute-start | bytes 2359304 | tf_op jit(solution)/shard_map/ppermute | solution.py:165
  77.6 4.4 %collective-permute-start.6 = (bf16[128,1024]{1,0:T(8,128)(2,1)S(1)}, bf16[128,1024]{1,0:T(8,128)(2,1)S(1)}, u32[]{:S(2)}, u32[]{:S(2)}) collective-permute-start(bf16[128,1024]{1,0:T(8,128)(2,1)S(1)} %get-tuple-element.10), channel_id=1, source_target_pairs={{0,3},{1,2},{2,1},{3,0},{4,7},{5,6},{6,5},{7,4},{8,11},{9,10},{10,... | collective-permute-start | bytes 786440 | tf_op jit(solution)/shard_map/ppermute | solution.py:162
  82.6 1.6 copy-done.1
  84.1 1.1 copy-done.3
  85.3 4.1 %half.1.half_ref = f32[2,256,384]{2,1,0:T(8,128)S(1)} custom-call(s32[2]{0:T(128)S(1)} %pad_add_fusion.1.place_ref, bf16[256,4096]{1,0:T(8,128)(2,1)S(1)} %copy-done.1, bf16[256,4096]{1,0:T(8,128)(2,1)} %collective-permute-done.other_ref, bf16[2,4,2,64,384]{4,3,2,1,0:T(8,128)(2,1)S(1)} %bitcast.22, bf16[2,4,2,64,384]{4,3,2,1,0:T(8,128)(2,1)} %collective-permute-done.3.w1_ref), custom_call_target="tpu_custom_call" | custom-call | flops 805306368 | bytes 6291456 | tf_op jit(solution)/shard_map/half/pallas_call | solution.py:171
  90.2 3.3 %collective-permute-done.4.w0_ref = bf16[2,4,2,64,384]{4,3,2,1,0:T(8,128)(2,1)} collective-permute-done((bf16[2,4,2,64,384]{4,3,2,1,0:T(8,128)(2,1)}, bf16[2,4,2,64,384]{4,3,2,1,0:T(8,128)(2,1)}, u32[]{:S(2)}, u32[]{:S(2)}) %collective-permute-start.4) | collective-permute-done | bytes 786464 | tf_op jit(solution)/shard_map/ppermute | solution.py:165
  93.6 5.6 %attend.1 = bf16[8,256,128]{2,1,0:T(8,128)(2,1)} custom-call(s32[2]{0:T(128)S(1)} %pad_add_fusion.1.place_ref, bf16[256,4096]{1,0:T(8,128)(2,1)S(1)} %copy-done.1, bf16[256,4096]{1,0:T(8,128)(2,1)} %collective-permute-done.other_ref, f32[2,256,384]{2,1,0:T(8,128)S(1)} %half.1.half_ref, bf16[2,4,2,64,384]{4,3,2,1,0:T(8,128)(2,1)} %collective-permute-done.4.w0_ref, ...), custom_call_target="tpu_custom_call" | custom-call | flops 805306368 | bytes 6291456 | tf_op jit(solution)/shard_map/attend/pallas_call | solution.py:181
  99.2 4.7 %all-to-all-start.2 = ((bf16[8,256,128]{2,1,0:T(8,128)(2,1)}), bf16[8,256,128]{2,1,0:T(8,128)(2,1)S(1)}, u32[]{:S(2)}, u32[]{:S(2)}) async-start(bf16[8,256,128]{2,1,0:T(8,128)(2,1)} %attend.1), calls=%async_computation.2 | async-start | bytes 1048576 | tf_op jit(solution)/shard_map/all_to_all | solution.py:193
  103.9 1.2 pad_maximum_fusion.held_ref
  105.1 2.4 %collective-permute-start.7 = (bf16[3,128,1024]{2,1,0:T(8,128)(2,1)S(1)}, bf16[3,128,1024]{2,1,0:T(8,128)(2,1)S(1)}, u32[]{:S(2)}, u32[]{:S(2)}) collective-permute-start(bf16[3,128,1024]{2,1,0:T(8,128)(2,1)S(1)} %pad_maximum_fusion.held_ref), channel_id=1, source_target_pairs={{0,8},{8,0},{1,9},{9,1},{2,10},{10,2},{3,11},{11,3},{4,12},{12,4},... | collective-permute-start | bytes 2359304 | tf_op jit(solution)/shard_map/ppermute | solution.py:192
  107.5 1.9 %collective-permute-done.7.partner_ref = bf16[3,128,1024]{2,1,0:T(8,128)(2,1)S(1)} collective-permute-done((bf16[3,128,1024]{2,1,0:T(8,128)(2,1)S(1)}, bf16[3,128,1024]{2,1,0:T(8,128)(2,1)S(1)}, u32[]{:S(2)}, u32[]{:S(2)}) %collective-permute-start.7) | collective-permute-done | bytes 786464 | tf_op jit(solution)/shard_map/ppermute | solution.py:192
  110.3 8.5 %all-to-all-done.2 = bf16[8,256,128]{2,1,0:T(8,128)(2,1)S(1)} async-done(((bf16[8,256,128]{2,1,0:T(8,128)(2,1)}), bf16[8,256,128]{2,1,0:T(8,128)(2,1)S(1)}, u32[]{:S(2)}, u32[]{:S(2)}) %all-to-all-start.2) | async-done | bytes 524320 | tf_op jit(solution)/shard_map/all_to_all | solution.py:193
  118.7 1.1 copy-done.6
  119.9 1.5 project.1
  121.4 37.0 %all_to_all.21 = bf16[8,32,1024]{2,1,0:T(8,128)(2,1)S(1)} all-to-all(bf16[8,32,1024]{2,1,0:T(8,128)(2,1)S(1)} %bitcast.24), channel_id=1, replica_groups=mesh['zh'=2,'x'=4,'y'=8,'c'=2,'rg'=2,'cb'=4] {'rg','cb'}, dimensions={0} | all-to-all | bytes 1048576 | tf_op jit(solution)/shard_map/all_to_all | solution.py:206
  (30 shorter events, 6.8 us)
Async XLA Ops:
  0.0 47.6 %copy-start = (bf16[256,4096]{1,0:T(8,128)(2,1)S(1)}, bf16[256,4096]{1,0:T(8,128)(2,1)}, u32[]{:S(2)}) copy-start(bf16[256,4096]{1,0:T(8,128)(2,1)} %w_ref.3) | copy-start | bytes 6291460
  35.6 31.9 %all-to-all-start.1 = ((bf16[8,4,32,384]{3,2,1,0:T(8,128)(2,1)}), bf16[8,4,32,384]{3,2,1,0:T(8,128)(2,1)S(1)}, u32[]{:S(2)}, u32[]{:S(2)}) async-start(bf16[8,4,32,384]{3,2,1,0:T(8,128)(2,1)} %broadcast_in_dim.15), calls=%async_computation.1 | async-start | bytes 1572864 | tf_op jit(solution)/shard_map/all_to_all | solution.py:63
  45.6 36.5 %collective-permute-start = (bf16[256,4096]{1,0:T(8,128)(2,1)}, bf16[256,4096]{1,0:T(8,128)(2,1)}, u32[]{:S(2)}, u32[]{:S(2)}) collective-permute-start(bf16[256,4096]{1,0:T(8,128)(2,1)} %own_ref.3), channel_id=1, source_target_pairs={{0,8},{8,0},{1,9},{9,1},{2,10},{10,2},{3,11},{11,3},{4,12},{12,4},... | collective-permute-start | bytes 6291464 | tf_op jit(solution)/shard_map/ppermute | solution.py:142
  48.3 14.2 %collective-permute-start.1 = (bf16[128,1024]{1,0:T(8,128)(2,1)S(1)}, bf16[128,1024]{1,0:T(8,128)(2,1)S(1)}, u32[]{:S(2)}, u32[]{:S(2)}) collective-permute-start(bf16[128,1024]{1,0:T(8,128)(2,1)S(1)} %get-tuple-element.8), channel_id=1, source_target_pairs={{0,1},{1,0},{2,3},{3,2},{4,5},{5,4},{6,7},{7,6},{8,9},{9,8},{10,11... | collective-permute-start | bytes 786440 | tf_op jit(solution)/shard_map/ppermute | solution.py:162
  50.2 17.3 %collective-permute-start.2 = (bf16[128,1024]{1,0:T(8,128)(2,1)S(1)}, bf16[128,1024]{1,0:T(8,128)(2,1)}, u32[]{:S(2)}, u32[]{:S(2)}) collective-permute-start(bf16[128,1024]{1,0:T(8,128)(2,1)S(1)} %get-tuple-element.9), channel_id=1, source_target_pairs={{0,2},{1,3},{2,0},{3,1},{4,6},{5,7},{6,4},{7,5},{8,10},{9,11},{10,... | collective-permute-start | bytes 786440 | tf_op jit(solution)/shard_map/ppermute | solution.py:162
  62.5 5.0 %copy-start.7 = (bf16[128,1024]{1,0:T(8,128)(2,1)}, bf16[128,1024]{1,0:T(8,128)(2,1)S(1)}, u32[]{:S(2)}) copy-start(bf16[128,1024]{1,0:T(8,128)(2,1)S(1)} %collective-permute-done.1.refs_1_) | copy-start | bytes 786436
  67.5 0.9 copy-start.2
  68.4 14.2 %collective-permute-start.3 = (bf16[2,4,2,64,384]{4,3,2,1,0:T(8,128)(2,1)}, bf16[2,4,2,64,384]{4,3,2,1,0:T(8,128)(2,1)}, u32[]{:S(2)}, u32[]{:S(2)}) collective-permute-start(bf16[2,4,2,64,384]{4,3,2,1,0:T(8,128)(2,1)} %bitcast.19), channel_id=1, source_target_pairs={{0,16},{8,120},{16,0},{24,40},{32,48},{40,24},{48,32},{56,72},{64,... | collective-permute-start | bytes 2359304 | tf_op jit(solution)/shard_map/ppermute | solution.py:165
  70.9 22.6 %collective-permute-start.4 = (bf16[2,4,2,64,384]{4,3,2,1,0:T(8,128)(2,1)}, bf16[2,4,2,64,384]{4,3,2,1,0:T(8,128)(2,1)}, u32[]{:S(2)}, u32[]{:S(2)}) collective-permute-start(bf16[2,4,2,64,384]{4,3,2,1,0:T(8,128)(2,1)} %bitcast.20), channel_id=1, source_target_pairs={{0,128},{8,392},{16,144},{24,408},{32,160},{40,424},{48,176},{56,4... | collective-permute-start | bytes 2359304 | tf_op jit(solution)/shard_map/ppermute | solution.py:165
  73.7 19.9 %collective-permute-start.5 = (bf16[2,4,2,64,384]{4,3,2,1,0:T(8,128)(2,1)}, bf16[2,4,2,64,384]{4,3,2,1,0:T(8,128)(2,1)}, u32[]{:S(2)}, u32[]{:S(2)}) collective-permute-start(bf16[2,4,2,64,384]{4,3,2,1,0:T(8,128)(2,1)} %bitcast.21), channel_id=1, source_target_pairs={{0,144},{8,504},{16,128},{24,424},{32,176},{40,408},{48,160},{56,4... | collective-permute-start | bytes 2359304 | tf_op jit(solution)/shard_map/ppermute | solution.py:165
  77.6 12.6 %collective-permute-start.6 = (bf16[128,1024]{1,0:T(8,128)(2,1)S(1)}, bf16[128,1024]{1,0:T(8,128)(2,1)S(1)}, u32[]{:S(2)}, u32[]{:S(2)}) collective-permute-start(bf16[128,1024]{1,0:T(8,128)(2,1)S(1)} %get-tuple-element.10), channel_id=1, source_target_pairs={{0,3},{1,2},{2,1},{3,0},{4,7},{5,6},{6,5},{7,4},{8,11},{9,10},{10,... | collective-permute-start | bytes 786440 | tf_op jit(solution)/shard_map/ppermute | solution.py:162
  82.6 1.6 copy-start.1
  84.1 1.1 copy-start.3
  90.2 8.9 %copy-start.4 = (bf16[128,1024]{1,0:T(8,128)(2,1)}, bf16[128,1024]{1,0:T(8,128)(2,1)S(1)}, u32[]{:S(2)}) copy-start(bf16[128,1024]{1,0:T(8,128)(2,1)S(1)} %collective-permute-done.6.after_ref) | copy-start | bytes 786436
  99.2 19.6 %all-to-all-start.2 = ((bf16[8,256,128]{2,1,0:T(8,128)(2,1)}), bf16[8,256,128]{2,1,0:T(8,128)(2,1)S(1)}, u32[]{:S(2)}, u32[]{:S(2)}) async-start(bf16[8,256,128]{2,1,0:T(8,128)(2,1)} %attend.1), calls=%async_computation.2 | async-start | bytes 1048576 | tf_op jit(solution)/shard_map/all_to_all | solution.py:193
  105.1 4.3 %collective-permute-start.7 = (bf16[3,128,1024]{2,1,0:T(8,128)(2,1)S(1)}, bf16[3,128,1024]{2,1,0:T(8,128)(2,1)S(1)}, u32[]{:S(2)}, u32[]{:S(2)}) collective-permute-start(bf16[3,128,1024]{2,1,0:T(8,128)(2,1)S(1)} %pad_maximum_fusion.held_ref), channel_id=1, source_target_pairs={{0,8},{8,0},{1,9},{9,1},{2,10},{10,2},{3,11},{11,3},{4,12},{12,4},... | collective-permute-start | bytes 2359304 | tf_op jit(solution)/shard_map/ppermute | solution.py:192
  109.4 0.9 copy-start.5
  118.7 1.1 copy-start.6
